TPU v7x, 1024 devices: a whole 4x8x16 slice. The times are simulated.
1024 devices in a mesh: dp: 512 (over y, x_hi, z, core), mp: 2 (over x_lo).
Axes of the slice: x: 4 (x_hi: 2, x_lo: 2; x = x_hi * 2 + x_lo), y: 8, z: 16, core: 2. Of those that a mesh axis runs over, the one named last changes fastest.
Arguments:
- image_emb: float32 [131072, 1152], P(('dp', 'mp')), may hold values from -0.1875 to 0.1875
- text_emb: float32 [131072, 1152], P(('dp', 'mp')), may hold values from -0.1875 to 0.1875
- video_ids: int32 [131072], P(('dp', 'mp')), may hold values from 0 to 32767, never falling along the last dimension, each value on 1 to 8 neighbouring positions
- log_scale: float32 [], replicated, may hold values from 4 to 5
- bias: float32 [], replicated, may hold values from -6 to -2
Outputs:
- loss: float32 [], replicated
- grad_image: float32 [131072, 1152], P(('dp', 'mp'))
- grad_text: float32 [131072, 1152], P(('dp', 'mp'))
- grad_log_scale: float32 [], replicated
- grad_bias: float32 [], replicated
Inputs may be any that keep to these rules, and one draw needn't show every extreme that they name: video_ids never fall along the rows; each video covers 1 to 8 consecutive pairs, one exactly 8.
All inputs are finite; a program needn't handle non-finite values.
Results may differ from a plain program's by a relative error of at most 0.00015.
Values sent between devices are 32-bit elements; how exact they have to be, the bound alone decides.
No kernel may reach another device: no remote copies, remote signals or barrier semaphores. Data moves between devices by JAX's collectives and lax.ppermute only.
A program may use at most 32 MiB of HBM per device.

v0:
```python
import jax
import jax.numpy as jnp
from jax import lax
from jax.sharding import PartitionSpec as P

STEPS = 7


def shifted_2(x, axis, by):
    count = lax.axis_size(axis)
    return lax.ppermute(x, axis, [(i, (i + by) % count) for i in range(count)])


def local(image_emb, text_emb, video_ids, log_scale, bias):
    rows = image_emb.shape[0]
    scale = jnp.exp(log_scale)
    norm = 1.0 / (STEPS * rows)
    mine = video_ids.astype(jnp.float32)
    carried = text_emb
    carried_ids = mine
    pending = jnp.zeros_like(text_emb)
    image_grad = jnp.zeros_like(image_emb)
    loss_sum = jnp.zeros((), jnp.float32)
    scale_sum = jnp.zeros((), jnp.float32)
    bias_sum = jnp.zeros((), jnp.float32)
    for step in range(STEPS):
        sim = lax.dot_general(
            image_emb,
            carried,
            (((1,), (1,)), ((), ())),
            precision=lax.Precision.HIGHEST,
            preferred_element_type=jnp.float32,
        )
        sign = jnp.where(mine[:, None] == carried_ids[None, :], 1.0, -1.0).astype(jnp.float32)
        shifted = sign * (scale * sim + bias)
        loss_sum = loss_sum + norm * jnp.sum(jax.nn.softplus(-shifted))
        weight = -sign * jax.nn.sigmoid(-shifted) * norm
        image_grad = image_grad + scale * jnp.dot(
            weight, carried, precision=lax.Precision.HIGHEST, preferred_element_type=jnp.float32
        )
        pending = pending + scale * lax.dot_general(
            weight,
            image_emb,
            (((0,), (0,)), ((), ())),
            precision=lax.Precision.HIGHEST,
            preferred_element_type=jnp.float32,
        )
        scale_sum = scale_sum + scale * jnp.sum(weight * sim)
        bias_sum = bias_sum + jnp.sum(weight)
        if step + 1 < STEPS:
            carried, carried_ids, pending = shifted_2(
                (carried, carried_ids, pending), ("dp", "mp"), 1
            )
    text_grad = shifted_2(pending, ("dp", "mp"), -(STEPS - 1))
    loss_all, scale_all, bias_all = lax.psum((loss_sum, scale_sum, bias_sum), ("dp", "mp"))
    tokens = rows * lax.axis_size(("dp", "mp"))
    return (loss_all / tokens, image_grad, text_grad, scale_all / tokens, bias_all / tokens)


def solution(mesh):
    placed = (P(("dp", "mp"), None), P(("dp", "mp"), None), P(("dp", "mp")), P(), P())
    return jax.shard_map(
        local,
        mesh=mesh,
        in_specs=placed,
        out_specs=(P(), P(("dp", "mp"), None), P(("dp", "mp"), None), P(), P()),
        check_vma=False,
    )
```

profile of v0, /device:TPU:1, one launch (start us, length us, event | category | flops | bytes accessed | tf_op | source)
XLA Modules:
  0.0 339.7 jit_solution(9262411827300946083)
XLA Ops:
  0.6 4.1 %collective-permute-start.1 = (f32[128,1152]{1,0:T(8,128)}, f32[128,1152]{1,0:T(8,128)S(1)}, u32[]{:S(2)}, u32[]{:S(2)}) collective-permute-start(f32[128,1152]{1,0:T(8,128)} %param.6), channel_id=1, source_target_pairs={{0,1},{1,2},{2,3},{3,4},{4,5},{5,6},{6,7},{7,8},{8,9},{9,10},{10,1... | collective-permute-start | bytes 1769480 | tf_op jit(solution)/shard_map/ppermute | solution.py:11
  8.7 4.5 %collective-permute-start.12 = (f32[128,1152]{1,0:T(8,128)S(1)}, f32[128,1152]{1,0:T(8,128)S(1)}, u32[]{:S(2)}, u32[]{:S(2)}) collective-permute-start(f32[128,1152]{1,0:T(8,128)S(1)} %convolution_multiply_fusion.6), channel_id=1, source_target_pairs={{0,1},{1,2},{2,3},{3,4},{4,5},{5,6},{6,7},{7,8},{8,9},{9,10},{10,1... | collective-permute-start | bytes 1769480 | tf_op jit(solution)/shard_map/ppermute | solution.py:11
  13.2 3.4 %collective-permute-start = (f32[128]{0:T(128)S(1)}, f32[128]{0:T(128)S(1)}, u32[]{:S(2)}, u32[]{:S(2)}) collective-permute-start(f32[128]{0:T(128)S(1)} %convert_element_type.3), channel_id=1, source_target_pairs={{0,1},{1,2},{2,3},{3,4},{4,5},{5,6},{6,7},{7,8},{8,9},{9,10},{10,1... | collective-permute-start | bytes 1544 | tf_op jit(solution)/shard_map/ppermute | solution.py:11
  23.1 5.2 %collective-permute-start.13 = (f32[128,1152]{1,0:T(8,128)S(1)}, f32[128,1152]{1,0:T(8,128)S(1)}, u32[]{:S(2)}, u32[]{:S(2)}) collective-permute-start(f32[128,1152]{1,0:T(8,128)S(1)} %fusion), channel_id=1, source_target_pairs={{0,1},{1,2},{2,3},{3,4},{4,5},{5,6},{6,7},{7,8},{8,9},{9,10},{10,1... | collective-permute-start | bytes 1769480 | tf_op jit(solution)/shard_map/ppermute | solution.py:11
  28.2 10.7 %collective-permute-start.2 = (f32[128]{0:T(128)S(1)}, f32[128]{0:T(128)S(1)}, u32[]{:S(2)}, u32[]{:S(2)}) collective-permute-start(f32[128]{0:T(128)S(1)} %collective-permute-done), channel_id=1, source_target_pairs={{0,1},{1,2},{2,3},{3,4},{4,5},{5,6},{6,7},{7,8},{8,9},{9,10},{10,1... | collective-permute-start | bytes 1544 | tf_op jit(solution)/shard_map/ppermute | solution.py:11
  38.9 4.2 %collective-permute-done.3 = f32[128,1152]{1,0:T(8,128)S(1)} collective-permute-done((f32[128,1152]{1,0:T(8,128)S(1)}, f32[128,1152]{1,0:T(8,128)S(1)}, u32[]{:S(2)}, u32[]{:S(2)}) %collective-permute-start.3) | collective-permute-done | bytes 589856 | tf_op jit(solution)/shard_map/ppermute | solution.py:11
  43.9 11.5 %collective-permute-start.5 = (f32[128,1152]{1,0:T(8,128)S(1)}, f32[128,1152]{1,0:T(8,128)S(1)}, u32[]{:S(2)}, u32[]{:S(2)}) collective-permute-start(f32[128,1152]{1,0:T(8,128)S(1)} %collective-permute-done.3), channel_id=1, source_target_pairs={{0,1},{1,2},{2,3},{3,4},{4,5},{5,6},{6,7},{7,8},{8,9},{9,10},{10,1... | collective-permute-start | bytes 1769480 | tf_op jit(solution)/shard_map/ppermute | solution.py:11
  56.9 3.1 collective-permute-start.14
  60.0 9.0 %collective-permute-start.4 = (f32[128]{0:T(128)S(1)}, f32[128]{0:T(128)S(1)}, u32[]{:S(2)}, u32[]{:S(2)}) collective-permute-start(f32[128]{0:T(128)S(1)} %collective-permute-done.2), channel_id=1, source_target_pairs={{0,1},{1,2},{2,3},{3,4},{4,5},{5,6},{6,7},{7,8},{8,9},{9,10},{10,1... | collective-permute-start | bytes 1544 | tf_op jit(solution)/shard_map/ppermute | solution.py:11
  69.8 4.4 %collective-permute-start.7 = (f32[128,1152]{1,0:T(8,128)S(1)}, f32[128,1152]{1,0:T(8,128)S(1)}, u32[]{:S(2)}, u32[]{:S(2)}) collective-permute-start(f32[128,1152]{1,0:T(8,128)S(1)} %collective-permute-done.5), channel_id=1, source_target_pairs={{0,1},{1,2},{2,3},{3,4},{4,5},{5,6},{6,7},{7,8},{8,9},{9,10},{10,1... | collective-permute-start | bytes 1769480 | tf_op jit(solution)/shard_map/ppermute | solution.py:11
  74.2 7.0 %collective-permute-done.4 = f32[128]{0:T(128)S(1)} collective-permute-done((f32[128]{0:T(128)S(1)}, f32[128]{0:T(128)S(1)}, u32[]{:S(2)}, u32[]{:S(2)}) %collective-permute-start.4) | collective-permute-done | bytes 544 | tf_op jit(solution)/shard_map/ppermute | solution.py:11
  82.0 4.1 %collective-permute-start.15 = (f32[128,1152]{1,0:T(8,128)S(1)}, f32[128,1152]{1,0:T(8,128)S(1)}, u32[]{:S(2)}, u32[]{:S(2)}) collective-permute-start(f32[128,1152]{1,0:T(8,128)S(1)} %fusion.48), channel_id=1, source_target_pairs={{0,1},{1,2},{2,3},{3,4},{4,5},{5,6},{6,7},{7,8},{8,9},{9,10},{10,1... | collective-permute-start | bytes 1769480 | tf_op jit(solution)/shard_map/ppermute | solution.py:11
  86.1 8.2 %collective-permute-start.6 = (f32[128]{0:T(128)S(1)}, f32[128]{0:T(128)S(1)}, u32[]{:S(2)}, u32[]{:S(2)}) collective-permute-start(f32[128]{0:T(128)S(1)} %collective-permute-done.4), channel_id=1, source_target_pairs={{0,1},{1,2},{2,3},{3,4},{4,5},{5,6},{6,7},{7,8},{8,9},{9,10},{10,1... | collective-permute-start | bytes 1544 | tf_op jit(solution)/shard_map/ppermute | solution.py:11
  94.3 12.2 %collective-permute-done.6 = f32[128]{0:T(128)S(1)} collective-permute-done((f32[128]{0:T(128)S(1)}, f32[128]{0:T(128)S(1)}, u32[]{:S(2)}, u32[]{:S(2)}) %collective-permute-start.6) | collective-permute-done | bytes 544 | tf_op jit(solution)/shard_map/ppermute | solution.py:11
  106.6 4.1 %collective-permute-start.8 = (f32[128]{0:T(128)S(1)}, f32[128]{0:T(128)S(1)}, u32[]{:S(2)}, u32[]{:S(2)}) collective-permute-start(f32[128]{0:T(128)S(1)} %collective-permute-done.6), channel_id=1, source_target_pairs={{0,1},{1,2},{2,3},{3,4},{4,5},{5,6},{6,7},{7,8},{8,9},{9,10},{10,1... | collective-permute-start | bytes 1544 | tf_op jit(solution)/shard_map/ppermute | solution.py:11
  110.6 7.9 %collective-permute-start.9 = (f32[128,1152]{1,0:T(8,128)S(1)}, f32[128,1152]{1,0:T(8,128)S(1)}, u32[]{:S(2)}, u32[]{:S(2)}) collective-permute-start(f32[128,1152]{1,0:T(8,128)S(1)} %collective-permute-done.7), channel_id=1, source_target_pairs={{0,1},{1,2},{2,3},{3,4},{4,5},{5,6},{6,7},{7,8},{8,9},{9,10},{10,1... | collective-permute-start | bytes 1769480 | tf_op jit(solution)/shard_map/ppermute | solution.py:11
  120.1 4.4 %collective-permute-start.16 = (f32[128,1152]{1,0:T(8,128)S(1)}, f32[128,1152]{1,0:T(8,128)S(1)}, u32[]{:S(2)}, u32[]{:S(2)}) collective-permute-start(f32[128,1152]{1,0:T(8,128)S(1)} %fusion.42), channel_id=1, source_target_pairs={{0,1},{1,2},{2,3},{3,4},{4,5},{5,6},{6,7},{7,8},{8,9},{9,10},{10,1... | collective-permute-start | bytes 1769480 | tf_op jit(solution)/shard_map/ppermute | solution.py:11
  127.9 4.0 %collective-permute-start.11 = (f32[128,1152]{1,0:T(8,128)S(1)}, f32[128,1152]{1,0:T(8,128)S(1)}, u32[]{:S(2)}, u32[]{:S(2)}) collective-permute-start(f32[128,1152]{1,0:T(8,128)S(1)} %collective-permute-done.9), channel_id=1, source_target_pairs={{0,1},{1,2},{2,3},{3,4},{4,5},{5,6},{6,7},{7,8},{8,9},{9,10},{10,1... | collective-permute-start | bytes 1769480 | tf_op jit(solution)/shard_map/ppermute | solution.py:11
  132.7 7.8 %collective-permute-done.16 = f32[128,1152]{1,0:T(8,128)S(1)} collective-permute-done((f32[128,1152]{1,0:T(8,128)S(1)}, f32[128,1152]{1,0:T(8,128)S(1)}, u32[]{:S(2)}, u32[]{:S(2)}) %collective-permute-start.16) | collective-permute-done | bytes 589856 | tf_op jit(solution)/shard_map/ppermute | solution.py:11
  141.2 4.3 %collective-permute-start.17 = (f32[128,1152]{1,0:T(8,128)S(1)}, f32[128,1152]{1,0:T(8,128)S(1)}, u32[]{:S(2)}, u32[]{:S(2)}) collective-permute-start(f32[128,1152]{1,0:T(8,128)S(1)} %fusion.36), channel_id=1, source_target_pairs={{0,1},{1,2},{2,3},{3,4},{4,5},{5,6},{6,7},{7,8},{8,9},{9,10},{10,1... | collective-permute-start | bytes 1769480 | tf_op jit(solution)/shard_map/ppermute | solution.py:11
  146.9 6.2 %collective-permute-done.11 = f32[128,1152]{1,0:T(8,128)S(1)} collective-permute-done((f32[128,1152]{1,0:T(8,128)S(1)}, f32[128,1152]{1,0:T(8,128)S(1)}, u32[]{:S(2)}, u32[]{:S(2)}) %collective-permute-start.11) | collective-permute-done | bytes 589856 | tf_op jit(solution)/shard_map/ppermute | solution.py:11
  155.0 10.8 %collective-permute-done.17 = f32[128,1152]{1,0:T(8,128)S(1)} collective-permute-done((f32[128,1152]{1,0:T(8,128)S(1)}, f32[128,1152]{1,0:T(8,128)S(1)}, u32[]{:S(2)}, u32[]{:S(2)}) %collective-permute-start.17) | collective-permute-done | bytes 589856 | tf_op jit(solution)/shard_map/ppermute | solution.py:11
  166.5 30.3 %collective-permute-start.18 = (f32[128,1152]{1,0:T(8,128)S(1)}, f32[128,1152]{1,0:T(8,128)}, u32[]{:S(2)}, u32[]{:S(2)}) collective-permute-start(f32[128,1152]{1,0:T(8,128)S(1)} %fusion.30), channel_id=1, source_target_pairs={{0,1018},{1,1019},{2,1020},{3,1021},{4,1022},{5,1023},{6,0},{7,1},... | collective-permute-start | bytes 1769480 | tf_op jit(solution)/shard_map/ppermute | solution.py:11
  212.2 118.0 %all-reduce = (f32[]{:T(128)}, f32[]{:T(128)}, f32[]{:T(128)}) all-reduce(f32[]{:T(128)S(6)} %multiply.8, f32[]{:T(128)S(6)} %multiply.20, f32[]{:T(128)S(6)} %add.220), channel_id=1, replica_groups=mesh['dp'=512,'mp'=2] {'dp','mp'}, use_global_device_ids=true, to_apply=%region_7.8 | all-reduce | flops 3 | bytes 24 | tf_op jit(solution)/shard_map/psum | solution.py:55
  (48 shorter events, 29.7 us)
Async XLA Ops:
  0.6 5.4 %copy-start = (f32[128,1152]{1,0:T(8,128)S(1)}, f32[128,1152]{1,0:T(8,128)}, u32[]{:S(2)}) copy-start(f32[128,1152]{1,0:T(8,128)} %param.5) | copy-start | bytes 1769476
  0.6 16.0 %collective-permute-start.1 = (f32[128,1152]{1,0:T(8,128)}, f32[128,1152]{1,0:T(8,128)S(1)}, u32[]{:S(2)}, u32[]{:S(2)}) collective-permute-start(f32[128,1152]{1,0:T(8,128)} %param.6), channel_id=1, source_target_pairs={{0,1},{1,2},{2,3},{3,4},{4,5},{5,6},{6,7},{7,8},{8,9},{9,10},{10,1... | collective-permute-start | bytes 1769480 | tf_op jit(solution)/shard_map/ppermute | solution.py:11
  6.1 1.8 copy-start.4
  8.7 13.6 %collective-permute-start.12 = (f32[128,1152]{1,0:T(8,128)S(1)}, f32[128,1152]{1,0:T(8,128)S(1)}, u32[]{:S(2)}, u32[]{:S(2)}) collective-permute-start(f32[128,1152]{1,0:T(8,128)S(1)} %convolution_multiply_fusion.6), channel_id=1, source_target_pairs={{0,1},{1,2},{2,3},{3,4},{4,5},{5,6},{6,7},{7,8},{8,9},{9,10},{10,1... | collective-permute-start | bytes 1769480 | tf_op jit(solution)/shard_map/ppermute | solution.py:11
  13.2 9.1 %collective-permute-start = (f32[128]{0:T(128)S(1)}, f32[128]{0:T(128)S(1)}, u32[]{:S(2)}, u32[]{:S(2)}) collective-permute-start(f32[128]{0:T(128)S(1)} %convert_element_type.3), channel_id=1, source_target_pairs={{0,1},{1,2},{2,3},{3,4},{4,5},{5,6},{6,7},{7,8},{8,9},{9,10},{10,1... | collective-permute-start | bytes 1544 | tf_op jit(solution)/shard_map/ppermute | solution.py:11
  17.4 25.8 %collective-permute-start.3 = (f32[128,1152]{1,0:T(8,128)S(1)}, f32[128,1152]{1,0:T(8,128)S(1)}, u32[]{:S(2)}, u32[]{:S(2)}) collective-permute-start(f32[128,1152]{1,0:T(8,128)S(1)} %collective-permute-done.1), channel_id=1, source_target_pairs={{0,1},{1,2},{2,3},{3,4},{4,5},{5,6},{6,7},{7,8},{8,9},{9,10},{10,1... | collective-permute-start | bytes 1769480 | tf_op jit(solution)/shard_map/ppermute | solution.py:11
  23.1 33.1 %collective-permute-start.13 = (f32[128,1152]{1,0:T(8,128)S(1)}, f32[128,1152]{1,0:T(8,128)S(1)}, u32[]{:S(2)}, u32[]{:S(2)}) collective-permute-start(f32[128,1152]{1,0:T(8,128)S(1)} %fusion), channel_id=1, source_target_pairs={{0,1},{1,2},{2,3},{3,4},{4,5},{5,6},{6,7},{7,8},{8,9},{9,10},{10,1... | collective-permute-start | bytes 1769480 | tf_op jit(solution)/shard_map/ppermute | solution.py:11
  28.2 27.9 %collective-permute-start.2 = (f32[128]{0:T(128)S(1)}, f32[128]{0:T(128)S(1)}, u32[]{:S(2)}, u32[]{:S(2)}) collective-permute-start(f32[128]{0:T(128)S(1)} %collective-permute-done), channel_id=1, source_target_pairs={{0,1},{1,2},{2,3},{3,4},{4,5},{5,6},{6,7},{7,8},{8,9},{9,10},{10,1... | collective-permute-start | bytes 1544 | tf_op jit(solution)/shard_map/ppermute | solution.py:11
  43.9 25.2 %collective-permute-start.5 = (f32[128,1152]{1,0:T(8,128)S(1)}, f32[128,1152]{1,0:T(8,128)S(1)}, u32[]{:S(2)}, u32[]{:S(2)}) collective-permute-start(f32[128,1152]{1,0:T(8,128)S(1)} %collective-permute-done.3), channel_id=1, source_target_pairs={{0,1},{1,2},{2,3},{3,4},{4,5},{5,6},{6,7},{7,8},{8,9},{9,10},{10,1... | collective-permute-start | bytes 1769480 | tf_op jit(solution)/shard_map/ppermute | solution.py:11
  56.9 24.3 %collective-permute-start.14 = (f32[128,1152]{1,0:T(8,128)S(1)}, f32[128,1152]{1,0:T(8,128)S(1)}, u32[]{:S(2)}, u32[]{:S(2)}) collective-permute-start(f32[128,1152]{1,0:T(8,128)S(1)} %fusion.54), channel_id=1, source_target_pairs={{0,1},{1,2},{2,3},{3,4},{4,5},{5,6},{6,7},{7,8},{8,9},{9,10},{10,1... | collective-permute-start | bytes 1769480 | tf_op jit(solution)/shard_map/ppermute | solution.py:11
  60.0 21.2 %collective-permute-start.4 = (f32[128]{0:T(128)S(1)}, f32[128]{0:T(128)S(1)}, u32[]{:S(2)}, u32[]{:S(2)}) collective-permute-start(f32[128]{0:T(128)S(1)} %collective-permute-done.2), channel_id=1, source_target_pairs={{0,1},{1,2},{2,3},{3,4},{4,5},{5,6},{6,7},{7,8},{8,9},{9,10},{10,1... | collective-permute-start | bytes 1544 | tf_op jit(solution)/shard_map/ppermute | solution.py:11
  69.8 40.8 %collective-permute-start.7 = (f32[128,1152]{1,0:T(8,128)S(1)}, f32[128,1152]{1,0:T(8,128)S(1)}, u32[]{:S(2)}, u32[]{:S(2)}) collective-permute-start(f32[128,1152]{1,0:T(8,128)S(1)} %collective-permute-done.5), channel_id=1, source_target_pairs={{0,1},{1,2},{2,3},{3,4},{4,5},{5,6},{6,7},{7,8},{8,9},{9,10},{10,1... | collective-permute-start | bytes 1769480 | tf_op jit(solution)/shard_map/ppermute | solution.py:11
  82.0 37.3 %collective-permute-start.15 = (f32[128,1152]{1,0:T(8,128)S(1)}, f32[128,1152]{1,0:T(8,128)S(1)}, u32[]{:S(2)}, u32[]{:S(2)}) collective-permute-start(f32[128,1152]{1,0:T(8,128)S(1)} %fusion.48), channel_id=1, source_target_pairs={{0,1},{1,2},{2,3},{3,4},{4,5},{5,6},{6,7},{7,8},{8,9},{9,10},{10,1... | collective-permute-start | bytes 1769480 | tf_op jit(solution)/shard_map/ppermute | solution.py:11
  86.1 20.4 %collective-permute-start.6 = (f32[128]{0:T(128)S(1)}, f32[128]{0:T(128)S(1)}, u32[]{:S(2)}, u32[]{:S(2)}) collective-permute-start(f32[128]{0:T(128)S(1)} %collective-permute-done.4), channel_id=1, source_target_pairs={{0,1},{1,2},{2,3},{3,4},{4,5},{5,6},{6,7},{7,8},{8,9},{9,10},{10,1... | collective-permute-start | bytes 1544 | tf_op jit(solution)/shard_map/ppermute | solution.py:11
  106.6 18.7 %collective-permute-start.8 = (f32[128]{0:T(128)S(1)}, f32[128]{0:T(128)S(1)}, u32[]{:S(2)}, u32[]{:S(2)}) collective-permute-start(f32[128]{0:T(128)S(1)} %collective-permute-done.6), channel_id=1, source_target_pairs={{0,1},{1,2},{2,3},{3,4},{4,5},{5,6},{6,7},{7,8},{8,9},{9,10},{10,1... | collective-permute-start | bytes 1544 | tf_op jit(solution)/shard_map/ppermute | solution.py:11
  110.6 17.3 %collective-permute-start.9 = (f32[128,1152]{1,0:T(8,128)S(1)}, f32[128,1152]{1,0:T(8,128)S(1)}, u32[]{:S(2)}, u32[]{:S(2)}) collective-permute-start(f32[128,1152]{1,0:T(8,128)S(1)} %collective-permute-done.7), channel_id=1, source_target_pairs={{0,1},{1,2},{2,3},{3,4},{4,5},{5,6},{6,7},{7,8},{8,9},{9,10},{10,1... | collective-permute-start | bytes 1769480 | tf_op jit(solution)/shard_map/ppermute | solution.py:11
  119.3 5.2 %copy-start.1 = (f32[128,1152]{1,0:T(8,128)S(1)}, f32[128,1152]{1,0:T(8,128)}, u32[]{:S(2)}) copy-start(f32[128,1152]{1,0:T(8,128)} %param.6) | copy-start | bytes 1769476
  120.1 20.3 %collective-permute-start.16 = (f32[128,1152]{1,0:T(8,128)S(1)}, f32[128,1152]{1,0:T(8,128)S(1)}, u32[]{:S(2)}, u32[]{:S(2)}) collective-permute-start(f32[128,1152]{1,0:T(8,128)S(1)} %fusion.42), channel_id=1, source_target_pairs={{0,1},{1,2},{2,3},{3,4},{4,5},{5,6},{6,7},{7,8},{8,9},{9,10},{10,1... | collective-permute-start | bytes 1769480 | tf_op jit(solution)/shard_map/ppermute | solution.py:11
  125.3 21.7 %collective-permute-start.10 = (f32[128]{0:T(128)S(1)}, f32[128]{0:T(128)S(1)}, u32[]{:S(2)}, u32[]{:S(2)}) collective-permute-start(f32[128]{0:T(128)S(1)} %collective-permute-done.8), channel_id=1, source_target_pairs={{0,1},{1,2},{2,3},{3,4},{4,5},{5,6},{6,7},{7,8},{8,9},{9,10},{10,1... | collective-permute-start | bytes 1544 | tf_op jit(solution)/shard_map/ppermute | solution.py:11
  127.9 25.2 %collective-permute-start.11 = (f32[128,1152]{1,0:T(8,128)S(1)}, f32[128,1152]{1,0:T(8,128)S(1)}, u32[]{:S(2)}, u32[]{:S(2)}) collective-permute-start(f32[128,1152]{1,0:T(8,128)S(1)} %collective-permute-done.9), channel_id=1, source_target_pairs={{0,1},{1,2},{2,3},{3,4},{4,5},{5,6},{6,7},{7,8},{8,9},{9,10},{10,1... | collective-permute-start | bytes 1769480 | tf_op jit(solution)/shard_map/ppermute | solution.py:11
  132.7 20.4 %copy-start.2 = (f32[128,128]{1,0:T(8,128)}, f32[128,128]{1,0:T(8,128)S(1)}, u32[]{:S(2)}) copy-start(f32[128,128]{1,0:T(8,128)S(1)} %fusion.65) | copy-start | bytes 196612
  141.2 24.5 %collective-permute-start.17 = (f32[128,1152]{1,0:T(8,128)S(1)}, f32[128,1152]{1,0:T(8,128)S(1)}, u32[]{:S(2)}, u32[]{:S(2)}) collective-permute-start(f32[128,1152]{1,0:T(8,128)S(1)} %fusion.36), channel_id=1, source_target_pairs={{0,1},{1,2},{2,3},{3,4},{4,5},{5,6},{6,7},{7,8},{8,9},{9,10},{10,1... | collective-permute-start | bytes 1769480 | tf_op jit(solution)/shard_map/ppermute | solution.py:11
  155.0 11.5 %copy-start.3 = (f32[128,128]{1,0:T(8,128)}, f32[128,128]{1,0:T(8,128)S(1)}, u32[]{:S(2)}) copy-start(f32[128,128]{1,0:T(8,128)S(1)} %get-tuple-element.47) | copy-start | bytes 196612
  166.5 167.9 %collective-permute-start.18 = (f32[128,1152]{1,0:T(8,128)S(1)}, f32[128,1152]{1,0:T(8,128)}, u32[]{:S(2)}, u32[]{:S(2)}) collective-permute-start(f32[128,1152]{1,0:T(8,128)S(1)} %fusion.30), channel_id=1, source_target_pairs={{0,1018},{1,1019},{2,1020},{3,1021},{4,1022},{5,1023},{6,0},{7,1},... | collective-permute-start | bytes 1769480 | tf_op jit(solution)/shard_map/ppermute | solution.py:11
where the time goes:
time: 341 us; the launch traced here: 340 us
  starting transfers between devices  127 us (37%)
  blocking collectives  118 us (35%)
  waiting for transfers between devices  51.9 us (15%)
  between operations  20.7 us (6%)
  matrix products  20.1 us (6%)
    ppermute x19, starting transfers between devices, shifted_2(): return lax.ppermute(x, axis, [(i, (i + by) % count) for i in range(count)])  127 us
    psum x1, blocking collectives, local(): lax.psum((loss_sum, scale_sum, bias_sum), ('dp', 'mp'))  118 us
    ppermute x19, waiting for transfers between devices, shifted_2(): return lax.ppermute(x, axis, [(i, (i + by) % count) for i in range(count)])  51.9 us
    dot_general x7, matrix products, local(): jnp.dot(weight, carried, precision=lax.Precision.HIGHEST, preferred_eleme...  7.41 us
    dot_general x7, matrix products, local(): lax.dot_general(image_emb, carried, (((1,), (1,)), ((), ())), precision=l...  7.41 us
  transfers between devices with their start and end apart: 19, of which 8 were waited for; matrix products, arithmetic and copies ran while one was open for 6% of the time, Pallas kernels for 0%

commit v1 on v0

v1 whole, which is shorter than its diff:
```python
import functools

import jax
import jax.numpy as jnp
from jax import lax
from jax.experimental import pallas as pl
from jax.experimental.pallas import tpu as pltpu
from jax.sharding import Mesh
from jax.sharding import PartitionSpec as P

STEPS = 7
LINES, DEEP = 16, 16
SHAPE = (2, 4, 2, 4, 4, 2, 2)
NAMES = ("y_hi", "y_lo", "x_hi", "z_hi", "z_lo", "core", "x_lo")
F32, BF16 = jnp.float32, jnp.bfloat16
VMEM = pl.BlockSpec(memory_space=pltpu.VMEM)
SMEM = pl.BlockSpec(memory_space=pltpu.SMEM)


def up(b):
    plane, pos = divmod(b, 4)
    if plane % DEEP < DEEP - 1:
        return b + 4
    return (plane + 1) % (LINES * DEEP) * 4 + (pos ^ 1)


def down(b):
    plane, pos = divmod(b, 4)
    if plane % DEEP > 0:
        return b - 4
    return (plane - 1) % (LINES * DEEP) * 4 + (pos ^ 1)


def halves(x):
    high = x.astype(BF16)
    return high, (x - high.astype(F32)).astype(BF16)


def product(a, b, dims):
    dot = functools.partial(lax.dot_general, dimension_numbers=(dims, ((), ())), preferred_element_type=F32)
    return dot(a[0], b[0]) + (dot(a[0], b[1]) + dot(a[1], b[0]))


def column(row):
    return jnp.transpose(jnp.broadcast_to(row, (row.shape[1], row.shape[1])))


def band(rows, cols, dists, own, beside, log_scale, bias):
    size, width = rows[0].shape
    left = halves(jnp.concatenate([row[...] for row in rows], 0))
    right = halves(jnp.concatenate([col[...] for col in cols], 0))
    sim = product(left, right, ((1,), (1,)))
    scale = jnp.exp(jnp.full((1, size), log_scale, F32))
    norm = 1.0 / (STEPS * size)
    loss = slope = plain = jnp.zeros((size, size), F32)
    weights = []
    for a in range(len(rows)):
        line = []
        mine = None if own[a] is None else column(own[a])
        for b in range(len(cols)):
            part = sim[a * size : (a + 1) * size, b * size : (b + 1) * size]
            dist, counts = dists[a][b]
            keep = jnp.where((dist >= 0) & (dist < STEPS) & counts, norm, 0.0).astype(F32)
            if mine is None:
                sign = -1.0
            else:
                other = jnp.where(dist == 0, own[a], jnp.where(dist == 1, beside[a], -1.0))
                sign = jnp.where(mine == other, 1.0, -1.0)
            u = sign * (scale * part + bias)
            small = jnp.exp(-jnp.abs(u))
            weight = -sign * (jnp.where(u >= 0, small, 1.0) / (1.0 + small)) * keep
            loss = loss + (jnp.maximum(-u, 0.0) + jnp.log1p(small)) * keep
            slope = slope + weight * part
            plain = plain + weight
            line.append(weight)
        weights.append(jnp.concatenate(line, 1))
    grads = product(halves(jnp.concatenate(weights, 0)), right, ((1,), (0,)))
    return jnp.exp(jnp.full((1, width), log_scale, F32)) * grads, (loss, scale * slope, plain)


def totals(sums):
    lane = lax.broadcasted_iota(jnp.int32, (1, 128), 1)
    loss, slope, plain = (jnp.sum(part) for part in sums)
    return jnp.where(lane == 0, loss, jnp.where(lane == 1, slope, jnp.where(lane == 2, plain, 0.0)))


def tags(ids):
    own = ids[0:1, :], ids[8:9, :], None
    before = ids[1:2, :], ids[9:10, :], None
    after = ids[2:3, :], ids[10:11, :], None
    return own, before, after


def plane_kernel(place, params, ids, i0, i1, i2, t0, t1, t2, images, texts, sums):
    own, before, after = tags(ids)
    p = place[0]
    rows, cols = (p, p ^ 2), (p, p ^ 1)
    dists = [[(i - t, True) for t in cols] for i in rows]
    images[...], parts = band((i0, i2), (t0, t1), dists, own, before, params[0], params[1])
    sums[...] = totals(parts)
    dists = [[(i - t, True) for i in cols] for t in rows]
    texts[...], _ = band((t0, t2), (i0, i1), dists, own, after, params[0], params[1])


def lower_kernel(place, params, ids, i0, i2, cross, u0, u1, images_in, sums_in, images, sums):
    own, before, _ = tags(ids)
    p, q, r, core = place[0], place[1], place[2], place[3]
    dists = [[(i + 4 - t, True) for t in (q, q ^ 1)] for i in (p, p ^ 2)]
    dists.append([((r ^ 2) + 8 - t, core == 1) for t in (q, q ^ 1)])
    grads, parts = band((i0, i2, cross), (u0, u1), dists, own, before, params[0], params[1])
    both = images_in.shape[0]
    images[0:both, :] = images_in[...] + grads[0:both, :]
    images[both:, :] = grads[both:, :]
    sums[...] = sums_in[...] + totals(parts)


def upper_kernel(place, params, ids, t0, t2, cross, d0, d1, texts_in, images_in, texts, swap, far):
    own, _, after = tags(ids)
    p, q, r, core = place[0], place[1], place[2], place[3]
    dists = [[(i + 4 - t, True) for i in (r, r ^ 1)] for t in (p, p ^ 2)]
    dists.append([(i + 8 - (q ^ 2), core == 0) for i in (r, r ^ 1)])
    grads, _ = band((t0, t2, cross), (d0, d1), dists, own, after, params[0], params[1])
    size = texts.shape[0]
    texts[...] = texts_in[0:size, :] + grads[0:size, :]
    swap[0:size, :] = images_in[size : 2 * size, :]
    swap[size:, :] = texts_in[size:, :] + grads[size : 2 * size, :]
    far[...] = jnp.where(core == 1, images_in[2 * size :, :], grads[2 * size :, :])


def kernel_call(body, name, shapes, rows, cols, passes):
    size, width = 128, 1152
    cost = pl.CostEstimate(
        flops=12 * passes * rows * cols * width,
        bytes_accessed=4 * width * (rows + cols) * 2,
        transcendentals=2 * rows * cols,
    )
    return lambda place, params, *blocks: pl.pallas_call(
        body,
        out_shape=[jax.ShapeDtypeStruct(shape, F32) for shape in shapes],
        in_specs=[SMEM, SMEM] + [VMEM] * len(blocks),
        out_specs=[VMEM] * len(shapes),
        compiler_params=pltpu.CompilerParams(vmem_limit_bytes=48 << 20),
        cost_estimate=cost,
        name=name,
    )(place, params, *blocks)


def local(image, text, video_ids, log_scale, bias):
    size, width = image.shape
    count = lax.axis_size(NAMES)
    everyone = range(count)

    def send(x, to):
        return lax.ppermute(x, NAMES, [(b, to(b)) for b in everyone])

    def other_core(x):
        return send(x, lambda b: b ^ 2)

    plane_z = lax.axis_index(("z_hi", "z_lo"))
    core = lax.axis_index("core")
    p = 2 * core + lax.axis_index("x_lo")
    q = jnp.where(plane_z > 0, p, p ^ 1)
    r = jnp.where(plane_z < DEEP - 1, p, p ^ 1)
    place = jnp.stack([p, q, r, core]).astype(jnp.int32)
    params = jnp.stack([log_scale, bias])

    t0, i0 = text, image
    u0 = send(t0, up)
    t1 = send(t0, lambda b: b ^ 1)
    d0 = send(i0, down)
    i1 = send(i0, lambda b: b ^ 1)
    t2, i2 = other_core(t0), other_core(i0)
    u1 = send(t1, up)
    d1 = send(i1, down)
    cross = other_core(jnp.where(core == 1, u0, d0))

    ids = video_ids.astype(F32)[None]
    before = send(ids, lambda b: (b + 1) % count)
    after = send(ids, lambda b: (b - 1) % count)
    mine = jnp.concatenate([ids, before, after, jnp.zeros((5, size), F32)], 0)
    ids = jnp.concatenate([mine, other_core(mine)], 0)

    wide = lambda n: (n * size, width)
    images, texts, sums = kernel_call(plane_kernel, "plane", (wide(2), wide(2), (1, 128)), 256, 256, 2)(
        place, params, ids, i0, i1, i2, t0, t1, t2
    )
    images, sums = kernel_call(lower_kernel, "lower", (wide(3), (1, 128)), 384, 256, 1)(
        place, params, ids, i0, i2, cross, u0, u1, images, sums
    )
    sums = lax.psum(lax.psum(sums, "core"), ("x_hi", "x_lo"))
    d1, sums = lax.optimization_barrier((d1, sums))
    texts, swap, far = kernel_call(upper_kernel, "upper", (wide(1), wide(2), wide(1)), 384, 256, 1)(
        place, params, ids, t0, t2, cross, d0, d1, texts, images
    )
    swap = other_core(swap)
    far = send(far, lambda b: (down(b) if b % 4 < 2 else up(b)) ^ 2)
    sums = lax.psum(lax.psum(lax.psum(sums, "z_lo"), "z_hi"), ("y_hi", "y_lo"))
    grad_image = images[:size] + swap[:size] + jnp.where(core == 0, far, 0.0)
    grad_text = texts + swap[size:] + jnp.where(core == 1, far, 0.0)
    tokens = size * count
    return sums[0, 0] / tokens, grad_image, grad_text, sums[0, 1] / tokens, sums[0, 2] / tokens


def solution(mesh):
    fine = Mesh(mesh.devices.reshape(SHAPE), NAMES)
    rows = P(NAMES, None)
    return jax.shard_map(
        local,
        mesh=fine,
        in_specs=(rows, rows, P(NAMES), P(), P()),
        out_specs=(P(), rows, rows, P(), P()),
        check_vma=False,
    )
```

time: 341 us -> 155 us (0.45)
  the two profiles are of different devices: /device:TPU:1 before, /device:TPU:64 now
where the time goes in v1:
time: 155 us; the launch traced here: 154 us
  starting transfers between devices  62.8 us (41%)
  blocking collectives  49.1 us (32%)
  Pallas kernels  17.5 us (11%)
  between operations  7.57 us (5%)
  waiting for transfers between devices  6.62 us (4%)
  local copies, waits for them, and re-layouts  6.38 us (4%)
  other arithmetic  3.92 us (3%)
    ppermute x14, starting transfers between devices, send(): return lax.ppermute(x, NAMES, [(b, to(b)) for b in everyone])  62.8 us
    psum x3, blocking collectives, local(): sums = lax.psum(lax.psum(lax.psum(sums, 'z_lo'), 'z_hi'), ('y_hi', 'y_lo'))  38 us
    pallas_call x3, Pallas kernels, kernel_call(): pl.pallas_call(body, out_shape=[jax.ShapeDtypeStruct(shape, F32) for shap...  17.5 us
    psum x2, blocking collectives, local(): sums = lax.psum(lax.psum(sums, 'core'), ('x_hi', 'x_lo'))  11.1 us
    ppermute x14, waiting for transfers between devices, send(): return lax.ppermute(x, NAMES, [(b, to(b)) for b in everyone])  6.62 us
    unnamed x22, local copies, waits for them, and re-layouts  4.4 us
  transfers between devices with their start and end apart: 14, of which 2 were waited for; matrix products, arithmetic and copies ran while one was open for 2% of the time, Pallas kernels for 7%

profile of v1, /device:TPU:64, one launch (start us, length us, event | category | flops | bytes accessed | tf_op | source)
XLA Modules:
  0.0 153.8 jit_solution(12912275098452224360)
XLA Ops:
  0.6 14.3 %collective-permute-start.7 = (f32[128,1152]{1,0:T(8,128)}, f32[128,1152]{1,0:T(8,128)S(1)}, u32[]{:S(2)}, u32[]{:S(2)}) collective-permute-start(f32[128,1152]{1,0:T(8,128)} %i0.3), channel_id=1, source_target_pairs={{0,1021},{1,1020},{2,1023},{3,1022},{4,0},{5,1},{6,2},{7,3},{8,4},... | collective-permute-start | bytes 1769480 | tf_op jit(solution)/shard_map/ppermute | solution.py:154
  15.0 1.9 %collective-permute-start.9 = (f32[128,1152]{1,0:T(8,128)}, f32[128,1152]{1,0:T(8,128)}, u32[]{:S(2)}, u32[]{:S(2)}) collective-permute-start(f32[128,1152]{1,0:T(8,128)} %t0.3), channel_id=1, source_target_pairs={{0,1},{1,0},{2,3},{3,2},{4,5},{5,4},{6,7},{7,6},{8,9},{9,8},{10,11... | collective-permute-start | bytes 1769480 | tf_op jit(solution)/shard_map/ppermute | solution.py:154
  16.9 1.9 %collective-permute-start.6 = (f32[128,1152]{1,0:T(8,128)}, f32[128,1152]{1,0:T(8,128)S(1)}, u32[]{:S(2)}, u32[]{:S(2)}) collective-permute-start(f32[128,1152]{1,0:T(8,128)} %t0.3), channel_id=1, source_target_pairs={{0,4},{1,5},{2,6},{3,7},{4,8},{5,9},{6,10},{7,11},{8,12},{9,13},{1... | collective-permute-start | bytes 1769480 | tf_op jit(solution)/shard_map/ppermute | solution.py:154
  19.5 11.0 %collective-permute-start.3 = (f32[1,128]{1,0:T(1,128)S(1)}, f32[1,128]{1,0:T(1,128)S(1)}, u32[]{:S(2)}, u32[]{:S(2)}) collective-permute-start(f32[1,128]{1,0:T(1,128)S(1)} %convert_bitcast_fusion), channel_id=1, source_target_pairs={{0,1023},{1,0},{2,1},{3,2},{4,3},{5,4},{6,5},{7,6},{8,7},{9,8},{10... | collective-permute-start | bytes 1544 | tf_op jit(solution)/shard_map/ppermute | solution.py:154
  30.5 1.9 %collective-permute-start.2 = (f32[1,128]{1,0:T(1,128)S(1)}, f32[1,128]{1,0:T(1,128)S(1)}, u32[]{:S(2)}, u32[]{:S(2)}) collective-permute-start(f32[1,128]{1,0:T(1,128)S(1)} %convert_bitcast_fusion), channel_id=1, source_target_pairs={{0,1},{1,2},{2,3},{3,4},{4,5},{5,6},{6,7},{7,8},{8,9},{9,10},{10,1... | collective-permute-start | bytes 1544 | tf_op jit(solution)/shard_map/ppermute | solution.py:154
  32.5 1.9 %collective-permute-start.5 = (f32[128,1152]{1,0:T(8,128)}, f32[128,1152]{1,0:T(8,128)}, u32[]{:S(2)}, u32[]{:S(2)}) collective-permute-start(f32[128,1152]{1,0:T(8,128)} %i0.3), channel_id=1, source_target_pairs={{0,2},{1,3},{2,0},{3,1},{4,6},{5,7},{6,4},{7,5},{8,10},{9,11},{10,... | collective-permute-start | bytes 1769480 | tf_op jit(solution)/shard_map/ppermute | solution.py:154
  34.4 6.1 %collective-permute-done.2 = f32[1,128]{1,0:T(1,128)S(1)} collective-permute-done((f32[1,128]{1,0:T(1,128)S(1)}, f32[1,128]{1,0:T(1,128)S(1)}, u32[]{:S(2)}, u32[]{:S(2)}) %collective-permute-start.2) | collective-permute-done | bytes 544 | tf_op jit(solution)/shard_map/ppermute | solution.py:154
  40.5 1.9 %collective-permute-start = (f32[128,1152]{1,0:T(8,128)}, f32[128,1152]{1,0:T(8,128)}, u32[]{:S(2)}, u32[]{:S(2)}) collective-permute-start(f32[128,1152]{1,0:T(8,128)} %i0.3), channel_id=1, source_target_pairs={{0,1},{1,0},{2,3},{3,2},{4,5},{5,4},{6,7},{7,6},{8,9},{9,8},{10,11... | collective-permute-start | bytes 1769480 | tf_op jit(solution)/shard_map/ppermute | solution.py:154
  43.1 1.9 %collective-permute-start.11 = (f32[128,1152]{1,0:T(8,128)}, f32[128,1152]{1,0:T(8,128)S(1)}, u32[]{:S(2)}, u32[]{:S(2)}) collective-permute-start(f32[128,1152]{1,0:T(8,128)} %t0.3), channel_id=1, source_target_pairs={{0,2},{1,3},{2,0},{3,1},{4,6},{5,7},{6,4},{7,5},{8,10},{9,11},{10,... | collective-permute-start | bytes 1769480 | tf_op jit(solution)/shard_map/ppermute | solution.py:154
  45.0 2.4 %collective-permute-start.4 = (f32[8,128]{1,0:T(8,128)S(1)}, f32[8,128]{1,0:T(8,128)S(1)}, u32[]{:S(2)}, u32[]{:S(2)}) collective-permute-start(f32[8,128]{1,0:T(8,128)S(1)} %pad_maximum_fusion), channel_id=1, source_target_pairs={{0,2},{1,3},{2,0},{3,1},{4,6},{5,7},{6,4},{7,5},{8,10},{9,11},{10,... | collective-permute-start | bytes 12296 | tf_op jit(solution)/shard_map/ppermute | solution.py:154
  47.4 1.9 %collective-permute-start.10 = (f32[128,1152]{1,0:T(8,128)}, f32[128,1152]{1,0:T(8,128)}, u32[]{:S(2)}, u32[]{:S(2)}) collective-permute-start(f32[128,1152]{1,0:T(8,128)} %collective-permute-done.9.t1), channel_id=1, source_target_pairs={{0,4},{1,5},{2,6},{3,7},{4,8},{5,9},{6,10},{7,11},{8,12},{9,13},{1... | collective-permute-start | bytes 1769480 | tf_op jit(solution)/shard_map/ppermute | solution.py:154
  50.2 1.9 %collective-permute-start.8 = (f32[128,1152]{1,0:T(8,128)}, f32[128,1152]{1,0:T(8,128)S(1)}, u32[]{:S(2)}, u32[]{:S(2)}) collective-permute-start(f32[128,1152]{1,0:T(8,128)} %broadcast_select_fusion), channel_id=1, source_target_pairs={{0,2},{1,3},{2,0},{3,1},{4,6},{5,7},{6,4},{7,5},{8,10},{9,11},{10,... | collective-permute-start | bytes 1769480 | tf_op jit(solution)/shard_map/ppermute | solution.py:154
  52.6 9.9 %collective-permute-start.1 = (f32[128,1152]{1,0:T(8,128)}, f32[128,1152]{1,0:T(8,128)S(1)}, u32[]{:S(2)}, u32[]{:S(2)}) collective-permute-start(f32[128,1152]{1,0:T(8,128)} %collective-permute-done.i1), channel_id=1, source_target_pairs={{0,1021},{1,1020},{2,1023},{3,1022},{4,0},{5,1},{6,2},{7,3},{8,4},... | collective-permute-start | bytes 1769480 | tf_op jit(solution)/shard_map/ppermute | solution.py:154
  66.5 6.2 %plane.1 = (f32[256,1152]{1,0:T(8,128)S(1)}, f32[256,1152]{1,0:T(8,128)S(1)}, f32[1,128]{1,0:T(1,128)S(1)}) custom-call(s32[4]{0:T(128)S(1)} %pad_add_fusion.place, f32[2]{0:T(128)S(1)} %pad_maximum_fusion.1.params, f32[16,128]{1,0:T(8,128)S(1)} %concatenate.8.ids, f32[128,1152]{1,0:T(8,128)S(1)} %copy-done.3, f32[128,1152]{1,0:T(8,128)} %collective-permute-done.i1, ...), custom_call_target="tpu_custom_call" | custom-call | flops 1811939328 | bytes 4718592 | tf_op jit(solution)/shard_map/plane/pallas_call | solution.py:137
  73.8 4.9 %lower.1 = (f32[384,1152]{1,0:T(8,128)S(1)}, f32[1,128]{1,0:T(1,128)S(1)}) custom-call(s32[4]{0:T(128)S(1)} %pad_add_fusion.place, f32[2]{0:T(128)S(1)} %pad_maximum_fusion.1.params, f32[16,128]{1,0:T(8,128)S(1)} %concatenate.8.ids, f32[128,1152]{1,0:T(8,128)S(1)} %copy-done.4, f32[128,1152]{1,0:T(8,128)} %collective-permute-done.5.i2, ...), custom_call_target="tpu_custom_call" | custom-call | flops 1358954496 | bytes 5898240 | tf_op jit(solution)/shard_map/lower/pallas_call | solution.py:137
  80.4 2.6 %psum.35 = f32[1,128]{1,0:T(1,128)S(1)} all-reduce(f32[1,128]{1,0:T(1,128)} %copy-done.5), channel_id=1, replica_groups=mesh['y_hi'=2,'y_lo'=4,'x_hi'=2,'z_hi'=4,'z_lo'=4,'core'=2,'x_lo'=2] {'c..., use_global_device_ids=true, to_apply=%region_0.1 | all-reduce | flops 128 | bytes 1024 | tf_op jit(solution)/shard_map/psum | solution.py:190
  83.0 8.5 %psum.36 = f32[1,128]{1,0:T(1,128)} all-reduce(f32[1,128]{1,0:T(1,128)S(1)} %psum.35), channel_id=1, replica_groups=mesh['y_hi'=2,'y_lo'=4,'x_hi'=2,'z_hi'=4,'z_lo'=4,'core'=2,'x_lo'=2] {'x..., use_global_device_ids=true, to_apply=%region_1.2 | all-reduce | flops 128 | bytes 1024 | tf_op jit(solution)/shard_map/psum | solution.py:190
  91.5 6.4 %upper.1 = (f32[128,1152]{1,0:T(8,128)S(1)}, f32[256,1152]{1,0:T(8,128)}, f32[128,1152]{1,0:T(8,128)}) custom-call(s32[4]{0:T(128)S(1)} %pad_add_fusion.place, f32[2]{0:T(128)S(1)} %pad_maximum_fusion.1.params, f32[16,128]{1,0:T(8,128)S(1)} %concatenate.8.ids, f32[128,1152]{1,0:T(8,128)S(1)} %copy-done.2, f32[128,1152]{1,0:T(8,128)S(1)} %collective-permute-done.11.t2, ...), custom_call_target="tpu_custom_call" | custom-call | flops 1358954496 | bytes 5898240 | tf_op jit(solution)/shard_map/upper/pallas_call | solution.py:137
  97.9 1.9 %collective-permute-start.12 = (f32[256,1152]{1,0:T(8,128)}, f32[256,1152]{1,0:T(8,128)S(1)}, u32[]{:S(2)}, u32[]{:S(2)}) collective-permute-start(f32[256,1152]{1,0:T(8,128)} %get-tuple-element.22), channel_id=1, source_target_pairs={{0,2},{1,3},{2,0},{3,1},{4,6},{5,7},{6,4},{7,5},{8,10},{9,11},{10,... | collective-permute-start | bytes 3538952 | tf_op jit(solution)/shard_map/ppermute | solution.py:154
  99.8 7.8 %collective-permute-start.13 = (f32[128,1152]{1,0:T(8,128)}, f32[128,1152]{1,0:T(8,128)S(1)}, u32[]{:S(2)}, u32[]{:S(2)}) collective-permute-start(f32[128,1152]{1,0:T(8,128)} %get-tuple-element.23), channel_id=1, source_target_pairs={{0,1023},{1,1022},{2,4},{3,5},{4,2},{5,3},{6,8},{7,9},{8,6},{9,7},... | collective-permute-start | bytes 1769480 | tf_op jit(solution)/shard_map/ppermute | solution.py:154
  107.6 11.8 %psum.37 = f32[1,128]{1,0:T(1,128)S(1)} all-reduce(f32[1,128]{1,0:T(1,128)} %psum.36), channel_id=1, replica_groups=mesh['y_hi'=2,'y_lo'=4,'x_hi'=2,'z_hi'=4,'z_lo'=4,'core'=2,'x_lo'=2] {'z..., use_global_device_ids=true, to_apply=%region_2.3 | all-reduce | flops 128 | bytes 1024 | tf_op jit(solution)/shard_map/psum | solution.py:197
  119.5 10.4 %psum.38 = f32[1,128]{1,0:T(1,128)S(1)} all-reduce(f32[1,128]{1,0:T(1,128)S(1)} %psum.37), channel_id=1, replica_groups=mesh['y_hi'=2,'y_lo'=4,'x_hi'=2,'z_hi'=4,'z_lo'=4,'core'=2,'x_lo'=2] {'z..., use_global_device_ids=true, to_apply=%region_3.4 | all-reduce | flops 128 | bytes 1024 | tf_op jit(solution)/shard_map/psum | solution.py:197
  129.9 15.7 %psum.39 = f32[1,128]{1,0:T(1,128)S(1)} all-reduce(f32[1,128]{1,0:T(1,128)S(1)} %psum.38), channel_id=1, replica_groups=mesh['y_hi'=2,'y_lo'=4,'x_hi'=2,'z_hi'=4,'z_lo'=4,'core'=2,'x_lo'=2] {'y..., use_global_device_ids=true, to_apply=%region_4.5 | all-reduce | flops 128 | bytes 1024 | tf_op jit(solution)/shard_map/psum | solution.py:197
  148.2 2.2 %fusion = (f32[128,1152]{1,0:T(8,128)}, f32[128,1152]{1,0:T(8,128)}) fusion(f32[128,1152]{1,0:T(8,128)S(1)} %get-tuple-element.24, f32[256,1152]{1,0:T(8,128)S(1)} %collective-permute-done.12, f32[128,1152]{1,0:T(8,128)S(1)} %collective-permute-done.13, pred[]{:T(512)S(6)} %eq.7, pred[]{:T(512)S(6)} %eq.8, f32[384,1152]{1,0:T(8,128)} %copy-done), kind=kLoop, calls=%fused_computation.1 | loop fusion | flops 884736 | bytes 4128770 | tf_op jit(solution)/shard_map/add | solution.py:199
  (43 shorter events, 8.6 us)
Async XLA Ops:
  0.6 64.8 %copy-start.2 = (f32[128,1152]{1,0:T(8,128)S(1)}, f32[128,1152]{1,0:T(8,128)}, u32[]{:S(2)}) copy-start(f32[128,1152]{1,0:T(8,128)} %t0.3) | copy-start | bytes 1769476
  0.6 42.4 %collective-permute-start.7 = (f32[128,1152]{1,0:T(8,128)}, f32[128,1152]{1,0:T(8,128)S(1)}, u32[]{:S(2)}, u32[]{:S(2)}) collective-permute-start(f32[128,1152]{1,0:T(8,128)} %i0.3), channel_id=1, source_target_pairs={{0,1021},{1,1020},{2,1023},{3,1022},{4,0},{5,1},{6,2},{7,3},{8,4},... | collective-permute-start | bytes 1769480 | tf_op jit(solution)/shard_map/ppermute | solution.py:154
  15.0 30.0 %collective-permute-start.9 = (f32[128,1152]{1,0:T(8,128)}, f32[128,1152]{1,0:T(8,128)}, u32[]{:S(2)}, u32[]{:S(2)}) collective-permute-start(f32[128,1152]{1,0:T(8,128)} %t0.3), channel_id=1, source_target_pairs={{0,1},{1,0},{2,3},{3,2},{4,5},{5,4},{6,7},{7,6},{8,9},{9,8},{10,11... | collective-permute-start | bytes 1769480 | tf_op jit(solution)/shard_map/ppermute | solution.py:154
  16.9 30.5 %collective-permute-start.6 = (f32[128,1152]{1,0:T(8,128)}, f32[128,1152]{1,0:T(8,128)S(1)}, u32[]{:S(2)}, u32[]{:S(2)}) collective-permute-start(f32[128,1152]{1,0:T(8,128)} %t0.3), channel_id=1, source_target_pairs={{0,4},{1,5},{2,6},{3,7},{4,8},{5,9},{6,10},{7,11},{8,12},{9,13},{1... | collective-permute-start | bytes 1769480 | tf_op jit(solution)/shard_map/ppermute | solution.py:154
  19.5 23.0 %copy-start.8 = (f32[1,128]{1,0:T(1,128)}, f32[1,128]{1,0:T(1,128)S(1)}, u32[]{:S(2)}) copy-start(f32[1,128]{1,0:T(1,128)S(1)} %convert_bitcast_fusion) | copy-start | bytes 1540
  19.5 12.9 %collective-permute-start.3 = (f32[1,128]{1,0:T(1,128)S(1)}, f32[1,128]{1,0:T(1,128)S(1)}, u32[]{:S(2)}, u32[]{:S(2)}) collective-permute-start(f32[1,128]{1,0:T(1,128)S(1)} %convert_bitcast_fusion), channel_id=1, source_target_pairs={{0,1023},{1,0},{2,1},{3,2},{4,3},{5,4},{6,5},{7,6},{8,7},{9,8},{10... | collective-permute-start | bytes 1544 | tf_op jit(solution)/shard_map/ppermute | solution.py:154
  30.5 10.0 %collective-permute-start.2 = (f32[1,128]{1,0:T(1,128)S(1)}, f32[1,128]{1,0:T(1,128)S(1)}, u32[]{:S(2)}, u32[]{:S(2)}) collective-permute-start(f32[1,128]{1,0:T(1,128)S(1)} %convert_bitcast_fusion), channel_id=1, source_target_pairs={{0,1},{1,2},{2,3},{3,4},{4,5},{5,6},{6,7},{7,8},{8,9},{9,10},{10,1... | collective-permute-start | bytes 1544 | tf_op jit(solution)/shard_map/ppermute | solution.py:154
  32.5 10.1 %copy-start.9 = (f32[1,128]{1,0:T(1,128)}, f32[1,128]{1,0:T(1,128)S(1)}, u32[]{:S(2)}) copy-start(f32[1,128]{1,0:T(1,128)S(1)} %collective-permute-done.3) | copy-start | bytes 1540
  32.5 32.9 %collective-permute-start.5 = (f32[128,1152]{1,0:T(8,128)}, f32[128,1152]{1,0:T(8,128)}, u32[]{:S(2)}, u32[]{:S(2)}) collective-permute-start(f32[128,1152]{1,0:T(8,128)} %i0.3), channel_id=1, source_target_pairs={{0,2},{1,3},{2,0},{3,1},{4,6},{5,7},{6,4},{7,5},{8,10},{9,11},{10,... | collective-permute-start | bytes 1769480 | tf_op jit(solution)/shard_map/ppermute | solution.py:154
  40.5 2.0 %copy-start.10 = (f32[1,128]{1,0:T(1,128)}, f32[1,128]{1,0:T(1,128)S(1)}, u32[]{:S(2)}) copy-start(f32[1,128]{1,0:T(1,128)S(1)} %collective-permute-done.2) | copy-start | bytes 1540
  40.5 12.1 %collective-permute-start = (f32[128,1152]{1,0:T(8,128)}, f32[128,1152]{1,0:T(8,128)}, u32[]{:S(2)}, u32[]{:S(2)}) collective-permute-start(f32[128,1152]{1,0:T(8,128)} %i0.3), channel_id=1, source_target_pairs={{0,1},{1,0},{2,3},{3,2},{4,5},{5,4},{6,7},{7,6},{8,9},{9,8},{10,11... | collective-permute-start | bytes 1769480 | tf_op jit(solution)/shard_map/ppermute | solution.py:154
  42.5 0.6 copy-start.6
  43.1 22.4 %collective-permute-start.11 = (f32[128,1152]{1,0:T(8,128)}, f32[128,1152]{1,0:T(8,128)S(1)}, u32[]{:S(2)}, u32[]{:S(2)}) collective-permute-start(f32[128,1152]{1,0:T(8,128)} %t0.3), channel_id=1, source_target_pairs={{0,2},{1,3},{2,0},{3,1},{4,6},{5,7},{6,4},{7,5},{8,10},{9,11},{10,... | collective-permute-start | bytes 1769480 | tf_op jit(solution)/shard_map/ppermute | solution.py:154
  45.0 5.2 %collective-permute-start.4 = (f32[8,128]{1,0:T(8,128)S(1)}, f32[8,128]{1,0:T(8,128)S(1)}, u32[]{:S(2)}, u32[]{:S(2)}) collective-permute-start(f32[8,128]{1,0:T(8,128)S(1)} %pad_maximum_fusion), channel_id=1, source_target_pairs={{0,2},{1,3},{2,0},{3,1},{4,6},{5,7},{6,4},{7,5},{8,10},{9,11},{10,... | collective-permute-start | bytes 12296 | tf_op jit(solution)/shard_map/ppermute | solution.py:154
  47.4 26.3 %collective-permute-start.10 = (f32[128,1152]{1,0:T(8,128)}, f32[128,1152]{1,0:T(8,128)}, u32[]{:S(2)}, u32[]{:S(2)}) collective-permute-start(f32[128,1152]{1,0:T(8,128)} %collective-permute-done.9.t1), channel_id=1, source_target_pairs={{0,4},{1,5},{2,6},{3,7},{4,8},{5,9},{6,10},{7,11},{8,12},{9,13},{1... | collective-permute-start | bytes 1769480 | tf_op jit(solution)/shard_map/ppermute | solution.py:154
  50.2 1.9 %copy-start.7 = (f32[8,128]{1,0:T(8,128)}, f32[8,128]{1,0:T(8,128)S(1)}, u32[]{:S(2)}) copy-start(f32[8,128]{1,0:T(8,128)S(1)} %collective-permute-done.4) | copy-start | bytes 12292
  50.2 23.5 %collective-permute-start.8 = (f32[128,1152]{1,0:T(8,128)}, f32[128,1152]{1,0:T(8,128)S(1)}, u32[]{:S(2)}, u32[]{:S(2)}) collective-permute-start(f32[128,1152]{1,0:T(8,128)} %broadcast_select_fusion), channel_id=1, source_target_pairs={{0,2},{1,3},{2,0},{3,1},{4,6},{5,7},{6,4},{7,5},{8,10},{9,11},{10,... | collective-permute-start | bytes 1769480 | tf_op jit(solution)/shard_map/ppermute | solution.py:154
  52.6 38.8 %collective-permute-start.1 = (f32[128,1152]{1,0:T(8,128)}, f32[128,1152]{1,0:T(8,128)S(1)}, u32[]{:S(2)}, u32[]{:S(2)}) collective-permute-start(f32[128,1152]{1,0:T(8,128)} %collective-permute-done.i1), channel_id=1, source_target_pairs={{0,1021},{1,1020},{2,1023},{3,1022},{4,0},{5,1},{6,2},{7,3},{8,4},... | collective-permute-start | bytes 1769480 | tf_op jit(solution)/shard_map/ppermute | solution.py:154
  65.4 1.1 copy-start.3
  66.5 7.3 %copy-start.4 = (f32[128,1152]{1,0:T(8,128)S(1)}, f32[128,1152]{1,0:T(8,128)}, u32[]{:S(2)}) copy-start(f32[128,1152]{1,0:T(8,128)} %i0.3) | copy-start | bytes 1769476
  72.7 1.0 copy-start.1
  78.6 1.2 copy-start
  97.9 50.3 %collective-permute-start.12 = (f32[256,1152]{1,0:T(8,128)}, f32[256,1152]{1,0:T(8,128)S(1)}, u32[]{:S(2)}, u32[]{:S(2)}) collective-permute-start(f32[256,1152]{1,0:T(8,128)} %get-tuple-element.22), channel_id=1, source_target_pairs={{0,2},{1,3},{2,0},{3,1},{4,6},{5,7},{6,4},{7,5},{8,10},{9,11},{10,... | collective-permute-start | bytes 3538952 | tf_op jit(solution)/shard_map/ppermute | solution.py:154
  99.8 48.4 %collective-permute-start.13 = (f32[128,1152]{1,0:T(8,128)}, f32[128,1152]{1,0:T(8,128)S(1)}, u32[]{:S(2)}, u32[]{:S(2)}) collective-permute-start(f32[128,1152]{1,0:T(8,128)} %get-tuple-element.23), channel_id=1, source_target_pairs={{0,1023},{1,1022},{2,4},{3,5},{4,2},{5,3},{6,8},{7,9},{8,6},{9,7},... | collective-permute-start | bytes 1769480 | tf_op jit(solution)/shard_map/ppermute | solution.py:154
  (1 other events, 0.5 us)

commit v2 on v1

v2 whole, which is shorter than its diff:
```python
import functools

import jax
import jax.numpy as jnp
from jax import lax
from jax.experimental import pallas as pl
from jax.experimental.pallas import tpu as pltpu
from jax.sharding import Mesh
from jax.sharding import PartitionSpec as P

STEPS = 7
LINES, DEEP = 16, 16
SHAPE = (2, 4, 2, 4, 4, 2, 2)
NAMES = ("y_hi", "y_lo", "x_hi", "z_hi", "z_lo", "core", "x_lo")
F32, BF16 = jnp.float32, jnp.bfloat16
VMEM = pl.BlockSpec(memory_space=pltpu.VMEM)
SMEM = pl.BlockSpec(memory_space=pltpu.SMEM)


def up(b):
    plane, pos = divmod(b, 4)
    if plane % DEEP < DEEP - 1:
        return b + 4
    return (plane + 1) % (LINES * DEEP) * 4 + (pos ^ 1)


def down(b):
    plane, pos = divmod(b, 4)
    if plane % DEEP > 0:
        return b - 4
    return (plane - 1) % (LINES * DEEP) * 4 + (pos ^ 1)


def halves(x):
    high = x.astype(BF16)
    return high, (x - high.astype(F32)).astype(BF16)


def joined(*pairs):
    return tuple(jnp.concatenate(parts, 0) for parts in zip(*pairs))


def product(a, b, dims):
    dot = functools.partial(lax.dot_general, dimension_numbers=(dims, ((), ())), preferred_element_type=F32)
    return dot(a[0], b[0]) + (dot(a[0], b[1]) + dot(a[1], b[0]))


def gradient(weights, cols, log_scale):
    grads = product(halves(weights), cols, ((1,), (0,)))
    return jnp.exp(jnp.full((1, grads.shape[1]), log_scale, F32)) * grads


def column(row):
    return jnp.transpose(jnp.broadcast_to(row, (row.shape[1], row.shape[1])))


def weigh(sim, dists, own, before, log_scale, bias, tokens):
    size = 128
    scale = jnp.exp(jnp.full((1, size), log_scale, F32))
    norm = 1.0 / (STEPS * size)
    loss = slope = plain = jnp.zeros((size, size), F32)
    weights = []
    for a, row in enumerate(dists):
        line = []
        mine = None if own[a] is None else column(own[a])
        for b, (dist, counts) in enumerate(row):
            part = sim[a * size : (a + 1) * size, b * size : (b + 1) * size]
            keep = jnp.where((dist >= 0) & (dist < STEPS) & counts, norm, 0.0).astype(F32)
            if mine is None:
                sign = -1.0
            else:
                other = jnp.where(dist == 0, own[a], jnp.where(dist == 1, before[a], -1.0))
                sign = jnp.where(mine == other, 1.0, -1.0)
            u = sign * (scale * part + bias)
            small = jnp.exp(-jnp.abs(u))
            weight = -sign * (jnp.where(u >= 0, small, 1.0) / (1.0 + small)) * keep
            loss = loss + (jnp.maximum(-u, 0.0) + jnp.log1p(small)) * keep
            slope = slope + weight * part
            plain = plain + weight
            line.append(weight)
        weights.append(jnp.concatenate(line, 1))
    lane = lax.broadcasted_iota(jnp.int32, (1, size), 1)
    loss, slope, plain = jnp.sum(loss), jnp.sum(scale * slope), jnp.sum(plain)
    sums = jnp.where(lane == 0, loss, jnp.where(lane == 1, slope, jnp.where(lane == 2, plain, 0.0)))
    return jnp.concatenate(weights, 0), sums * (1.0 / tokens)


def tags(ids):
    return (ids[0:1, :], ids[8:9, :], None), (ids[1:2, :], ids[9:10, :], None)


def ready_kernel(image, text, i_high, i_low, t_high, t_low):
    i_high[...], i_low[...] = halves(image[...])
    t_high[...], t_low[...] = halves(text[...])


def first_kernel(
    tokens, place, params, ids, i_high, i_low, i2, far, t_high, t_low, t1, u0, high, low, images, gt0, gt1, gu0, sums
):
    own, before = tags(ids)
    p, q, r, core = place[0], place[1], place[2], place[3]
    size = t1.shape[0]
    rows = joined((i_high[...], i_low[...]), halves(i2[...]), halves(far[...]))
    high[...], low[...] = rows
    cols = joined((t_high[...], t_low[...]), halves(t1[...]), halves(u0[...]))
    dists = [[(i - p, True), (i - (p ^ 1), True), (i + 4 - q, True)] for i in (p, p ^ 2)]
    dists.append([(0, False), (0, False), ((r ^ 2) + 8 - q, core == 1)])
    sim = product(rows, cols, ((1,), (1,)))
    weights, sums[...] = weigh(sim, dists, own, before, params[0], params[1], tokens)
    images[...] = gradient(weights, cols, params[0])
    texts = gradient(jnp.transpose(weights), rows, params[0])
    gt0[...] = texts[0:size, :]
    gt1[...] = texts[size : 2 * size, :]
    gu0[...] = texts[2 * size :, :]


def last_kernel(tokens, place, params, ids, high, low, u1, images, sums_in, gi0, gi2, gfar, gu1, sums):
    own, before = tags(ids)
    p, q, r, core = place[0], place[1], place[2], place[3]
    size = u1.shape[0]
    rows, cols = (high[...], low[...]), halves(u1[...])
    dists = [[(i + 4 - (q ^ 1), True)] for i in (p, p ^ 2)]
    dists.append([((r ^ 2) + 8 - (q ^ 1), core == 1)])
    sim = product(rows, cols, ((1,), (1,)))
    weights, parts = weigh(sim, dists, own, before, params[0], params[1], tokens)
    sums[...] = sums_in[...] + parts
    grads = images[...] + gradient(weights, cols, params[0])
    gi0[...] = grads[0:size, :]
    gi2[...] = grads[size : 2 * size, :]
    gfar[...] = grads[2 * size :, :]
    gu1[...] = gradient(jnp.transpose(weights), rows, params[0])


def kernel_call(body, name, shapes, rows, cols, *args, scalars=2):
    cost = pl.CostEstimate(
        flops=18 * rows * cols * 1152, bytes_accessed=8 * 1152 * (rows + cols), transcendentals=2 * rows * cols
    )
    return pl.pallas_call(
        body,
        out_shape=[jax.ShapeDtypeStruct(shape, dtype) for shape, dtype in shapes],
        in_specs=[SMEM] * scalars + [VMEM] * (len(args) - scalars),
        out_specs=[VMEM] * len(shapes),
        compiler_params=pltpu.CompilerParams(vmem_limit_bytes=16 << 20),
        cost_estimate=cost,
        name=name,
    )(*args)


def local(image, text, video_ids, log_scale, bias):
    size, width = image.shape
    count = lax.axis_size(NAMES)
    tokens = size * count
    everyone = range(count)

    def send(x, to, senders=everyone):
        return lax.ppermute(x, NAMES, [(b, to(b)) for b in senders])

    def other_core(x):
        return send(x, lambda b: b ^ 2)

    def beside(x):
        return send(x, lambda b: b ^ 1)

    plane_z = lax.axis_index(("z_hi", "z_lo"))
    core = lax.axis_index("core")
    p = 2 * core + lax.axis_index("x_lo")
    q = jnp.where(plane_z > 0, p, p ^ 1)
    r = jnp.where(plane_z < DEEP - 1, p, p ^ 1)
    place = jnp.stack([p, q, r, core]).astype(jnp.int32)
    params = jnp.stack([log_scale, bias])

    t1 = beside(text)
    ids = video_ids.astype(F32)[None]
    before = send(ids, lambda b: (b + 1) % count)
    near_text, near_image, before = lax.optimization_barrier((text, image, before))
    u0 = send(near_text, up)
    mine = jnp.concatenate([ids, before, jnp.zeros((6, size), F32)], 0)
    ids = jnp.concatenate([mine, other_core(mine)], 0)
    i2 = other_core(near_image)
    far = send(near_image, lambda b: down(b) ^ 2, [b for b in everyone if b % 4 < 2])
    half = ((size, width), BF16)
    ready = kernel_call(ready_kernel, "ready", [half] * 4, 2, 2, image, text, scalars=0)
    u0, t1, i_high, i_low, t_high, t_low = lax.optimization_barrier((u0, t1, *ready))
    u1 = send(t1, up)

    block, three, row = ((size, width), F32), (3 * size, width), ((1, size), F32)
    high, low, images, gt0, gt1, gu0, sums = kernel_call(
        functools.partial(first_kernel, tokens),
        "first",
        [(three, BF16), (three, BF16), (three, F32), block, block, block, row],
        384,
        384,
        *(place, params, ids, i_high, i_low, i2, far, t_high, t_low, t1, u0),
    )
    gt1, gu0 = beside(gt1), send(gu0, down)
    gi0, gi2, gfar, gu1, sums = kernel_call(
        functools.partial(last_kernel, tokens),
        "last",
        [block, block, block, block, row],
        384,
        128,
        *(place, params, ids, high, low, u1, images, sums),
    )
    gu1 = send(gu1, lambda b: down(b) ^ 1)
    gi2 = other_core(gi2)
    gfar = send(gfar, lambda b: up(b) ^ 2, [b for b in everyone if b % 4 >= 2])
    sums, gt1, gu0 = lax.optimization_barrier((sums, gt1, gu0))

    def add_up(row, axes):
        shares = jnp.broadcast_to(row, (lax.axis_size(axes), size))
        return jnp.sum(lax.all_to_all(shares, axes, 0, 0, tiled=True), axis=0, keepdims=True)

    sums = add_up(sums, ("z_hi", "z_lo"))
    sums, gu1, gi2, gfar = lax.optimization_barrier((sums, gu1, gi2, gfar))
    sums = add_up(sums, ("y_hi", "y_lo", "x_hi", "core", "x_lo"))
    grad_image = gi0 + gi2 + gfar
    grad_text = gt0 + gt1 + gu0 + gu1
    return sums[0, 0], grad_image, grad_text, sums[0, 1], sums[0, 2]


def solution(mesh):
    fine = Mesh(mesh.devices.reshape(SHAPE), NAMES)
    rows = P(NAMES, None)
    return jax.shard_map(
        local,
        mesh=fine,
        in_specs=(rows, rows, P(NAMES), P(), P()),
        out_specs=(P(), rows, rows, P(), P()),
        check_vma=False,
    )
```

time: 155 us -> 119 us (0.77)
  the two profiles are of different devices: /device:TPU:64 before, /device:TPU:1 now
where the time goes in v2:
time: 119 us; the launch traced here: 118 us
  starting transfers between devices  72.4 us (61%)
  blocking collectives  13.8 us (12%)
  waiting for transfers between devices  9.24 us (8%)
  Pallas kernels  8.97 us (8%)
  local copies, waits for them, and re-layouts  7.49 us (6%)
  other arithmetic  3.67 us (3%)
  between operations  2.16 us (2%)
    ppermute x12, starting transfers between devices, send(): return lax.ppermute(x, NAMES, [(b, to(b)) for b in senders])  65.9 us
    all_to_all x1, blocking collectives, add_up(): lax.all_to_all(shares, axes, 0, 0, tiled=True)  13.8 us
    pallas_call x3, Pallas kernels, kernel_call(): pl.pallas_call(body, out_shape=[jax.ShapeDtypeStruct(shape, dtype) for sh...  8.97 us
    all_to_all x1, waiting for transfers between devices, add_up(): lax.all_to_all(shares, axes, 0, 0, tiled=True)  6.62 us
    all_to_all x1, starting transfers between devices, add_up(): lax.all_to_all(shares, axes, 0, 0, tiled=True)  6.51 us
    unnamed x14, local copies, waits for them, and re-layouts  6.26 us
    add x1, other arithmetic, local(): grad_text = gt0 + gt1 + gu0 + gu1  2.8 us
    ppermute x12, waiting for transfers between devices, send(): return lax.ppermute(x, NAMES, [(b, to(b)) for b in senders])  2.63 us
  transfers between devices with their start and end apart: 13, of which 3 were waited for; matrix products, arithmetic and copies ran while one was open for 3% of the time, Pallas kernels for 8%

profile of v2, /device:TPU:1, one launch (start us, length us, event | category | flops | bytes accessed | tf_op | source)
XLA Modules:
  0.0 117.8 jit_solution(16283623598633028916)
XLA Ops:
  1.3 3.9 %collective-permute-start = (f32[1,128]{1,0:T(1,128)S(1)}, f32[1,128]{1,0:T(1,128)S(1)}, u32[]{:S(2)}, u32[]{:S(2)}) collective-permute-start(f32[1,128]{1,0:T(1,128)S(1)} %convert_bitcast_fusion), channel_id=1, source_target_pairs={{0,1},{1,2},{2,3},{3,4},{4,5},{5,6},{6,7},{7,8},{8,9},{9,10},{10,1... | collective-permute-start | bytes 1544 | tf_op jit(solution)/shard_map/ppermute | solution.py:156
  5.2 4.5 %collective-permute-start.3 = (f32[128,1152]{1,0:T(8,128)}, f32[128,1152]{1,0:T(8,128)S(1)}, u32[]{:S(2)}, u32[]{:S(2)}) collective-permute-start(f32[128,1152]{1,0:T(8,128)} %text.1), channel_id=1, source_target_pairs={{0,1},{1,0},{2,3},{3,2},{4,5},{5,4},{6,7},{7,6},{8,9},{9,8},{10,11... | collective-permute-start | bytes 1769480 | tf_op jit(solution)/shard_map/ppermute | solution.py:156
  9.8 4.0 %collective-permute-start.2 = (f32[128,1152]{1,0:T(8,128)}, f32[128,1152]{1,0:T(8,128)S(1)}, u32[]{:S(2)}, u32[]{:S(2)}) collective-permute-start(f32[128,1152]{1,0:T(8,128)} %text.1), channel_id=1, source_target_pairs={{0,4},{1,5},{2,6},{3,7},{4,8},{5,9},{6,10},{7,11},{8,12},{9,13},{1... | collective-permute-start | bytes 1769480 | tf_op jit(solution)/shard_map/ppermute | solution.py:156
  13.8 16.8 %collective-permute-start.4 = (f32[128,1152]{1,0:T(8,128)}, f32[128,1152]{1,0:T(8,128)S(1)}, u32[]{:S(2)}, u32[]{:S(2)}) collective-permute-start(f32[128,1152]{1,0:T(8,128)} %image.1), channel_id=1, source_target_pairs={{0,2},{1,3},{2,0},{3,1},{4,6},{5,7},{6,4},{7,5},{8,10},{9,11},{10,... | collective-permute-start | bytes 1769480 | tf_op jit(solution)/shard_map/ppermute | solution.py:156
  30.6 1.3 %collective-permute-start.5 = (f32[128,1152]{1,0:T(8,128)}, f32[128,1152]{1,0:T(8,128)S(1)}, u32[]{:S(2)}, u32[]{:S(2)}) collective-permute-start(f32[128,1152]{1,0:T(8,128)} %image.1), channel_id=1, source_target_pairs={{0,1023},{1,1022},{4,2},{5,3},{8,6},{9,7},{12,10},{13,11},{16,14},... | collective-permute-start | bytes 1769480 | tf_op jit(solution)/shard_map/ppermute | solution.py:156
  31.9 1.1 copy-done
  33.0 1.1 copy-done.1
  37.1 1.9 %collective-permute-done.2.u0 = f32[128,1152]{1,0:T(8,128)S(1)} collective-permute-done((f32[128,1152]{1,0:T(8,128)}, f32[128,1152]{1,0:T(8,128)S(1)}, u32[]{:S(2)}, u32[]{:S(2)}) %collective-permute-start.2) | collective-permute-done | bytes 589856 | tf_op jit(solution)/shard_map/ppermute | solution.py:156
  38.9 1.9 %collective-permute-start.6 = (f32[128,1152]{1,0:T(8,128)S(1)}, f32[128,1152]{1,0:T(8,128)S(1)}, u32[]{:S(2)}, u32[]{:S(2)}) collective-permute-start(f32[128,1152]{1,0:T(8,128)S(1)} %collective-permute-done.3.t1), channel_id=1, source_target_pairs={{0,4},{1,5},{2,6},{3,7},{4,8},{5,9},{6,10},{7,11},{8,12},{9,13},{1... | collective-permute-start | bytes 1769480 | tf_op jit(solution)/shard_map/ppermute | solution.py:156
  40.9 8.2 %collective-permute-start.1 = (f32[8,128]{1,0:T(8,128)S(1)}, f32[8,128]{1,0:T(8,128)S(1)}, u32[]{:S(2)}, u32[]{:S(2)}) collective-permute-start(f32[8,128]{1,0:T(8,128)S(1)} %pad_maximum_fusion.1), channel_id=1, source_target_pairs={{0,2},{1,3},{2,0},{3,1},{4,6},{5,7},{6,4},{7,5},{8,10},{9,11},{10,... | collective-permute-start | bytes 12296 | tf_op jit(solution)/shard_map/ppermute | solution.py:156
  50.0 1.0 copy-done.3
  50.9 1.0 copy-done.5
  51.9 5.8 %first.1 = (bf16[384,1152]{1,0:T(8,128)(2,1)S(1)}, bf16[384,1152]{1,0:T(8,128)(2,1)S(1)}, f32[384,1152]{1,0:T(8,128)S(1)}, f32[128,1152]{1,0:T(8,128)S(1)}, f32[...) custom-call(s32[4]{0:T(128)S(1)} %pad_add_fusion.place, f32[2]{0:T(128)S(1)} %pad_maximum_fusion.2.params, ...), custom_call_target="tpu_custom_call" | custom-call | flops 3057647616 | bytes 7077888 | tf_op jit(solution)/shard_map/first/pallas_call | solution.py:138
  57.7 1.9 %collective-permute-start.7 = (f32[128,1152]{1,0:T(8,128)S(1)}, f32[128,1152]{1,0:T(8,128)S(1)}, u32[]{:S(2)}, u32[]{:S(2)}) collective-permute-start(f32[128,1152]{1,0:T(8,128)S(1)} %get-tuple-element.55), channel_id=1, source_target_pairs={{0,1},{1,0},{2,3},{3,2},{4,5},{5,4},{6,7},{7,6},{8,9},{9,8},{10,11... | collective-permute-start | bytes 1769480 | tf_op jit(solution)/shard_map/ppermute | solution.py:156
  59.6 9.1 %collective-permute-start.8 = (f32[128,1152]{1,0:T(8,128)S(1)}, f32[128,1152]{1,0:T(8,128)S(1)}, u32[]{:S(2)}, u32[]{:S(2)}) collective-permute-start(f32[128,1152]{1,0:T(8,128)S(1)} %get-tuple-element.56), channel_id=1, source_target_pairs={{0,1021},{1,1020},{2,1023},{3,1022},{4,0},{5,1},{6,2},{7,3},{8,4},... | collective-permute-start | bytes 1769480 | tf_op jit(solution)/shard_map/ppermute | solution.py:156
  68.7 3.0 %last.1 = (f32[128,1152]{1,0:T(8,128)S(1)}, f32[128,1152]{1,0:T(8,128)S(1)}, f32[128,1152]{1,0:T(8,128)S(1)}, f32[128,1152]{1,0:T(8,128)S(1)}, f32[1,128]{1,0:T(1,128)S(1)}) custom-call(s32[4]{0:T(128)S(1)} %pad_add_fusion.place, f32[2]{0:T(128)S(1)} %pad_maximum_fusion.2.params, f32[16,128]{1,0:T(8,128)S(1)} %pad_maximum_fusion.ids, ...), custom_call_target="tpu_custom_call" | custom-call | flops 1019215872 | bytes 4718592 | tf_op jit(solution)/shard_map/last/pallas_call | solution.py:138
  71.7 2.5 %collective-permute-start.10 = (f32[128,1152]{1,0:T(8,128)S(1)}, f32[128,1152]{1,0:T(8,128)}, u32[]{:S(2)}, u32[]{:S(2)}) collective-permute-start(f32[128,1152]{1,0:T(8,128)S(1)} %get-tuple-element.59), channel_id=1, source_target_pairs={{0,2},{1,3},{2,0},{3,1},{4,6},{5,7},{6,4},{7,5},{8,10},{9,11},{10,... | collective-permute-start | bytes 1769480 | tf_op jit(solution)/shard_map/ppermute | solution.py:156
  74.2 2.1 %collective-permute-start.11 = (f32[128,1152]{1,0:T(8,128)S(1)}, f32[128,1152]{1,0:T(8,128)}, u32[]{:S(2)}, u32[]{:S(2)}) collective-permute-start(f32[128,1152]{1,0:T(8,128)S(1)} %get-tuple-element.60), channel_id=1, source_target_pairs={{2,4},{3,5},{6,8},{7,9},{10,12},{11,13},{14,16},{15,17},{18,20},{1... | collective-permute-start | bytes 1769480 | tf_op jit(solution)/shard_map/ppermute | solution.py:156
  76.4 9.5 %collective-permute-start.9 = (f32[128,1152]{1,0:T(8,128)S(1)}, f32[128,1152]{1,0:T(8,128)}, u32[]{:S(2)}, u32[]{:S(2)}) collective-permute-start(f32[128,1152]{1,0:T(8,128)S(1)} %get-tuple-element.58), channel_id=1, source_target_pairs={{0,1020},{1,1021},{2,1022},{3,1023},{4,1},{5,0},{6,3},{7,2},{8,5},... | collective-permute-start | bytes 1769480 | tf_op jit(solution)/shard_map/ppermute | solution.py:156
  86.0 0.8 copy-done.6
  86.8 13.8 %all_to_all.12 = f32[16,1,128]{2,1,0:T(1,128)S(1)} all-to-all(f32[16,1,128]{2,1,0:T(1,128)S(1)} %broadcast_in_dim.24), channel_id=1, replica_groups=mesh['y_hi'=2,'y_lo'=4,'x_hi'=2,'z_hi'=4,'z_lo'=4,'core'=2,'x_lo'=2] {'z..., dimensions={0} | all-to-all | bytes 16384 | tf_op jit(solution)/shard_map/all_to_all | solution.py:211
  101.2 6.5 %all-to-all-start.1 = ((f32[64,1,128]{2,1,0:T(1,128)}), f32[64,1,128]{2,1,0:T(1,128)S(1)}, u32[]{:S(2)}, u32[]{:S(2)}) async-start(f32[64,1,128]{2,1,0:T(1,128)} %broadcast_in_dim.26), calls=%async_computation.1 | async-start | bytes 65536 | tf_op jit(solution)/shard_map/all_to_all | solution.py:211
  107.8 2.8 %add_add_fusion = (f32[128,1152]{1,0:T(8,128)}, f32[128,1152]{1,0:T(8,128)}) fusion(f32[128,1152]{1,0:T(8,128)} %collective-permute-done.9, f32[128,1152]{1,0:T(8,128)} %copy-done.6, f32[128,1152]{1,0:T(8,128)S(1)} %get-tuple-element.65, f32[128,1152]{1,0:T(8,128)S(1)} %collective-permute-done.7, f32[128,1152]{1,0:T(8,128)} %collective-permute-done.11, ...), kind=kLoop, calls=%fused_computation | loop fusion | flops 737280 | bytes 5308416 | tf_op jit(solution)/shard_map/add | solution.py:217
  110.6 6.6 %all-to-all-done.1 = f32[64,1,128]{2,1,0:T(1,128)S(1)} async-done(((f32[64,1,128]{2,1,0:T(1,128)}), f32[64,1,128]{2,1,0:T(1,128)S(1)}, u32[]{:S(2)}, u32[]{:S(2)}) %all-to-all-start.1) | async-done | bytes 32800 | tf_op jit(solution)/shard_map/all_to_all | solution.py:211
  (32 shorter events, 4.5 us)
Async XLA Ops:
  1.3 8.5 %collective-permute-start = (f32[1,128]{1,0:T(1,128)S(1)}, f32[1,128]{1,0:T(1,128)S(1)}, u32[]{:S(2)}, u32[]{:S(2)}) collective-permute-start(f32[1,128]{1,0:T(1,128)S(1)} %convert_bitcast_fusion), channel_id=1, source_target_pairs={{0,1},{1,2},{2,3},{3,4},{4,5},{5,6},{6,7},{7,8},{8,9},{9,10},{10,1... | collective-permute-start | bytes 1544 | tf_op jit(solution)/shard_map/ppermute | solution.py:156
  5.2 31.8 %collective-permute-start.3 = (f32[128,1152]{1,0:T(8,128)}, f32[128,1152]{1,0:T(8,128)S(1)}, u32[]{:S(2)}, u32[]{:S(2)}) collective-permute-start(f32[128,1152]{1,0:T(8,128)} %text.1), channel_id=1, source_target_pairs={{0,1},{1,0},{2,3},{3,2},{4,5},{5,4},{6,7},{7,6},{8,9},{9,8},{10,11... | collective-permute-start | bytes 1769480 | tf_op jit(solution)/shard_map/ppermute | solution.py:156
  9.8 29.2 %collective-permute-start.2 = (f32[128,1152]{1,0:T(8,128)}, f32[128,1152]{1,0:T(8,128)S(1)}, u32[]{:S(2)}, u32[]{:S(2)}) collective-permute-start(f32[128,1152]{1,0:T(8,128)} %text.1), channel_id=1, source_target_pairs={{0,4},{1,5},{2,6},{3,7},{4,8},{5,9},{6,10},{7,11},{8,12},{9,13},{1... | collective-permute-start | bytes 1769480 | tf_op jit(solution)/shard_map/ppermute | solution.py:156
  13.8 36.2 %collective-permute-start.4 = (f32[128,1152]{1,0:T(8,128)}, f32[128,1152]{1,0:T(8,128)S(1)}, u32[]{:S(2)}, u32[]{:S(2)}) collective-permute-start(f32[128,1152]{1,0:T(8,128)} %image.1), channel_id=1, source_target_pairs={{0,2},{1,3},{2,0},{3,1},{4,6},{5,7},{6,4},{7,5},{8,10},{9,11},{10,... | collective-permute-start | bytes 1769480 | tf_op jit(solution)/shard_map/ppermute | solution.py:156
  30.6 19.4 %collective-permute-start.5 = (f32[128,1152]{1,0:T(8,128)}, f32[128,1152]{1,0:T(8,128)S(1)}, u32[]{:S(2)}, u32[]{:S(2)}) collective-permute-start(f32[128,1152]{1,0:T(8,128)} %image.1), channel_id=1, source_target_pairs={{0,1023},{1,1022},{4,2},{5,3},{8,6},{9,7},{12,10},{13,11},{16,14},... | collective-permute-start | bytes 1769480 | tf_op jit(solution)/shard_map/ppermute | solution.py:156
  31.9 1.1 copy-start
  33.0 1.1 copy-start.1
  34.3 0.7 copy-start.2
  35.0 0.7 copy-start.4
  38.9 29.7 %collective-permute-start.6 = (f32[128,1152]{1,0:T(8,128)S(1)}, f32[128,1152]{1,0:T(8,128)S(1)}, u32[]{:S(2)}, u32[]{:S(2)}) collective-permute-start(f32[128,1152]{1,0:T(8,128)S(1)} %collective-permute-done.3.t1), channel_id=1, source_target_pairs={{0,4},{1,5},{2,6},{3,7},{4,8},{5,9},{6,10},{7,11},{8,12},{9,13},{1... | collective-permute-start | bytes 1769480 | tf_op jit(solution)/shard_map/ppermute | solution.py:156
  40.9 9.0 %collective-permute-start.1 = (f32[8,128]{1,0:T(8,128)S(1)}, f32[8,128]{1,0:T(8,128)S(1)}, u32[]{:S(2)}, u32[]{:S(2)}) collective-permute-start(f32[8,128]{1,0:T(8,128)S(1)} %pad_maximum_fusion.1), channel_id=1, source_target_pairs={{0,2},{1,3},{2,0},{3,1},{4,6},{5,7},{6,4},{7,5},{8,10},{9,11},{10,... | collective-permute-start | bytes 12296 | tf_op jit(solution)/shard_map/ppermute | solution.py:156
  50.0 1.0 copy-start.3
  50.9 1.0 copy-start.5
  57.7 28.3 %collective-permute-start.7 = (f32[128,1152]{1,0:T(8,128)S(1)}, f32[128,1152]{1,0:T(8,128)S(1)}, u32[]{:S(2)}, u32[]{:S(2)}) collective-permute-start(f32[128,1152]{1,0:T(8,128)S(1)} %get-tuple-element.55), channel_id=1, source_target_pairs={{0,1},{1,0},{2,3},{3,2},{4,5},{5,4},{6,7},{7,6},{8,9},{9,8},{10,11... | collective-permute-start | bytes 1769480 | tf_op jit(solution)/shard_map/ppermute | solution.py:156
  59.6 26.3 %collective-permute-start.8 = (f32[128,1152]{1,0:T(8,128)S(1)}, f32[128,1152]{1,0:T(8,128)S(1)}, u32[]{:S(2)}, u32[]{:S(2)}) collective-permute-start(f32[128,1152]{1,0:T(8,128)S(1)} %get-tuple-element.56), channel_id=1, source_target_pairs={{0,1021},{1,1020},{2,1023},{3,1022},{4,0},{5,1},{6,2},{7,3},{8,4},... | collective-permute-start | bytes 1769480 | tf_op jit(solution)/shard_map/ppermute | solution.py:156
  71.7 28.9 %collective-permute-start.10 = (f32[128,1152]{1,0:T(8,128)S(1)}, f32[128,1152]{1,0:T(8,128)}, u32[]{:S(2)}, u32[]{:S(2)}) collective-permute-start(f32[128,1152]{1,0:T(8,128)S(1)} %get-tuple-element.59), channel_id=1, source_target_pairs={{0,2},{1,3},{2,0},{3,1},{4,6},{5,7},{6,4},{7,5},{8,10},{9,11},{10,... | collective-permute-start | bytes 1769480 | tf_op jit(solution)/shard_map/ppermute | solution.py:156
  74.2 26.4 %collective-permute-start.11 = (f32[128,1152]{1,0:T(8,128)S(1)}, f32[128,1152]{1,0:T(8,128)}, u32[]{:S(2)}, u32[]{:S(2)}) collective-permute-start(f32[128,1152]{1,0:T(8,128)S(1)} %get-tuple-element.60), channel_id=1, source_target_pairs={{2,4},{3,5},{6,8},{7,9},{10,12},{11,13},{14,16},{15,17},{18,20},{1... | collective-permute-start | bytes 1769480 | tf_op jit(solution)/shard_map/ppermute | solution.py:156
  76.4 24.2 %collective-permute-start.9 = (f32[128,1152]{1,0:T(8,128)S(1)}, f32[128,1152]{1,0:T(8,128)}, u32[]{:S(2)}, u32[]{:S(2)}) collective-permute-start(f32[128,1152]{1,0:T(8,128)S(1)} %get-tuple-element.58), channel_id=1, source_target_pairs={{0,1020},{1,1021},{2,1022},{3,1023},{4,1},{5,0},{6,3},{7,2},{8,5},... | collective-permute-start | bytes 1769480 | tf_op jit(solution)/shard_map/ppermute | solution.py:156
  85.9 0.8 copy-start.6
  101.2 15.9 %all-to-all-start.1 = ((f32[64,1,128]{2,1,0:T(1,128)}), f32[64,1,128]{2,1,0:T(1,128)S(1)}, u32[]{:S(2)}, u32[]{:S(2)}) async-start(f32[64,1,128]{2,1,0:T(1,128)} %broadcast_in_dim.26), calls=%async_computation.1 | async-start | bytes 65536 | tf_op jit(solution)/shard_map/all_to_all | solution.py:211

commit v3 on v2

v3 whole, which is shorter than its diff:
```python
import functools

import jax
import jax.numpy as jnp
from jax import lax
from jax.experimental import pallas as pl
from jax.experimental.pallas import tpu as pltpu
from jax.sharding import Mesh
from jax.sharding import PartitionSpec as P

STEPS = 7
LINES, DEEP = 16, 16
SHAPE = (2, 4, 2, 4, 4, 2, 2)
NAMES = ("y_hi", "y_lo", "x_hi", "z_hi", "z_lo", "core", "x_lo")
F32, BF16 = jnp.float32, jnp.bfloat16
VMEM = pl.BlockSpec(memory_space=pltpu.VMEM)
SMEM = pl.BlockSpec(memory_space=pltpu.SMEM)


def up(b):
    plane, pos = divmod(b, 4)
    if plane % DEEP < DEEP - 1:
        return b + 4
    return (plane + 1) % (LINES * DEEP) * 4 + (pos ^ 1)


def down(b):
    plane, pos = divmod(b, 4)
    if plane % DEEP > 0:
        return b - 4
    return (plane - 1) % (LINES * DEEP) * 4 + (pos ^ 1)


def halves(x):
    high = x.astype(BF16)
    return high, (x - high.astype(F32)).astype(BF16)


def joined(*pairs):
    return tuple(jnp.concatenate(parts, 0) for parts in zip(*pairs))


def product(a, b, dims):
    dot = functools.partial(lax.dot_general, dimension_numbers=(dims, ((), ())), preferred_element_type=F32)
    return dot(a[0], b[0]) + (dot(a[0], b[1]) + dot(a[1], b[0]))


def long_product(a, b, dims):
    left = jnp.concatenate([a[0], a[0], a[1]], dims[0][0])
    right = jnp.concatenate([b[0], b[1], b[0]], dims[1][0])
    return lax.dot_general(left, right, (dims, ((), ())), preferred_element_type=F32)


def gradient(weights, cols, log_scale, product):
    grads = product(halves(weights), cols, ((1,), (0,)))
    return jnp.exp(jnp.full((1, grads.shape[1]), log_scale, F32)) * grads


def tag(packet):
    return packet[128:129, 0:128]


def column(row):
    return jnp.transpose(jnp.broadcast_to(row, (row.shape[1], row.shape[1])))


def weigh(sim, dists, row_ids, col_ids, log_scale, bias, tokens):
    size = 128
    scale = jnp.exp(jnp.full((1, size), log_scale, F32))
    norm = 1.0 / (STEPS * size)
    loss = slope = plain = jnp.zeros((size, size), F32)
    weights = []
    for a, row in enumerate(dists):
        line = []
        mine = column(row_ids[a]) if a < len(row_ids) else None
        for b, (dist, counts) in enumerate(row):
            part = sim[a * size : (a + 1) * size, b * size : (b + 1) * size]
            keep = jnp.where((dist >= 0) & (dist < STEPS) & counts, norm, 0.0).astype(F32)
            if mine is None:
                sign = -1.0
            else:
                other = jnp.where((dist == 0) | (dist == 1), col_ids[b], -1.0)
                sign = jnp.where(mine == other, 1.0, -1.0)
            u = sign * (scale * part + bias)
            small = jnp.exp(-jnp.abs(u))
            weight = -sign * (jnp.where(u >= 0, small, 1.0) / (1.0 + small)) * keep
            loss = loss + (jnp.maximum(-u, 0.0) + jnp.log1p(small)) * keep
            slope = slope + weight * part
            plain = plain + weight
            line.append(weight)
        weights.append(jnp.concatenate(line, 1))
    lane = lax.broadcasted_iota(jnp.int32, (1, size), 1)
    loss, slope, plain = jnp.sum(loss), jnp.sum(scale * slope), jnp.sum(plain)
    sums = jnp.where(lane == 0, loss, jnp.where(lane == 1, slope, jnp.where(lane == 2, plain, 0.0)))
    return jnp.concatenate(weights, 0), sums * (1.0 / tokens)


def first_kernel(
    tokens, place, params, own, i2, far, t1, u0, image, text,
    high, low, images, gt0, gt1, gu0, mate, sums, i0, t0, arrived,
):
    copies = [
        pltpu.make_async_copy(source, target, arrived.at[n])
        for n, (source, target) in enumerate(((image, i0), (text, t0)))
    ]
    for copy in copies:
        copy.start()
    p, q, r, core = place[0], place[1], place[2], place[3]
    size = image.shape[0]
    both = 2 * size
    lone_rows, lone_cols = halves(far[...]), halves(u0[0:size, :])
    sim = product(lone_rows, lone_cols, ((1,), (1,)))
    lone, parts = weigh(sim, [[((r ^ 2) + 8 - q, core == 1)]], (), (), params[0], params[1], tokens)
    images[both:, :] = gradient(lone, lone_cols, params[0], product)
    gu0[...] = gradient(jnp.transpose(lone), lone_rows, params[0], product)
    high[both:, :], low[both:, :] = lone_rows
    mate_rows, near_cols = halves(i2[0:size, :]), halves(t1[0:size, :])
    for copy in copies:
        copy.wait()
    rows = joined(halves(i0[...]), mate_rows)
    high[0:both, :], low[0:both, :] = rows
    cols = joined(halves(t0[...]), near_cols, lone_cols)
    dists = [[(i - p, True), (i - (p ^ 1), True), (i + 4 - q, True)] for i in (p, p ^ 2)]
    sim = long_product(rows, cols, ((1,), (1,)))
    mate[...] = tag(i2)
    row_ids, col_ids = (own[...], mate[...]), (own[...], tag(t1), tag(u0))
    weights, more = weigh(sim, dists, row_ids, col_ids, params[0], params[1], tokens)
    sums[...] = parts + more
    images[0:both, :] = gradient(weights, cols, params[0], long_product)
    texts = gradient(jnp.transpose(weights), rows, params[0], long_product)
    gt0[...] = texts[0:size, :]
    gt1[...] = texts[size:both, :]
    gu0[...] += texts[both:, :]


def last_kernel(tokens, place, params, own, mate, high, low, u1, images, sums_in, gi0, gi2, gfar, gu1, sums):
    p, q, r, core = place[0], place[1], place[2], place[3]
    size = own.shape[1]
    rows, cols = (high[...], low[...]), halves(u1[0:size, :])
    dists = [[(i + 4 - (q ^ 1), True)] for i in (p, p ^ 2)]
    dists.append([((r ^ 2) + 8 - (q ^ 1), core == 1)])
    sim = product(rows, cols, ((1,), (1,)))
    weights, parts = weigh(sim, dists, (own[...], mate[...]), (tag(u1),), params[0], params[1], tokens)
    sums[...] = sums_in[...] + parts
    grads = images[...] + gradient(weights, cols, params[0], product)
    gi0[...] = grads[0:size, :]
    gi2[...] = grads[size : 2 * size, :]
    gfar[...] = grads[2 * size :, :]
    gu1[...] = gradient(jnp.transpose(weights), rows, params[0], product)


def kernel_call(body, name, shapes, rows, cols, *args, plain=0):
    cost = pl.CostEstimate(
        flops=18 * rows * cols * 1152, bytes_accessed=8 * 1152 * (rows + cols), transcendentals=2 * rows * cols
    )
    near = len(args) - plain
    far = [pltpu.with_memory_space_constraint(arg, pltpu.HBM) for arg in args[near:]]
    block = pltpu.VMEM((128, 1152), F32)
    return pl.pallas_call(
        body,
        out_shape=[jax.ShapeDtypeStruct(shape, dtype) for shape, dtype in shapes],
        in_specs=[SMEM, SMEM] + [VMEM] * (near - 2) + [pl.BlockSpec(memory_space=pltpu.HBM)] * plain,
        out_specs=[VMEM] * len(shapes),
        scratch_shapes=[block] * plain + [pltpu.SemaphoreType.DMA((plain,))] * (plain > 0),
        compiler_params=pltpu.CompilerParams(vmem_limit_bytes=16 << 20),
        cost_estimate=cost,
        name=name,
    )(*args[:near], *far)


def local(image, text, video_ids, log_scale, bias):
    size, width = image.shape
    count = lax.axis_size(NAMES)
    tokens = size * count
    everyone = range(count)

    def send(x, to, senders=everyone):
        return lax.ppermute(x, NAMES, [(b, to(b)) for b in senders])

    def other_core(x):
        return send(x, lambda b: b ^ 2)

    def beside(x):
        return send(x, lambda b: b ^ 1)

    plane_z = lax.axis_index(("z_hi", "z_lo"))
    core = lax.axis_index("core")
    p = 2 * core + lax.axis_index("x_lo")
    q = jnp.where(plane_z > 0, p, p ^ 1)
    r = jnp.where(plane_z < DEEP - 1, p, p ^ 1)
    place = jnp.stack([p, q, r, core]).astype(jnp.int32)
    params = jnp.stack([log_scale, bias])

    own = video_ids.astype(F32)[None]
    label = jnp.pad(own, ((0, 7), (0, width - size)))
    packet = jnp.concatenate([text, label], 0)
    t1 = beside(packet)
    u0 = send(packet, up)
    far = send(image, lambda b: down(b) ^ 2, [b for b in everyone if b % 4 < 2])
    label = lax.optimization_barrier(label)
    i2 = other_core(jnp.concatenate([image, label], 0))
    t1, place, params = lax.optimization_barrier((t1, place, params))
    u1 = send(t1, up)

    block, three, row = ((size, width), F32), (3 * size, width), ((1, size), F32)
    high, low, images, gt0, gt1, gu0, mate, sums = kernel_call(
        functools.partial(first_kernel, tokens),
        "first",
        [(three, BF16), (three, BF16), (three, F32), block, block, block, row, row],
        384,
        384,
        *(place, params, own, i2, far, t1, u0, image, text),
        plain=2,
    )
    gt1, gu0 = beside(gt1), send(gu0, down)
    gi0, gi2, gfar, gu1, sums = kernel_call(
        functools.partial(last_kernel, tokens),
        "last",
        [block, block, block, block, row],
        384,
        128,
        *(place, params, own, mate, high, low, u1, images, sums),
    )
    gu1 = send(gu1, lambda b: down(b) ^ 1)
    gi2 = other_core(gi2)
    gfar = send(gfar, lambda b: up(b) ^ 2, [b for b in everyone if b % 4 >= 2])

    def add_up(row, axes):
        shares = jnp.broadcast_to(row, (lax.axis_size(axes), size))
        return jnp.sum(lax.all_to_all(shares, axes, 0, 0, tiled=True), axis=0, keepdims=True)

    sums = add_up(sums, ("y_hi", "y_lo"))
    sums = add_up(sums, ("x_hi", "core", "x_lo"))
    sums, gt1, gu0, gu1, gi2, gfar = lax.optimization_barrier((sums, gt1, gu0, gu1, gi2, gfar))
    sums = add_up(sums, ("z_hi", "z_lo"))
    grad_image = gi0 + gi2 + gfar
    grad_text = gt0 + gt1 + gu0 + gu1
    return sums[0, 0], grad_image, grad_text, sums[0, 1], sums[0, 2]


def solution(mesh):
    fine = Mesh(mesh.devices.reshape(SHAPE), NAMES)
    rows = P(NAMES, None)
    return jax.shard_map(
        local,
        mesh=fine,
        in_specs=(rows, rows, P(NAMES), P(), P()),
        out_specs=(P(), rows, rows, P(), P()),
        check_vma=False,
    )
```

time: 119 us -> 109 us (0.916)
  starting transfers between devices: 72.4 us -> 48.2 us
  waiting for transfers between devices: 9.24 us -> 22 us
  local copies, waits for them, and re-layouts: 7.49 us -> 1.21 us
  other arithmetic: 3.67 us -> 7.6 us
  blocking collectives: 13.8 us -> 17.2 us
    ppermute x12 -> x10, starting transfers between devices: 65.9 us -> 43.6 us  [send(): return lax.ppermute(x, NAMES, [(b, to(b)) for b in senders])]
    ppermute x12 -> x10, waiting for transfers between devices: 2.63 us -> 13.5 us  [send(): return lax.ppermute(x, NAMES, [(b, to(b)) for b in senders])]
    unnamed x14 -> x2, local copies, waits for them, and re-layouts: 6.26 us -> 0.01 us
    concatenate x2, other arithmetic: 0.02 us -> 3.86 us  [the longest x1 1.93 us: local(): i2 = other_core(jnp.concatenate([image, label], 0))]
    all_to_all x1 -> x2, blocking collectives: 13.8 us -> 17.2 us  [add_up(): lax.all_to_all(shares, axes, 0, 0, tiled=True)]
    all_to_all x1, starting transfers between devices: 6.51 us -> 4.58 us  [add_up(): lax.all_to_all(shares, axes, 0, 0, tiled=True)]
    all_to_all x1, waiting for transfers between devices: 6.62 us -> 8.43 us  [add_up(): lax.all_to_all(shares, axes, 0, 0, tiled=True)]
    pallas_call x3 -> x2, Pallas kernels: 8.97 us -> 9.91 us  [kernel_call(): pl.pallas_call(body, out_shape=[jax.ShapeDtypeStruct(shape, dtype) for sh...]
  transfers between devices with their start and end apart: 13 -> 11, of which waited for: 3 -> 3; matrix products, arithmetic and copies ran while one was open for 3% -> 5% of each run, Pallas kernels for 8% -> 9%
where the time goes in v3:
time: 109 us; the launch traced here: 108 us
  starting transfers between devices  48.2 us (44%)
  waiting for transfers between devices  22 us (20%)
  blocking collectives  17.2 us (16%)
  Pallas kernels  9.91 us (9%)
  other arithmetic  7.6 us (7%)
  between operations  2.1 us (2%)
  local copies, waits for them, and re-layouts  1.21 us (1%)
    ppermute x10, starting transfers between devices, send(): return lax.ppermute(x, NAMES, [(b, to(b)) for b in senders])  43.6 us
    all_to_all x2, blocking collectives, add_up(): lax.all_to_all(shares, axes, 0, 0, tiled=True)  17.2 us
    ppermute x10, waiting for transfers between devices, send(): return lax.ppermute(x, NAMES, [(b, to(b)) for b in senders])  13.5 us
    pallas_call x2, Pallas kernels, kernel_call(): pl.pallas_call(body, out_shape=[jax.ShapeDtypeStruct(shape, dtype) for sh...  9.91 us
    all_to_all x1, waiting for transfers between devices, add_up(): lax.all_to_all(shares, axes, 0, 0, tiled=True)  8.43 us
    all_to_all x1, starting transfers between devices, add_up(): lax.all_to_all(shares, axes, 0, 0, tiled=True)  4.58 us
    add x1, other arithmetic, local(): grad_text = gt0 + gt1 + gu0 + gu1  2.82 us
  transfers between devices with their start and end apart: 11, of which 3 were waited for; matrix products, arithmetic and copies ran while one was open for 5% of the time, Pallas kernels for 9%

profile of v3, /device:TPU:1, one launch (start us, length us, event | category | flops | bytes accessed | tf_op | source)
XLA Modules:
  0.0 108.2 jit_solution(5690957053396093640)
XLA Ops:
  0.6 0.7 convert_bitcast_fusion.own
  1.4 1.9 %pad_maximum_fusion = f32[136,1152]{1,0:T(8,128)} fusion(f32[8,1152]{1,0:T(8,128)S(1)} %pad.4, f32[128,1152]{1,0:T(8,128)} %text.1), kind=kLoop, calls=%fused_computation | loop fusion | flops 156672 | bytes 1253376 | tf_op jit(solution)/shard_map/concatenate | solution.py:196
  3.3 3.9 %collective-permute-start = (f32[136,1152]{1,0:T(8,128)}, f32[136,1152]{1,0:T(8,128)S(1)}, u32[]{:S(2)}, u32[]{:S(2)}) collective-permute-start(f32[136,1152]{1,0:T(8,128)} %pad_maximum_fusion), channel_id=1, source_target_pairs={{0,1},{1,0},{2,3},{3,2},{4,5},{5,4},{6,7},{7,6},{8,9},{9,8},{10,11... | collective-permute-start | bytes 1880072 | tf_op jit(solution)/shard_map/ppermute | solution.py:178
  7.2 4.0 %collective-permute-start.3 = (f32[136,1152]{1,0:T(8,128)}, f32[136,1152]{1,0:T(8,128)S(1)}, u32[]{:S(2)}, u32[]{:S(2)}) collective-permute-start(f32[136,1152]{1,0:T(8,128)} %pad_maximum_fusion), channel_id=1, source_target_pairs={{0,4},{1,5},{2,6},{3,7},{4,8},{5,9},{6,10},{7,11},{8,12},{9,13},{1... | collective-permute-start | bytes 1880072 | tf_op jit(solution)/shard_map/ppermute | solution.py:178
  11.2 1.9 %pad_maximum_fusion.1 = f32[136,1152]{1,0:T(8,128)} fusion(f32[8,1152]{1,0:T(8,128)S(1)} %pad.4, f32[128,1152]{1,0:T(8,128)} %image.1), kind=kLoop, calls=%fused_computation.1 | loop fusion | flops 156672 | bytes 1253376 | tf_op jit(solution)/shard_map/concatenate | solution.py:201
  13.2 11.9 %collective-permute-start.1 = (f32[136,1152]{1,0:T(8,128)}, f32[136,1152]{1,0:T(8,128)S(1)}, u32[]{:S(2)}, u32[]{:S(2)}) collective-permute-start(f32[136,1152]{1,0:T(8,128)} %pad_maximum_fusion.1), channel_id=1, source_target_pairs={{0,2},{1,3},{2,0},{3,1},{4,6},{5,7},{6,4},{7,5},{8,10},{9,11},{10,... | collective-permute-start | bytes 1880072 | tf_op jit(solution)/shard_map/ppermute | solution.py:178
  25.1 1.3 %collective-permute-start.2 = (f32[128,1152]{1,0:T(8,128)S(1)}, f32[128,1152]{1,0:T(8,128)S(1)}, u32[]{:S(2)}, u32[]{:S(2)}) collective-permute-start(f32[128,1152]{1,0:T(8,128)S(1)} %copy-done), channel_id=1, source_target_pairs={{0,1023},{1,1022},{4,2},{5,3},{8,6},{9,7},{12,10},{13,11},{16,14},... | collective-permute-start | bytes 1769480 | tf_op jit(solution)/shard_map/ppermute | solution.py:178
  27.9 1.9 %collective-permute-start.4 = (f32[136,1152]{1,0:T(8,128)S(1)}, f32[136,1152]{1,0:T(8,128)S(1)}, u32[]{:S(2)}, u32[]{:S(2)}) collective-permute-start(f32[136,1152]{1,0:T(8,128)S(1)} %collective-permute-done.t1), channel_id=1, source_target_pairs={{0,4},{1,5},{2,6},{3,7},{4,8},{5,9},{6,10},{7,11},{8,12},{9,13},{1... | collective-permute-start | bytes 1880072 | tf_op jit(solution)/shard_map/ppermute | solution.py:178
  29.8 6.8 %collective-permute-done.2.far = f32[128,1152]{1,0:T(8,128)S(1)} collective-permute-done((f32[128,1152]{1,0:T(8,128)S(1)}, f32[128,1152]{1,0:T(8,128)S(1)}, u32[]{:S(2)}, u32[]{:S(2)}) %collective-permute-start.2) | collective-permute-done | bytes 589856 | tf_op jit(solution)/shard_map/ppermute | solution.py:178
  36.6 6.7 %collective-permute-done.3.u0 = f32[136,1152]{1,0:T(8,128)S(1)} collective-permute-done((f32[136,1152]{1,0:T(8,128)}, f32[136,1152]{1,0:T(8,128)S(1)}, u32[]{:S(2)}, u32[]{:S(2)}) %collective-permute-start.3) | collective-permute-done | bytes 626720 | tf_op jit(solution)/shard_map/ppermute | solution.py:178
  43.4 6.9 %first.1 = (bf16[384,1152]{1,0:T(8,128)(2,1)S(1)}, bf16[384,1152]{1,0:T(8,128)(2,1)S(1)}, f32[384,1152]{1,0:T(8,128)S(1)}, f32[128,1152]{1,0:T(8,128)S(1)}, f32[...) custom-call(s32[4]{0:T(128)S(1)} %pad_add_fusion.place, ...), custom_call_target="tpu_custom_call" | custom-call | flops 3057647616 | bytes 7077888 | tf_op jit(solution)/shard_map/first/pallas_call | solution.py:159
  50.3 2.2 %collective-permute-start.5 = (f32[128,1152]{1,0:T(8,128)}, f32[128,1152]{1,0:T(8,128)S(1)}, u32[]{:S(2)}, u32[]{:S(2)}) collective-permute-start(f32[128,1152]{1,0:T(8,128)} %get-tuple-element.36), channel_id=1, source_target_pairs={{0,1},{1,0},{2,3},{3,2},{4,5},{5,4},{6,7},{7,6},{8,9},{9,8},{10,11... | collective-permute-start | bytes 1769480 | tf_op jit(solution)/shard_map/ppermute | solution.py:178
  52.5 9.3 %collective-permute-start.6 = (f32[128,1152]{1,0:T(8,128)}, f32[128,1152]{1,0:T(8,128)}, u32[]{:S(2)}, u32[]{:S(2)}) collective-permute-start(f32[128,1152]{1,0:T(8,128)} %get-tuple-element.37), channel_id=1, source_target_pairs={{0,1021},{1,1020},{2,1023},{3,1022},{4,0},{5,1},{6,2},{7,3},{8,4},... | collective-permute-start | bytes 1769480 | tf_op jit(solution)/shard_map/ppermute | solution.py:178
  61.9 3.0 %last.1 = (f32[128,1152]{1,0:T(8,128)S(1)}, f32[128,1152]{1,0:T(8,128)S(1)}, f32[128,1152]{1,0:T(8,128)S(1)}, f32[128,1152]{1,0:T(8,128)S(1)}, f32[1,128]{1,0:T(1,128)S(1)}) custom-call(s32[4]{0:T(128)S(1)} %pad_add_fusion.place, f32[2]{0:T(128)S(1)} %pad_maximum_fusion.2.params, f32[1,128]{1,0:T(1,128)S(1)} %convert_bitcast_fusion.own, ...), custom_call_target="tpu_custom_call" | custom-call | flops 1019215872 | bytes 4718592 | tf_op jit(solution)/shard_map/last/pallas_call | solution.py:159
  64.9 3.1 %collective-permute-start.7 = (f32[128,1152]{1,0:T(8,128)S(1)}, f32[128,1152]{1,0:T(8,128)}, u32[]{:S(2)}, u32[]{:S(2)}) collective-permute-start(f32[128,1152]{1,0:T(8,128)S(1)} %get-tuple-element.38), channel_id=1, source_target_pairs={{0,1020},{1,1021},{2,1022},{3,1023},{4,1},{5,0},{6,3},{7,2},{8,5},... | collective-permute-start | bytes 1769480 | tf_op jit(solution)/shard_map/ppermute | solution.py:178
  68.0 1.9 %collective-permute-start.8 = (f32[128,1152]{1,0:T(8,128)S(1)}, f32[128,1152]{1,0:T(8,128)}, u32[]{:S(2)}, u32[]{:S(2)}) collective-permute-start(f32[128,1152]{1,0:T(8,128)S(1)} %get-tuple-element.39), channel_id=1, source_target_pairs={{0,2},{1,3},{2,0},{3,1},{4,6},{5,7},{6,4},{7,5},{8,10},{9,11},{10,... | collective-permute-start | bytes 1769480 | tf_op jit(solution)/shard_map/ppermute | solution.py:178
  69.9 4.0 %collective-permute-start.9 = (f32[128,1152]{1,0:T(8,128)S(1)}, f32[128,1152]{1,0:T(8,128)}, u32[]{:S(2)}, u32[]{:S(2)}) collective-permute-start(f32[128,1152]{1,0:T(8,128)S(1)} %get-tuple-element.40), channel_id=1, source_target_pairs={{2,4},{3,5},{6,8},{7,9},{10,12},{11,13},{14,16},{15,17},{18,20},{1... | collective-permute-start | bytes 1769480 | tf_op jit(solution)/shard_map/ppermute | solution.py:178
  73.9 10.5 %all_to_all.18 = f32[8,1,128]{2,1,0:T(1,128)S(1)} all-to-all(f32[8,1,128]{2,1,0:T(1,128)S(1)} %broadcast_in_dim.26), channel_id=1, replica_groups=mesh['y_hi'=2,'y_lo'=4,'x_hi'=2,'z_hi'=4,'z_lo'=4,'core'=2,'x_lo'=2] {'y..., dimensions={0} | all-to-all | bytes 8192 | tf_op jit(solution)/shard_map/all_to_all | solution.py:230
  84.4 6.6 %all_to_all.19 = f32[8,1,128]{2,1,0:T(1,128)S(1)} all-to-all(f32[8,1,128]{2,1,0:T(1,128)S(1)} %broadcast_in_dim.27), channel_id=1, replica_groups=mesh['y_hi'=2,'y_lo'=4,'x_hi'=2,'z_hi'=4,'z_lo'=4,'core'=2,'x_lo'=2] {'x..., dimensions={0} | all-to-all | bytes 8192 | tf_op jit(solution)/shard_map/all_to_all | solution.py:230
  91.1 0.6 broadcast_in_dim.29
  91.7 4.6 %all-to-all-start.2 = ((f32[16,1,128]{2,1,0:T(1,128)}), f32[16,1,128]{2,1,0:T(1,128)S(1)}, u32[]{:S(2)}, u32[]{:S(2)}) async-start(f32[16,1,128]{2,1,0:T(1,128)} %broadcast_in_dim.29), calls=%async_computation.2 | async-start | bytes 16384 | tf_op jit(solution)/shard_map/all_to_all | solution.py:230
  96.3 2.8 %add_add_fusion = (f32[128,1152]{1,0:T(8,128)}, f32[128,1152]{1,0:T(8,128)}) fusion(f32[128,1152]{1,0:T(8,128)} %collective-permute-done.7, f32[128,1152]{1,0:T(8,128)} %collective-permute-done.6, f32[128,1152]{1,0:T(8,128)S(1)} %get-tuple-element.45, f32[128,1152]{1,0:T(8,128)S(1)} %collective-permute-done.5, f32[128,1152]{1,0:T(8,128)} %collective-permute-done.9, ...), kind=kLoop, calls=%fused_computation.2 | loop fusion | flops 737280 | bytes 5308416 | tf_op jit(solution)/shard_map/add | solution.py:237
  99.1 8.4 %all-to-all-done.2 = f32[16,1,128]{2,1,0:T(1,128)S(1)} async-done(((f32[16,1,128]{2,1,0:T(1,128)}), f32[16,1,128]{2,1,0:T(1,128)S(1)}, u32[]{:S(2)}, u32[]{:S(2)}) %all-to-all-start.2) | async-done | bytes 8224 | tf_op jit(solution)/shard_map/all_to_all | solution.py:230
  107.6 0.6 fusion
  (18 shorter events, 0.2 us)
Async XLA Ops:
  0.6 24.5 %copy-start = (f32[128,1152]{1,0:T(8,128)S(1)}, f32[128,1152]{1,0:T(8,128)}, u32[]{:S(2)}) copy-start(f32[128,1152]{1,0:T(8,128)} %image.1) | copy-start | bytes 1769476
  3.3 24.6 %collective-permute-start = (f32[136,1152]{1,0:T(8,128)}, f32[136,1152]{1,0:T(8,128)S(1)}, u32[]{:S(2)}, u32[]{:S(2)}) collective-permute-start(f32[136,1152]{1,0:T(8,128)} %pad_maximum_fusion), channel_id=1, source_target_pairs={{0,1},{1,0},{2,3},{3,2},{4,5},{5,4},{6,7},{7,6},{8,9},{9,8},{10,11... | collective-permute-start | bytes 1880072 | tf_op jit(solution)/shard_map/ppermute | solution.py:178
  7.2 36.1 %collective-permute-start.3 = (f32[136,1152]{1,0:T(8,128)}, f32[136,1152]{1,0:T(8,128)S(1)}, u32[]{:S(2)}, u32[]{:S(2)}) collective-permute-start(f32[136,1152]{1,0:T(8,128)} %pad_maximum_fusion), channel_id=1, source_target_pairs={{0,4},{1,5},{2,6},{3,7},{4,8},{5,9},{6,10},{7,11},{8,12},{9,13},{1... | collective-permute-start | bytes 1880072 | tf_op jit(solution)/shard_map/ppermute | solution.py:178
  13.2 30.2 %collective-permute-start.1 = (f32[136,1152]{1,0:T(8,128)}, f32[136,1152]{1,0:T(8,128)S(1)}, u32[]{:S(2)}, u32[]{:S(2)}) collective-permute-start(f32[136,1152]{1,0:T(8,128)} %pad_maximum_fusion.1), channel_id=1, source_target_pairs={{0,2},{1,3},{2,0},{3,1},{4,6},{5,7},{6,4},{7,5},{8,10},{9,11},{10,... | collective-permute-start | bytes 1880072 | tf_op jit(solution)/shard_map/ppermute | solution.py:178
  25.1 11.5 %collective-permute-start.2 = (f32[128,1152]{1,0:T(8,128)S(1)}, f32[128,1152]{1,0:T(8,128)S(1)}, u32[]{:S(2)}, u32[]{:S(2)}) collective-permute-start(f32[128,1152]{1,0:T(8,128)S(1)} %copy-done), channel_id=1, source_target_pairs={{0,1023},{1,1022},{4,2},{5,3},{8,6},{9,7},{12,10},{13,11},{16,14},... | collective-permute-start | bytes 1769480 | tf_op jit(solution)/shard_map/ppermute | solution.py:178
  27.9 33.9 %collective-permute-start.4 = (f32[136,1152]{1,0:T(8,128)S(1)}, f32[136,1152]{1,0:T(8,128)S(1)}, u32[]{:S(2)}, u32[]{:S(2)}) collective-permute-start(f32[136,1152]{1,0:T(8,128)S(1)} %collective-permute-done.t1), channel_id=1, source_target_pairs={{0,4},{1,5},{2,6},{3,7},{4,8},{5,9},{6,10},{7,11},{8,12},{9,13},{1... | collective-permute-start | bytes 1880072 | tf_op jit(solution)/shard_map/ppermute | solution.py:178
  50.3 40.8 %collective-permute-start.5 = (f32[128,1152]{1,0:T(8,128)}, f32[128,1152]{1,0:T(8,128)S(1)}, u32[]{:S(2)}, u32[]{:S(2)}) collective-permute-start(f32[128,1152]{1,0:T(8,128)} %get-tuple-element.36), channel_id=1, source_target_pairs={{0,1},{1,0},{2,3},{3,2},{4,5},{5,4},{6,7},{7,6},{8,9},{9,8},{10,11... | collective-permute-start | bytes 1769480 | tf_op jit(solution)/shard_map/ppermute | solution.py:178
  52.5 38.6 %collective-permute-start.6 = (f32[128,1152]{1,0:T(8,128)}, f32[128,1152]{1,0:T(8,128)}, u32[]{:S(2)}, u32[]{:S(2)}) collective-permute-start(f32[128,1152]{1,0:T(8,128)} %get-tuple-element.37), channel_id=1, source_target_pairs={{0,1021},{1,1020},{2,1023},{3,1022},{4,0},{5,1},{6,2},{7,3},{8,4},... | collective-permute-start | bytes 1769480 | tf_op jit(solution)/shard_map/ppermute | solution.py:178
  64.9 26.2 %collective-permute-start.7 = (f32[128,1152]{1,0:T(8,128)S(1)}, f32[128,1152]{1,0:T(8,128)}, u32[]{:S(2)}, u32[]{:S(2)}) collective-permute-start(f32[128,1152]{1,0:T(8,128)S(1)} %get-tuple-element.38), channel_id=1, source_target_pairs={{0,1020},{1,1021},{2,1022},{3,1023},{4,1},{5,0},{6,3},{7,2},{8,5},... | collective-permute-start | bytes 1769480 | tf_op jit(solution)/shard_map/ppermute | solution.py:178
  68.0 23.1 %collective-permute-start.8 = (f32[128,1152]{1,0:T(8,128)S(1)}, f32[128,1152]{1,0:T(8,128)}, u32[]{:S(2)}, u32[]{:S(2)}) collective-permute-start(f32[128,1152]{1,0:T(8,128)S(1)} %get-tuple-element.39), channel_id=1, source_target_pairs={{0,2},{1,3},{2,0},{3,1},{4,6},{5,7},{6,4},{7,5},{8,10},{9,11},{10,... | collective-permute-start | bytes 1769480 | tf_op jit(solution)/shard_map/ppermute | solution.py:178
  69.9 21.2 %collective-permute-start.9 = (f32[128,1152]{1,0:T(8,128)S(1)}, f32[128,1152]{1,0:T(8,128)}, u32[]{:S(2)}, u32[]{:S(2)}) collective-permute-start(f32[128,1152]{1,0:T(8,128)S(1)} %get-tuple-element.40), channel_id=1, source_target_pairs={{2,4},{3,5},{6,8},{7,9},{10,12},{11,13},{14,16},{15,17},{18,20},{1... | collective-permute-start | bytes 1769480 | tf_op jit(solution)/shard_map/ppermute | solution.py:178
  91.7 15.8 %all-to-all-start.2 = ((f32[16,1,128]{2,1,0:T(1,128)}), f32[16,1,128]{2,1,0:T(1,128)S(1)}, u32[]{:S(2)}, u32[]{:S(2)}) async-start(f32[16,1,128]{2,1,0:T(1,128)} %broadcast_in_dim.29), calls=%async_computation.2 | async-start | bytes 16384 | tf_op jit(solution)/shard_map/all_to_all | solution.py:230

commit v4 on v3

--- a/solution.py
+++ b/solution.py
@@ -95,13 +95,29 @@
     return jnp.concatenate(weights, 0), sums * (1.0 / tokens)
 
 
+def pack_kernel(ids, image, text, image_packet, text_packet, arrived):
+    size = ids.shape[1]
+    packets = (text_packet, image_packet)
+    copies = [
+        pltpu.make_async_copy(source, packet.at[0:size], arrived.at[n])
+        for n, (source, packet) in enumerate(zip((text, image), packets))
+    ]
+    for copy in copies:
+        copy.start()
+    for packet in packets:
+        packet[size:, :] = jnp.zeros_like(packet[size:, :])
+        packet[size : size + 1, 0:size] = ids[...].astype(F32)
+    for copy in copies:
+        copy.wait()
+
+
 def first_kernel(
-    tokens, place, params, own, i2, far, t1, u0, image, text,
-    high, low, images, gt0, gt1, gu0, mate, sums, i0, t0, arrived,
+    tokens, place, params, i2, far, t1, u0, image, text, ids,
+    high, low, images, gt0, gt1, gu0, tags, sums, i0, t0, held_ids, arrived,
 ):
     copies = [
         pltpu.make_async_copy(source, target, arrived.at[n])
-        for n, (source, target) in enumerate(((image, i0), (text, t0)))
+        for n, (source, target) in enumerate(((image, i0), (text, t0), (ids, held_ids)))
     ]
     for copy in copies:
         copy.start()
@@ -122,8 +138,9 @@
     cols = joined(halves(t0[...]), near_cols, lone_cols)
     dists = [[(i - p, True), (i - (p ^ 1), True), (i + 4 - q, True)] for i in (p, p ^ 2)]
     sim = long_product(rows, cols, ((1,), (1,)))
-    mate[...] = tag(i2)
-    row_ids, col_ids = (own[...], mate[...]), (own[...], tag(t1), tag(u0))
+    own, mate = held_ids[...].astype(F32), tag(i2)
+    tags[0:1, :], tags[1:2, :] = own, mate
+    row_ids, col_ids = (own, mate), (own, tag(t1), tag(u0))
     weights, more = weigh(sim, dists, row_ids, col_ids, params[0], params[1], tokens)
     sums[...] = parts + more
     images[0:both, :] = gradient(weights, cols, params[0], long_product)
@@ -133,14 +150,14 @@
     gu0[...] += texts[both:, :]
 
 
-def last_kernel(tokens, place, params, own, mate, high, low, u1, images, sums_in, gi0, gi2, gfar, gu1, sums):
+def last_kernel(tokens, place, params, tags, high, low, u1, images, sums_in, gi0, gi2, gfar, gu1, sums):
     p, q, r, core = place[0], place[1], place[2], place[3]
-    size = own.shape[1]
+    size = tags.shape[1]
     rows, cols = (high[...], low[...]), halves(u1[0:size, :])
     dists = [[(i + 4 - (q ^ 1), True)] for i in (p, p ^ 2)]
     dists.append([((r ^ 2) + 8 - (q ^ 1), core == 1)])
     sim = product(rows, cols, ((1,), (1,)))
-    weights, parts = weigh(sim, dists, (own[...], mate[...]), (tag(u1),), params[0], params[1], tokens)
+    weights, parts = weigh(sim, dists, (tags[0:1, :], tags[1:2, :]), (tag(u1),), params[0], params[1], tokens)
     sums[...] = sums_in[...] + parts
     grads = images[...] + gradient(weights, cols, params[0], product)
     gi0[...] = grads[0:size, :]
@@ -149,19 +166,35 @@
     gu1[...] = gradient(jnp.transpose(weights), rows, params[0], product)
 
 
+def pack(ids, image, text):
+    plain = pl.BlockSpec(memory_space=pltpu.HBM)
+    size, width = image.shape
+    packet = jax.ShapeDtypeStruct((size + 8, width), F32)
+    image, text = (pltpu.with_memory_space_constraint(x, pltpu.HBM) for x in (image, text))
+    return pl.pallas_call(
+        pack_kernel,
+        out_shape=[packet] * 2,
+        in_specs=[VMEM, plain, plain],
+        out_specs=[VMEM] * 2,
+        scratch_shapes=[pltpu.SemaphoreType.DMA((2,))],
+        cost_estimate=pl.CostEstimate(flops=0, bytes_accessed=2 << 21, transcendentals=0),
+        name="pack",
+    )(ids, image, text)
+
+
 def kernel_call(body, name, shapes, rows, cols, *args, plain=0):
     cost = pl.CostEstimate(
         flops=18 * rows * cols * 1152, bytes_accessed=8 * 1152 * (rows + cols), transcendentals=2 * rows * cols
     )
     near = len(args) - plain
     far = [pltpu.with_memory_space_constraint(arg, pltpu.HBM) for arg in args[near:]]
-    block = pltpu.VMEM((128, 1152), F32)
     return pl.pallas_call(
         body,
         out_shape=[jax.ShapeDtypeStruct(shape, dtype) for shape, dtype in shapes],
         in_specs=[SMEM, SMEM] + [VMEM] * (near - 2) + [pl.BlockSpec(memory_space=pltpu.HBM)] * plain,
         out_specs=[VMEM] * len(shapes),
-        scratch_shapes=[block] * plain + [pltpu.SemaphoreType.DMA((plain,))] * (plain > 0),
+        scratch_shapes=[pltpu.VMEM(arg.shape, arg.dtype) for arg in far]
+        + [pltpu.SemaphoreType.DMA((plain,))] * (plain > 0),
         compiler_params=pltpu.CompilerParams(vmem_limit_bytes=16 << 20),
         cost_estimate=cost,
         name=name,
@@ -191,26 +224,24 @@
     place = jnp.stack([p, q, r, core]).astype(jnp.int32)
     params = jnp.stack([log_scale, bias])
 
-    own = video_ids.astype(F32)[None]
-    label = jnp.pad(own, ((0, 7), (0, width - size)))
-    packet = jnp.concatenate([text, label], 0)
-    t1 = beside(packet)
-    u0 = send(packet, up)
+    own = video_ids[None]
+    image_packet, text_packet = pack(own, image, text)
+    t1 = beside(text_packet)
+    u0 = send(text_packet, up)
     far = send(image, lambda b: down(b) ^ 2, [b for b in everyone if b % 4 < 2])
-    label = lax.optimization_barrier(label)
-    i2 = other_core(jnp.concatenate([image, label], 0))
-    t1, place, params = lax.optimization_barrier((t1, place, params))
+    i2 = other_core(image_packet)
+    t1, far, place, params = lax.optimization_barrier((t1, far, place, params))
     u1 = send(t1, up)
 
     block, three, row = ((size, width), F32), (3 * size, width), ((1, size), F32)
-    high, low, images, gt0, gt1, gu0, mate, sums = kernel_call(
+    high, low, images, gt0, gt1, gu0, tags, sums = kernel_call(
         functools.partial(first_kernel, tokens),
         "first",
-        [(three, BF16), (three, BF16), (three, F32), block, block, block, row, row],
+        [(three, BF16), (three, BF16), (three, F32), block, block, block, ((2, size), F32), row],
         384,
         384,
-        *(place, params, own, i2, far, t1, u0, image, text),
-        plain=2,
+        *(place, params, i2, far, t1, u0, image, text, own),
+        plain=3,
     )
     gt1, gu0 = beside(gt1), send(gu0, down)
     gi0, gi2, gfar, gu1, sums = kernel_call(
@@ -219,7 +250,7 @@
         [block, block, block, block, row],
         384,
         128,
-        *(place, params, own, mate, high, low, u1, images, sums),
+        *(place, params, tags, high, low, u1, images, sums),
     )
     gu1 = send(gu1, lambda b: down(b) ^ 1)
     gi2 = other_core(gi2)
@@ -229,8 +260,7 @@
         shares = jnp.broadcast_to(row, (lax.axis_size(axes), size))
         return jnp.sum(lax.all_to_all(shares, axes, 0, 0, tiled=True), axis=0, keepdims=True)
 
-    sums = add_up(sums, ("y_hi", "y_lo"))
-    sums = add_up(sums, ("x_hi", "core", "x_lo"))
+    sums = add_up(sums, ("y_hi", "y_lo", "x_hi", "core", "x_lo"))
     sums, gt1, gu0, gu1, gi2, gfar = lax.optimization_barrier((sums, gt1, gu0, gu1, gi2, gfar))
     sums = add_up(sums, ("z_hi", "z_lo"))
     grad_image = gi0 + gi2 + gfar

time: 109 us -> 107 us (0.982)
  starting transfers between devices: 48.2 us -> 57 us
  waiting for transfers between devices: 22 us -> 13.4 us
  other arithmetic: 7.6 us -> 3.74 us
  Pallas kernels: 9.91 us -> 12.9 us
    ppermute x10, waiting for transfers between devices: 13.5 us -> 4.93 us  [send(): return lax.ppermute(x, NAMES, [(b, to(b)) for b in senders])]
    ppermute x10, starting transfers between devices: 43.6 us -> 52 us  [send(): return lax.ppermute(x, NAMES, [(b, to(b)) for b in senders])]
    concatenate x2 -> x0, other arithmetic: 3.86 us -> none  [the longest x1 1.93 us: local(): i2 = other_core(jnp.concatenate([image, label], 0))]
    pallas_call x0 -> x1, Pallas kernels: none -> 2.97 us  [pack(): pl.pallas_call(pack_kernel, out_shape=[packet] * 2, in_specs=[VMEM, plain...]
    all_to_all x2 -> x1, blocking collectives: 17.2 us -> 16.2 us  [add_up(): lax.all_to_all(shares, axes, 0, 0, tiled=True)]
  transfers between devices with their start and end apart: 11 -> 11, of which waited for: 3 -> 3; matrix products, arithmetic and copies ran while one was open for 5% -> 4% of each run, Pallas kernels for 9% -> 9%
where the time goes in v4:
time: 107 us
  starting transfers between devices  57 us (53%)
  blocking collectives  16.2 us (15%)
  waiting for transfers between devices  13.4 us (13%)
  Pallas kernels  12.9 us (12%)
  other arithmetic  3.74 us (3%)
  between operations  2.09 us (2%)
  local copies, waits for them, and re-layouts  1.21 us (1%)
    ppermute x10, starting transfers between devices, send(): return lax.ppermute(x, NAMES, [(b, to(b)) for b in senders])  52 us
    all_to_all x1, blocking collectives, add_up(): lax.all_to_all(shares, axes, 0, 0, tiled=True)  16.2 us
    pallas_call x2, Pallas kernels, kernel_call(): pl.pallas_call(body, out_shape=[jax.ShapeDtypeStruct(shape, dtype) for sh...  9.91 us
    all_to_all x1, waiting for transfers between devices, add_up(): lax.all_to_all(shares, axes, 0, 0, tiled=True)  8.45 us
    all_to_all x1, starting transfers between devices, add_up(): lax.all_to_all(shares, axes, 0, 0, tiled=True)  5.01 us
    ppermute x10, waiting for transfers between devices, send(): return lax.ppermute(x, NAMES, [(b, to(b)) for b in senders])  4.93 us
    pallas_call x1, Pallas kernels, pack(): pl.pallas_call(pack_kernel, out_shape=[packet] * 2, in_specs=[VMEM, plain...  2.97 us
    add x1, other arithmetic, local(): grad_text = gt0 + gt1 + gu0 + gu1  2.79 us
  transfers between devices with their start and end apart: 11, of which 3 were waited for; matrix products, arithmetic and copies ran while one was open for 4% of the time, Pallas kernels for 9%

profile of v4, /device:TPU:1, one launch (start us, length us, event | category | flops | bytes accessed | tf_op | source)
XLA Modules:
  0.0 106.5 jit_solution(8792494526880018720)
XLA Ops:
  0.6 3.0 %pack.1 = (f32[136,1152]{1,0:T(8,128)}, f32[136,1152]{1,0:T(8,128)}) custom-call(s32[1,128]{1,0:T(1,128)} %bitcast.22, f32[128,1152]{1,0:T(8,128)} %image.3, f32[128,1152]{1,0:T(8,128)} %text.3), custom_call_target="tpu_custom_call" | custom-call | bytes 4194304 | tf_op jit(solution)/shard_map/pack/pallas_call | solution.py:174
  3.6 3.9 %collective-permute-start = (f32[136,1152]{1,0:T(8,128)}, f32[136,1152]{1,0:T(8,128)S(1)}, u32[]{:S(2)}, u32[]{:S(2)}) collective-permute-start(f32[136,1152]{1,0:T(8,128)} %get-tuple-element.30), channel_id=1, source_target_pairs={{0,1},{1,0},{2,3},{3,2},{4,5},{5,4},{6,7},{7,6},{8,9},{9,8},{10,11... | collective-permute-start | bytes 1880072 | tf_op jit(solution)/shard_map/ppermute | solution.py:211
  7.6 1.3 %collective-permute-start.1 = (f32[128,1152]{1,0:T(8,128)}, f32[128,1152]{1,0:T(8,128)S(1)}, u32[]{:S(2)}, u32[]{:S(2)}) collective-permute-start(f32[128,1152]{1,0:T(8,128)} %image.3), channel_id=1, source_target_pairs={{0,1023},{1,1022},{4,2},{5,3},{8,6},{9,7},{12,10},{13,11},{16,14},... | collective-permute-start | bytes 1769480 | tf_op jit(solution)/shard_map/ppermute | solution.py:211
  8.9 4.0 %collective-permute-start.3 = (f32[136,1152]{1,0:T(8,128)}, f32[136,1152]{1,0:T(8,128)S(1)}, u32[]{:S(2)}, u32[]{:S(2)}) collective-permute-start(f32[136,1152]{1,0:T(8,128)} %get-tuple-element.30), channel_id=1, source_target_pairs={{0,4},{1,5},{2,6},{3,7},{4,8},{5,9},{6,10},{7,11},{8,12},{9,13},{1... | collective-permute-start | bytes 1880072 | tf_op jit(solution)/shard_map/ppermute | solution.py:211
  12.9 21.3 %collective-permute-start.2 = (f32[136,1152]{1,0:T(8,128)}, f32[136,1152]{1,0:T(8,128)S(1)}, u32[]{:S(2)}, u32[]{:S(2)}) collective-permute-start(f32[136,1152]{1,0:T(8,128)} %get-tuple-element.33), channel_id=1, source_target_pairs={{0,2},{1,3},{2,0},{3,1},{4,6},{5,7},{6,4},{7,5},{8,10},{9,11},{10,... | collective-permute-start | bytes 1880072 | tf_op jit(solution)/shard_map/ppermute | solution.py:211
  35.5 0.1 pad_maximum_fusion.params
  35.6 0.1 pad_add_fusion.place
  35.7 1.9 %collective-permute-start.4 = (f32[136,1152]{1,0:T(8,128)S(1)}, f32[136,1152]{1,0:T(8,128)S(1)}, u32[]{:S(2)}, u32[]{:S(2)}) collective-permute-start(f32[136,1152]{1,0:T(8,128)S(1)} %collective-permute-done.t1), channel_id=1, source_target_pairs={{0,4},{1,5},{2,6},{3,7},{4,8},{5,9},{6,10},{7,11},{8,12},{9,13},{1... | collective-permute-start | bytes 1880072 | tf_op jit(solution)/shard_map/ppermute | solution.py:211
  37.6 1.5 %collective-permute-done.3.u0 = f32[136,1152]{1,0:T(8,128)S(1)} collective-permute-done((f32[136,1152]{1,0:T(8,128)}, f32[136,1152]{1,0:T(8,128)S(1)}, u32[]{:S(2)}, u32[]{:S(2)}) %collective-permute-start.3) | collective-permute-done | bytes 626720 | tf_op jit(solution)/shard_map/ppermute | solution.py:211
  39.1 6.9 %first.1 = (bf16[384,1152]{1,0:T(8,128)(2,1)S(1)}, bf16[384,1152]{1,0:T(8,128)(2,1)S(1)}, f32[384,1152]{1,0:T(8,128)S(1)}, f32[128,1152]{1,0:T(8,128)S(1)}, f32[...) custom-call(s32[4]{0:T(128)S(1)} %pad_add_fusion.place, ...), custom_call_target="tpu_custom_call" | custom-call | flops 3057647616 | bytes 7077888 | tf_op jit(solution)/shard_map/first/pallas_call | solution.py:191
  46.0 2.2 %collective-permute-start.5 = (f32[128,1152]{1,0:T(8,128)}, f32[128,1152]{1,0:T(8,128)S(1)}, u32[]{:S(2)}, u32[]{:S(2)}) collective-permute-start(f32[128,1152]{1,0:T(8,128)} %get-tuple-element.42), channel_id=1, source_target_pairs={{0,1},{1,0},{2,3},{3,2},{4,5},{5,4},{6,7},{7,6},{8,9},{9,8},{10,11... | collective-permute-start | bytes 1769480 | tf_op jit(solution)/shard_map/ppermute | solution.py:211
  48.3 9.3 %collective-permute-start.6 = (f32[128,1152]{1,0:T(8,128)}, f32[128,1152]{1,0:T(8,128)}, u32[]{:S(2)}, u32[]{:S(2)}) collective-permute-start(f32[128,1152]{1,0:T(8,128)} %get-tuple-element.43), channel_id=1, source_target_pairs={{0,1021},{1,1020},{2,1023},{3,1022},{4,0},{5,1},{6,2},{7,3},{8,4},... | collective-permute-start | bytes 1769480 | tf_op jit(solution)/shard_map/ppermute | solution.py:211
  57.6 3.4 %collective-permute-done.4.u1 = f32[136,1152]{1,0:T(8,128)S(1)} collective-permute-done((f32[136,1152]{1,0:T(8,128)S(1)}, f32[136,1152]{1,0:T(8,128)S(1)}, u32[]{:S(2)}, u32[]{:S(2)}) %collective-permute-start.4) | collective-permute-done | bytes 626720 | tf_op jit(solution)/shard_map/ppermute | solution.py:211
  61.0 3.0 %last.1 = (f32[128,1152]{1,0:T(8,128)S(1)}, f32[128,1152]{1,0:T(8,128)S(1)}, f32[128,1152]{1,0:T(8,128)S(1)}, f32[128,1152]{1,0:T(8,128)S(1)}, f32[1,128]{1,0:T(1,128)S(1)}) custom-call(s32[4]{0:T(128)S(1)} %pad_add_fusion.place, f32[2]{0:T(128)S(1)} %pad_maximum_fusion.params, f32[2,128]{1,0:T(2,128)S(1)} %get-tuple-element.36.tags, ...), custom_call_target="tpu_custom_call" | custom-call | flops 1019215872 | bytes 4718592 | tf_op jit(solution)/shard_map/last/pallas_call | solution.py:191
  64.0 2.7 %collective-permute-start.7 = (f32[128,1152]{1,0:T(8,128)S(1)}, f32[128,1152]{1,0:T(8,128)}, u32[]{:S(2)}, u32[]{:S(2)}) collective-permute-start(f32[128,1152]{1,0:T(8,128)S(1)} %get-tuple-element.44), channel_id=1, source_target_pairs={{0,1020},{1,1021},{2,1022},{3,1023},{4,1},{5,0},{6,3},{7,2},{8,5},... | collective-permute-start | bytes 1769480 | tf_op jit(solution)/shard_map/ppermute | solution.py:211
  66.7 3.2 %collective-permute-start.8 = (f32[128,1152]{1,0:T(8,128)S(1)}, f32[128,1152]{1,0:T(8,128)}, u32[]{:S(2)}, u32[]{:S(2)}) collective-permute-start(f32[128,1152]{1,0:T(8,128)S(1)} %get-tuple-element.45), channel_id=1, source_target_pairs={{0,2},{1,3},{2,0},{3,1},{4,6},{5,7},{6,4},{7,5},{8,10},{9,11},{10,... | collective-permute-start | bytes 1769480 | tf_op jit(solution)/shard_map/ppermute | solution.py:211
  69.9 2.1 %collective-permute-start.9 = (f32[128,1152]{1,0:T(8,128)S(1)}, f32[128,1152]{1,0:T(8,128)}, u32[]{:S(2)}, u32[]{:S(2)}) collective-permute-start(f32[128,1152]{1,0:T(8,128)S(1)} %get-tuple-element.46), channel_id=1, source_target_pairs={{2,4},{3,5},{6,8},{7,9},{10,12},{11,13},{14,16},{15,17},{18,20},{1... | collective-permute-start | bytes 1769480 | tf_op jit(solution)/shard_map/ppermute | solution.py:211
  72.0 16.2 %all_to_all.12 = f32[64,1,128]{2,1,0:T(1,128)} all-to-all(f32[64,1,128]{2,1,0:T(1,128)S(1)} %broadcast_in_dim.20), channel_id=1, replica_groups=mesh['y_hi'=2,'y_lo'=4,'x_hi'=2,'z_hi'=4,'z_lo'=4,'core'=2,'x_lo'=2] {'y..., dimensions={0} | all-to-all | bytes 65536 | tf_op jit(solution)/shard_map/all_to_all | solution.py:261
  88.2 0.8 reduce_sum.18
  89.0 0.6 broadcast_in_dim.22
  89.6 5.0 %all-to-all-start.1 = ((f32[16,1,128]{2,1,0:T(1,128)}), f32[16,1,128]{2,1,0:T(1,128)S(1)}, u32[]{:S(2)}, u32[]{:S(2)}) async-start(f32[16,1,128]{2,1,0:T(1,128)} %broadcast_in_dim.22), calls=%async_computation.1 | async-start | bytes 16384 | tf_op jit(solution)/shard_map/all_to_all | solution.py:261
  94.6 2.8 %add_add_fusion = (f32[128,1152]{1,0:T(8,128)}, f32[128,1152]{1,0:T(8,128)}) fusion(f32[128,1152]{1,0:T(8,128)} %collective-permute-done.7, f32[128,1152]{1,0:T(8,128)} %collective-permute-done.6, f32[128,1152]{1,0:T(8,128)S(1)} %get-tuple-element.51, f32[128,1152]{1,0:T(8,128)S(1)} %collective-permute-done.5, f32[128,1152]{1,0:T(8,128)} %collective-permute-done.9, ...), kind=kLoop, calls=%fused_computation | loop fusion | flops 737280 | bytes 5308416 | tf_op jit(solution)/shard_map/add | solution.py:267
  97.4 8.4 %all-to-all-done.1 = f32[16,1,128]{2,1,0:T(1,128)S(1)} async-done(((f32[16,1,128]{2,1,0:T(1,128)}), f32[16,1,128]{2,1,0:T(1,128)S(1)}, u32[]{:S(2)}, u32[]{:S(2)}) %all-to-all-start.1) | async-done | bytes 8224 | tf_op jit(solution)/shard_map/all_to_all | solution.py:261
  105.9 0.6 fusion
  (10 shorter events, 0.1 us)
Async XLA Ops:
  3.6 32.1 %collective-permute-start = (f32[136,1152]{1,0:T(8,128)}, f32[136,1152]{1,0:T(8,128)S(1)}, u32[]{:S(2)}, u32[]{:S(2)}) collective-permute-start(f32[136,1152]{1,0:T(8,128)} %get-tuple-element.30), channel_id=1, source_target_pairs={{0,1},{1,0},{2,3},{3,2},{4,5},{5,4},{6,7},{7,6},{8,9},{9,8},{10,11... | collective-permute-start | bytes 1880072 | tf_op jit(solution)/shard_map/ppermute | solution.py:211
  7.6 28.1 %collective-permute-start.1 = (f32[128,1152]{1,0:T(8,128)}, f32[128,1152]{1,0:T(8,128)S(1)}, u32[]{:S(2)}, u32[]{:S(2)}) collective-permute-start(f32[128,1152]{1,0:T(8,128)} %image.3), channel_id=1, source_target_pairs={{0,1023},{1,1022},{4,2},{5,3},{8,6},{9,7},{12,10},{13,11},{16,14},... | collective-permute-start | bytes 1769480 | tf_op jit(solution)/shard_map/ppermute | solution.py:211
  8.9 30.3 %collective-permute-start.3 = (f32[136,1152]{1,0:T(8,128)}, f32[136,1152]{1,0:T(8,128)S(1)}, u32[]{:S(2)}, u32[]{:S(2)}) collective-permute-start(f32[136,1152]{1,0:T(8,128)} %get-tuple-element.30), channel_id=1, source_target_pairs={{0,4},{1,5},{2,6},{3,7},{4,8},{5,9},{6,10},{7,11},{8,12},{9,13},{1... | collective-permute-start | bytes 1880072 | tf_op jit(solution)/shard_map/ppermute | solution.py:211
  12.9 26.2 %collective-permute-start.2 = (f32[136,1152]{1,0:T(8,128)}, f32[136,1152]{1,0:T(8,128)S(1)}, u32[]{:S(2)}, u32[]{:S(2)}) collective-permute-start(f32[136,1152]{1,0:T(8,128)} %get-tuple-element.33), channel_id=1, source_target_pairs={{0,2},{1,3},{2,0},{3,1},{4,6},{5,7},{6,4},{7,5},{8,10},{9,11},{10,... | collective-permute-start | bytes 1880072 | tf_op jit(solution)/shard_map/ppermute | solution.py:211
  35.7 25.3 %collective-permute-start.4 = (f32[136,1152]{1,0:T(8,128)S(1)}, f32[136,1152]{1,0:T(8,128)S(1)}, u32[]{:S(2)}, u32[]{:S(2)}) collective-permute-start(f32[136,1152]{1,0:T(8,128)S(1)} %collective-permute-done.t1), channel_id=1, source_target_pairs={{0,4},{1,5},{2,6},{3,7},{4,8},{5,9},{6,10},{7,11},{8,12},{9,13},{1... | collective-permute-start | bytes 1880072 | tf_op jit(solution)/shard_map/ppermute | solution.py:211
  46.0 43.0 %collective-permute-start.5 = (f32[128,1152]{1,0:T(8,128)}, f32[128,1152]{1,0:T(8,128)S(1)}, u32[]{:S(2)}, u32[]{:S(2)}) collective-permute-start(f32[128,1152]{1,0:T(8,128)} %get-tuple-element.42), channel_id=1, source_target_pairs={{0,1},{1,0},{2,3},{3,2},{4,5},{5,4},{6,7},{7,6},{8,9},{9,8},{10,11... | collective-permute-start | bytes 1769480 | tf_op jit(solution)/shard_map/ppermute | solution.py:211
  48.3 40.7 %collective-permute-start.6 = (f32[128,1152]{1,0:T(8,128)}, f32[128,1152]{1,0:T(8,128)}, u32[]{:S(2)}, u32[]{:S(2)}) collective-permute-start(f32[128,1152]{1,0:T(8,128)} %get-tuple-element.43), channel_id=1, source_target_pairs={{0,1021},{1,1020},{2,1023},{3,1022},{4,0},{5,1},{6,2},{7,3},{8,4},... | collective-permute-start | bytes 1769480 | tf_op jit(solution)/shard_map/ppermute | solution.py:211
  64.0 25.0 %collective-permute-start.7 = (f32[128,1152]{1,0:T(8,128)S(1)}, f32[128,1152]{1,0:T(8,128)}, u32[]{:S(2)}, u32[]{:S(2)}) collective-permute-start(f32[128,1152]{1,0:T(8,128)S(1)} %get-tuple-element.44), channel_id=1, source_target_pairs={{0,1020},{1,1021},{2,1022},{3,1023},{4,1},{5,0},{6,3},{7,2},{8,5},... | collective-permute-start | bytes 1769480 | tf_op jit(solution)/shard_map/ppermute | solution.py:211
  66.7 22.3 %collective-permute-start.8 = (f32[128,1152]{1,0:T(8,128)S(1)}, f32[128,1152]{1,0:T(8,128)}, u32[]{:S(2)}, u32[]{:S(2)}) collective-permute-start(f32[128,1152]{1,0:T(8,128)S(1)} %get-tuple-element.45), channel_id=1, source_target_pairs={{0,2},{1,3},{2,0},{3,1},{4,6},{5,7},{6,4},{7,5},{8,10},{9,11},{10,... | collective-permute-start | bytes 1769480 | tf_op jit(solution)/shard_map/ppermute | solution.py:211
  69.9 19.2 %collective-permute-start.9 = (f32[128,1152]{1,0:T(8,128)S(1)}, f32[128,1152]{1,0:T(8,128)}, u32[]{:S(2)}, u32[]{:S(2)}) collective-permute-start(f32[128,1152]{1,0:T(8,128)S(1)} %get-tuple-element.46), channel_id=1, source_target_pairs={{2,4},{3,5},{6,8},{7,9},{10,12},{11,13},{14,16},{15,17},{18,20},{1... | collective-permute-start | bytes 1769480 | tf_op jit(solution)/shard_map/ppermute | solution.py:211
  89.6 16.3 %all-to-all-start.1 = ((f32[16,1,128]{2,1,0:T(1,128)}), f32[16,1,128]{2,1,0:T(1,128)S(1)}, u32[]{:S(2)}, u32[]{:S(2)}) async-start(f32[16,1,128]{2,1,0:T(1,128)} %broadcast_in_dim.22), calls=%async_computation.1 | async-start | bytes 16384 | tf_op jit(solution)/shard_map/all_to_all | solution.py:261

commit v5 on v4

--- a/solution.py
+++ b/solution.py
@@ -95,25 +95,18 @@
     return jnp.concatenate(weights, 0), sums * (1.0 / tokens)
 
 
-def pack_kernel(ids, image, text, image_packet, text_packet, arrived):
-    size = ids.shape[1]
-    packets = (text_packet, image_packet)
-    copies = [
-        pltpu.make_async_copy(source, packet.at[0:size], arrived.at[n])
-        for n, (source, packet) in enumerate(zip((text, image), packets))
-    ]
-    for copy in copies:
-        copy.start()
-    for packet in packets:
-        packet[size:, :] = jnp.zeros_like(packet[size:, :])
-        packet[size : size + 1, 0:size] = ids[...].astype(F32)
-    for copy in copies:
-        copy.wait()
+def pack_kernel(ids, image, packet, arrived):
+    size = image.shape[0]
+    copy = pltpu.make_async_copy(image, packet.at[0:size], arrived)
+    copy.start()
+    packet[size:, :] = jnp.zeros_like(packet[size:, :])
+    packet[size : size + 1, 0:size] = ids[...].astype(F32)
+    copy.wait()
 
 
 def first_kernel(
-    tokens, place, params, i2, far, t1, u0, image, text, ids,
-    high, low, images, gt0, gt1, gu0, tags, sums, i0, t0, held_ids, arrived,
+    tokens, place, params, before, i2, far, t1, u0, image, text, ids,
+    high, low, images, gt0, gt1, gu0, tags, sums, i0, t0, held_ids, arrived, back, left,
 ):
     copies = [
         pltpu.make_async_copy(source, target, arrived.at[n])
@@ -124,13 +117,13 @@
     p, q, r, core = place[0], place[1], place[2], place[3]
     size = image.shape[0]
     both = 2 * size
-    lone_rows, lone_cols = halves(far[...]), halves(u0[0:size, :])
+    lone_rows, lone_cols = halves(far[...]), halves(u0[...])
     sim = product(lone_rows, lone_cols, ((1,), (1,)))
     lone, parts = weigh(sim, [[((r ^ 2) + 8 - q, core == 1)]], (), (), params[0], params[1], tokens)
-    images[both:, :] = gradient(lone, lone_cols, params[0], product)
-    gu0[...] = gradient(jnp.transpose(lone), lone_rows, params[0], product)
+    images[both:, :] = gradient(lone, lone_cols, params[0], long_product)
+    lone_texts = gradient(jnp.transpose(lone), lone_rows, params[0], long_product)
     high[both:, :], low[both:, :] = lone_rows
-    mate_rows, near_cols = halves(i2[0:size, :]), halves(t1[0:size, :])
+    mate_rows, near_cols = halves(i2[0:size, :]), halves(t1[...])
     for copy in copies:
         copy.wait()
     rows = joined(halves(i0[...]), mate_rows)
@@ -138,26 +131,34 @@
     cols = joined(halves(t0[...]), near_cols, lone_cols)
     dists = [[(i - p, True), (i - (p ^ 1), True), (i + 4 - q, True)] for i in (p, p ^ 2)]
     sim = long_product(rows, cols, ((1,), (1,)))
-    own, mate = held_ids[...].astype(F32), tag(i2)
-    tags[0:1, :], tags[1:2, :] = own, mate
-    row_ids, col_ids = (own, mate), (own, tag(t1), tag(u0))
+    own, mate, last = held_ids[...].astype(F32), tag(i2), before[...].astype(F32)
+    tags[0:1, :], tags[1:2, :], tags[2:3, :] = own, mate, last
+    row_ids, col_ids = (own, mate), (own, last, last)
     weights, more = weigh(sim, dists, row_ids, col_ids, params[0], params[1], tokens)
     sums[...] = parts + more
+    texts = gradient(jnp.transpose(weights), rows, params[0], long_product)
+    back[0:size, :] = texts[size:both, :]
+    back[size:, :] = texts[both:, :] + lone_texts
+    copies = [
+        pltpu.make_async_copy(back.at[n * size : (n + 1) * size], target, left.at[n])
+        for n, target in enumerate((gt1, gu0))
+    ]
+    for copy in copies:
+        copy.start()
+    gt0[...] = texts[0:size, :]
     images[0:both, :] = gradient(weights, cols, params[0], long_product)
-    texts = gradient(jnp.transpose(weights), rows, params[0], long_product)
-    gt0[...] = texts[0:size, :]
-    gt1[...] = texts[size:both, :]
-    gu0[...] += texts[both:, :]
+    for copy in copies:
+        copy.wait()
 
 
 def last_kernel(tokens, place, params, tags, high, low, u1, images, sums_in, gi0, gi2, gfar, gu1, sums):
     p, q, r, core = place[0], place[1], place[2], place[3]
     size = tags.shape[1]
-    rows, cols = (high[...], low[...]), halves(u1[0:size, :])
+    rows, cols = (high[...], low[...]), halves(u1[...])
     dists = [[(i + 4 - (q ^ 1), True)] for i in (p, p ^ 2)]
     dists.append([((r ^ 2) + 8 - (q ^ 1), core == 1)])
     sim = product(rows, cols, ((1,), (1,)))
-    weights, parts = weigh(sim, dists, (tags[0:1, :], tags[1:2, :]), (tag(u1),), params[0], params[1], tokens)
+    weights, parts = weigh(sim, dists, (tags[0:1, :], tags[1:2, :]), (tags[2:3, :],), params[0], params[1], tokens)
     sums[...] = sums_in[...] + parts
     grads = images[...] + gradient(weights, cols, params[0], product)
     gi0[...] = grads[0:size, :]
@@ -166,23 +167,20 @@
     gu1[...] = gradient(jnp.transpose(weights), rows, params[0], product)
 
 
-def pack(ids, image, text):
-    plain = pl.BlockSpec(memory_space=pltpu.HBM)
+def pack(ids, image):
     size, width = image.shape
-    packet = jax.ShapeDtypeStruct((size + 8, width), F32)
-    image, text = (pltpu.with_memory_space_constraint(x, pltpu.HBM) for x in (image, text))
     return pl.pallas_call(
         pack_kernel,
-        out_shape=[packet] * 2,
-        in_specs=[VMEM, plain, plain],
-        out_specs=[VMEM] * 2,
-        scratch_shapes=[pltpu.SemaphoreType.DMA((2,))],
-        cost_estimate=pl.CostEstimate(flops=0, bytes_accessed=2 << 21, transcendentals=0),
+        out_shape=jax.ShapeDtypeStruct((size + 8, width), F32),
+        in_specs=[VMEM, pl.BlockSpec(memory_space=pltpu.HBM)],
+        out_specs=VMEM,
+        scratch_shapes=[pltpu.SemaphoreType.DMA],
+        cost_estimate=pl.CostEstimate(flops=0, bytes_accessed=1 << 21, transcendentals=0),
         name="pack",
-    )(ids, image, text)
-
-
-def kernel_call(body, name, shapes, rows, cols, *args, plain=0):
+    )(ids, pltpu.with_memory_space_constraint(image, pltpu.HBM))
+
+
+def kernel_call(body, name, shapes, rows, cols, *args, plain=0, out=()):
     cost = pl.CostEstimate(
         flops=18 * rows * cols * 1152, bytes_accessed=8 * 1152 * (rows + cols), transcendentals=2 * rows * cols
     )
@@ -192,9 +190,10 @@
         body,
         out_shape=[jax.ShapeDtypeStruct(shape, dtype) for shape, dtype in shapes],
         in_specs=[SMEM, SMEM] + [VMEM] * (near - 2) + [pl.BlockSpec(memory_space=pltpu.HBM)] * plain,
-        out_specs=[VMEM] * len(shapes),
+        out_specs=[pl.BlockSpec(memory_space=pl.ANY) if n in out else VMEM for n in range(len(shapes))],
         scratch_shapes=[pltpu.VMEM(arg.shape, arg.dtype) for arg in far]
-        + [pltpu.SemaphoreType.DMA((plain,))] * (plain > 0),
+        + [pltpu.SemaphoreType.DMA((plain,))] * (plain > 0)
+        + [pltpu.VMEM((256, 1152), F32), pltpu.SemaphoreType.DMA((2,))] * (len(out) > 0),
         compiler_params=pltpu.CompilerParams(vmem_limit_bytes=16 << 20),
         cost_estimate=cost,
         name=name,
@@ -225,23 +224,24 @@
     params = jnp.stack([log_scale, bias])
 
     own = video_ids[None]
-    image_packet, text_packet = pack(own, image, text)
-    t1 = beside(text_packet)
-    u0 = send(text_packet, up)
+    t1 = beside(text)
+    u0 = send(text, up)
     far = send(image, lambda b: down(b) ^ 2, [b for b in everyone if b % 4 < 2])
-    i2 = other_core(image_packet)
-    t1, far, place, params = lax.optimization_barrier((t1, far, place, params))
+    before = send(own, lambda b: (b ^ 1) if b % 4 < 3 else (b + 3) % count)
+    i2 = other_core(pack(own, image))
+    t1, u0, far, before, place, params = lax.optimization_barrier((t1, u0, far, before, place, params))
     u1 = send(t1, up)
 
     block, three, row = ((size, width), F32), (3 * size, width), ((1, size), F32)
     high, low, images, gt0, gt1, gu0, tags, sums = kernel_call(
         functools.partial(first_kernel, tokens),
         "first",
-        [(three, BF16), (three, BF16), (three, F32), block, block, block, ((2, size), F32), row],
+        [(three, BF16), (three, BF16), (three, F32), block, block, block, ((3, size), F32), row],
         384,
         384,
-        *(place, params, i2, far, t1, u0, image, text, own),
+        *(place, params, before, i2, far, t1, u0, image, text, own),
         plain=3,
+        out=(4, 5),
     )
     gt1, gu0 = beside(gt1), send(gu0, down)
     gi0, gi2, gfar, gu1, sums = kernel_call(

time: 107 us -> 111 us (1.037)
  waiting for transfers between devices: 13.4 us -> 16.3 us
  starting transfers between devices: 57 us -> 59.1 us
  Pallas kernels: 12.9 us -> 11.5 us
    ppermute x10 -> x11, starting transfers between devices: 52 us -> 55.7 us  [send(): return lax.ppermute(x, NAMES, [(b, to(b)) for b in senders])]
    ppermute x10 -> x11, waiting for transfers between devices: 4.93 us -> 8.16 us  [send(): return lax.ppermute(x, NAMES, [(b, to(b)) for b in senders])]
    all_to_all x1, starting transfers between devices: 5.01 us -> 3.38 us  [add_up(): lax.all_to_all(shares, axes, 0, 0, tiled=True)]
  transfers between devices with their start and end apart: 11 -> 12, of which waited for: 3 -> 3; matrix products, arithmetic and copies ran while one was open for 4% -> 3% of each run, Pallas kernels for 9% -> 10%
where the time goes in v5:
time: 111 us; the launch traced here: 110 us
  starting transfers between devices  59.1 us (53%)
  blocking collectives  16.6 us (15%)
  waiting for transfers between devices  16.3 us (15%)
  Pallas kernels  11.5 us (10%)
  other arithmetic  3.23 us (3%)
  between operations  2.11 us (2%)
  local copies, waits for them, and re-layouts  1.21 us (1%)
    ppermute x11, starting transfers between devices, send(): return lax.ppermute(x, NAMES, [(b, to(b)) for b in senders])  55.7 us
    all_to_all x1, blocking collectives, add_up(): lax.all_to_all(shares, axes, 0, 0, tiled=True)  16.6 us
    pallas_call x2, Pallas kernels, kernel_call(): pl.pallas_call(body, out_shape=[jax.ShapeDtypeStruct(shape, dtype) for sh...  8.94 us
    ppermute x11, waiting for transfers between devices, send(): return lax.ppermute(x, NAMES, [(b, to(b)) for b in senders])  8.16 us
    all_to_all x1, waiting for transfers between devices, add_up(): lax.all_to_all(shares, axes, 0, 0, tiled=True)  8.13 us
    all_to_all x1, starting transfers between devices, add_up(): lax.all_to_all(shares, axes, 0, 0, tiled=True)  3.38 us
    add x1, other arithmetic, local(): grad_text = gt0 + gt1 + gu0 + gu1  3.04 us
    pallas_call x1, Pallas kernels, pack(): pl.pallas_call(pack_kernel, out_shape=jax.ShapeDtypeStruct((size + 8, wid...  2.55 us
  transfers between devices with their start and end apart: 12, of which 3 were waited for; matrix products, arithmetic and copies ran while one was open for 3% of the time, Pallas kernels for 10%

profile of v5, /device:TPU:1, one launch (start us, length us, event | category | flops | bytes accessed | tf_op | source)
XLA Modules:
  0.0 110.0 jit_solution(2749767756784723492)
XLA Ops:
  0.6 4.0 %collective-permute-start = (f32[128,1152]{1,0:T(8,128)}, f32[128,1152]{1,0:T(8,128)S(1)}, u32[]{:S(2)}, u32[]{:S(2)}) collective-permute-start(f32[128,1152]{1,0:T(8,128)} %text.1), channel_id=1, source_target_pairs={{0,1},{1,0},{2,3},{3,2},{4,5},{5,4},{6,7},{7,6},{8,9},{9,8},{10,11... | collective-permute-start | bytes 1769480 | tf_op jit(solution)/shard_map/ppermute | solution.py:210
  4.6 4.0 %collective-permute-start.1 = (f32[128,1152]{1,0:T(8,128)}, f32[128,1152]{1,0:T(8,128)S(1)}, u32[]{:S(2)}, u32[]{:S(2)}) collective-permute-start(f32[128,1152]{1,0:T(8,128)} %text.1), channel_id=1, source_target_pairs={{0,4},{1,5},{2,6},{3,7},{4,8},{5,9},{6,10},{7,11},{8,12},{9,13},{1... | collective-permute-start | bytes 1769480 | tf_op jit(solution)/shard_map/ppermute | solution.py:210
  8.6 1.3 %collective-permute-start.2 = (f32[128,1152]{1,0:T(8,128)}, f32[128,1152]{1,0:T(8,128)S(1)}, u32[]{:S(2)}, u32[]{:S(2)}) collective-permute-start(f32[128,1152]{1,0:T(8,128)} %image.3), channel_id=1, source_target_pairs={{0,1023},{1,1022},{4,2},{5,3},{8,6},{9,7},{12,10},{13,11},{16,14},... | collective-permute-start | bytes 1769480 | tf_op jit(solution)/shard_map/ppermute | solution.py:210
  9.9 2.6 %pack.1 = f32[136,1152]{1,0:T(8,128)} custom-call(s32[1,128]{1,0:T(1,128)} %bitcast.22, f32[128,1152]{1,0:T(8,128)} %image.3), custom_call_target="tpu_custom_call" | custom-call | bytes 2097152 | tf_op jit(solution)/shard_map/pack/pallas_call | solution.py:172
  12.5 21.3 %collective-permute-start.4 = (f32[136,1152]{1,0:T(8,128)}, f32[136,1152]{1,0:T(8,128)S(1)}, u32[]{:S(2)}, u32[]{:S(2)}) collective-permute-start(f32[136,1152]{1,0:T(8,128)} %pack.1), channel_id=1, source_target_pairs={{0,2},{1,3},{2,0},{3,1},{4,6},{5,7},{6,4},{7,5},{8,10},{9,11},{10,... | collective-permute-start | bytes 1880072 | tf_op jit(solution)/shard_map/ppermute | solution.py:210
  33.8 2.2 %collective-permute-start.3 = (s32[1,128]{1,0:T(1,128)}, s32[1,128]{1,0:T(1,128)S(1)}, u32[]{:S(2)}, u32[]{:S(2)}) collective-permute-start(s32[1,128]{1,0:T(1,128)} %bitcast.23), channel_id=1, source_target_pairs={{0,1},{1,0},{2,3},{3,6},{4,5},{5,4},{6,7},{7,10},{8,9},{9,8},{10,1... | collective-permute-start | bytes 1544 | tf_op jit(solution)/shard_map/ppermute | solution.py:210
  37.4 0.1 pad_maximum_fusion.params
  37.4 0.1 pad_add_fusion.place
  37.5 6.2 %collective-permute-done.3.before = s32[1,128]{1,0:T(1,128)S(1)} collective-permute-done((s32[1,128]{1,0:T(1,128)}, s32[1,128]{1,0:T(1,128)S(1)}, u32[]{:S(2)}, u32[]{:S(2)}) %collective-permute-start.3) | collective-permute-done | bytes 544 | tf_op jit(solution)/shard_map/ppermute | solution.py:210
  43.7 1.9 %collective-permute-start.5 = (f32[128,1152]{1,0:T(8,128)S(1)}, f32[128,1152]{1,0:T(8,128)S(1)}, u32[]{:S(2)}, u32[]{:S(2)}) collective-permute-start(f32[128,1152]{1,0:T(8,128)S(1)} %collective-permute-done.t1), channel_id=1, source_target_pairs={{0,4},{1,5},{2,6},{3,7},{4,8},{5,9},{6,10},{7,11},{8,12},{9,13},{1... | collective-permute-start | bytes 1769480 | tf_op jit(solution)/shard_map/ppermute | solution.py:210
  45.6 5.9 %first.1 = (bf16[384,1152]{1,0:T(8,128)(2,1)S(1)}, bf16[384,1152]{1,0:T(8,128)(2,1)S(1)}, f32[384,1152]{1,0:T(8,128)S(1)}, f32[128,1152]{1,0:T(8,128)S(1)}, f32[...) custom-call(s32[4]{0:T(128)S(1)} %pad_add_fusion.place, ...), custom_call_target="tpu_custom_call" | custom-call | flops 3057647616 | bytes 7077888 | tf_op jit(solution)/shard_map/first/pallas_call | solution.py:189
  51.6 1.9 %collective-permute-start.6 = (f32[128,1152]{1,0:T(8,128)}, f32[128,1152]{1,0:T(8,128)}, u32[]{:S(2)}, u32[]{:S(2)}) collective-permute-start(f32[128,1152]{1,0:T(8,128)} %get-tuple-element.42), channel_id=1, source_target_pairs={{0,1},{1,0},{2,3},{3,2},{4,5},{5,4},{6,7},{7,6},{8,9},{9,8},{10,11... | collective-permute-start | bytes 1769480 | tf_op jit(solution)/shard_map/ppermute | solution.py:210
  53.5 8.8 %collective-permute-start.7 = (f32[128,1152]{1,0:T(8,128)}, f32[128,1152]{1,0:T(8,128)}, u32[]{:S(2)}, u32[]{:S(2)}) collective-permute-start(f32[128,1152]{1,0:T(8,128)} %get-tuple-element.43), channel_id=1, source_target_pairs={{0,1021},{1,1020},{2,1023},{3,1022},{4,0},{5,1},{6,2},{7,3},{8,4},... | collective-permute-start | bytes 1769480 | tf_op jit(solution)/shard_map/ppermute | solution.py:210
  62.3 2.0 %collective-permute-done.5.u1 = f32[128,1152]{1,0:T(8,128)S(1)} collective-permute-done((f32[128,1152]{1,0:T(8,128)S(1)}, f32[128,1152]{1,0:T(8,128)S(1)}, u32[]{:S(2)}, u32[]{:S(2)}) %collective-permute-start.5) | collective-permute-done | bytes 589856 | tf_op jit(solution)/shard_map/ppermute | solution.py:210
  64.3 3.0 %last.1 = (f32[128,1152]{1,0:T(8,128)S(1)}, f32[128,1152]{1,0:T(8,128)S(1)}, f32[128,1152]{1,0:T(8,128)S(1)}, f32[128,1152]{1,0:T(8,128)S(1)}, f32[1,128]{1,0:T(1,128)S(1)}) custom-call(s32[4]{0:T(128)S(1)} %pad_add_fusion.place, f32[2]{0:T(128)S(1)} %pad_maximum_fusion.params, f32[3,128]{1,0:T(4,128)S(1)} %get-tuple-element.36.tags, ...), custom_call_target="tpu_custom_call" | custom-call | flops 1019215872 | bytes 4718592 | tf_op jit(solution)/shard_map/last/pallas_call | solution.py:189
  67.3 2.1 %collective-permute-start.10 = (f32[128,1152]{1,0:T(8,128)S(1)}, f32[128,1152]{1,0:T(8,128)}, u32[]{:S(2)}, u32[]{:S(2)}) collective-permute-start(f32[128,1152]{1,0:T(8,128)S(1)} %get-tuple-element.46), channel_id=1, source_target_pairs={{2,4},{3,5},{6,8},{7,9},{10,12},{11,13},{14,16},{15,17},{18,20},{1... | collective-permute-start | bytes 1769480 | tf_op jit(solution)/shard_map/ppermute | solution.py:210
  69.4 6.2 %collective-permute-start.8 = (f32[128,1152]{1,0:T(8,128)S(1)}, f32[128,1152]{1,0:T(8,128)}, u32[]{:S(2)}, u32[]{:S(2)}) collective-permute-start(f32[128,1152]{1,0:T(8,128)S(1)} %get-tuple-element.44), channel_id=1, source_target_pairs={{0,1020},{1,1021},{2,1022},{3,1023},{4,1},{5,0},{6,3},{7,2},{8,5},... | collective-permute-start | bytes 1769480 | tf_op jit(solution)/shard_map/ppermute | solution.py:210
  75.6 1.9 %collective-permute-start.9 = (f32[128,1152]{1,0:T(8,128)S(1)}, f32[128,1152]{1,0:T(8,128)}, u32[]{:S(2)}, u32[]{:S(2)}) collective-permute-start(f32[128,1152]{1,0:T(8,128)S(1)} %get-tuple-element.45), channel_id=1, source_target_pairs={{0,2},{1,3},{2,0},{3,1},{4,6},{5,7},{6,4},{7,5},{8,10},{9,11},{10,... | collective-permute-start | bytes 1769480 | tf_op jit(solution)/shard_map/ppermute | solution.py:210
  77.5 16.6 %all_to_all.12 = f32[64,1,128]{2,1,0:T(1,128)S(1)} all-to-all(f32[64,1,128]{2,1,0:T(1,128)S(1)} %broadcast_in_dim.20), channel_id=1, replica_groups=mesh['y_hi'=2,'y_lo'=4,'x_hi'=2,'z_hi'=4,'z_lo'=4,'core'=2,'x_lo'=2] {'y..., dimensions={0} | all-to-all | bytes 65536 | tf_op jit(solution)/shard_map/all_to_all | solution.py:261
  94.2 0.6 broadcast_in_dim.22
  94.8 3.4 %all-to-all-start.1 = ((f32[16,1,128]{2,1,0:T(1,128)}), f32[16,1,128]{2,1,0:T(1,128)S(1)}, u32[]{:S(2)}, u32[]{:S(2)}) async-start(f32[16,1,128]{2,1,0:T(1,128)} %broadcast_in_dim.22), calls=%async_computation.1 | async-start | bytes 16384 | tf_op jit(solution)/shard_map/all_to_all | solution.py:261
  98.2 3.0 %add_add_fusion = (f32[128,1152]{1,0:T(8,128)}, f32[128,1152]{1,0:T(8,128)}) fusion(f32[128,1152]{1,0:T(8,128)} %collective-permute-done.8, f32[128,1152]{1,0:T(8,128)} %collective-permute-done.7, f32[128,1152]{1,0:T(8,128)S(1)} %get-tuple-element.51, f32[128,1152]{1,0:T(8,128)} %collective-permute-done.6, f32[128,1152]{1,0:T(8,128)} %collective-permute-done.10, ...), kind=kLoop, calls=%fused_computation | loop fusion | flops 737280 | bytes 5308416 | tf_op jit(solution)/shard_map/add | solution.py:267
  101.2 8.1 %all-to-all-done.1 = f32[16,1,128]{2,1,0:T(1,128)S(1)} async-done(((f32[16,1,128]{2,1,0:T(1,128)}), f32[16,1,128]{2,1,0:T(1,128)S(1)}, u32[]{:S(2)}, u32[]{:S(2)}) %all-to-all-start.1) | async-done | bytes 8224 | tf_op jit(solution)/shard_map/all_to_all | solution.py:261
  109.4 0.6 fusion
  (12 shorter events, 0.1 us)
Async XLA Ops:
  0.6 43.0 %collective-permute-start = (f32[128,1152]{1,0:T(8,128)}, f32[128,1152]{1,0:T(8,128)S(1)}, u32[]{:S(2)}, u32[]{:S(2)}) collective-permute-start(f32[128,1152]{1,0:T(8,128)} %text.1), channel_id=1, source_target_pairs={{0,1},{1,0},{2,3},{3,2},{4,5},{5,4},{6,7},{7,6},{8,9},{9,8},{10,11... | collective-permute-start | bytes 1769480 | tf_op jit(solution)/shard_map/ppermute | solution.py:210
  4.6 39.1 %collective-permute-start.1 = (f32[128,1152]{1,0:T(8,128)}, f32[128,1152]{1,0:T(8,128)S(1)}, u32[]{:S(2)}, u32[]{:S(2)}) collective-permute-start(f32[128,1152]{1,0:T(8,128)} %text.1), channel_id=1, source_target_pairs={{0,4},{1,5},{2,6},{3,7},{4,8},{5,9},{6,10},{7,11},{8,12},{9,13},{1... | collective-permute-start | bytes 1769480 | tf_op jit(solution)/shard_map/ppermute | solution.py:210
  8.6 35.1 %collective-permute-start.2 = (f32[128,1152]{1,0:T(8,128)}, f32[128,1152]{1,0:T(8,128)S(1)}, u32[]{:S(2)}, u32[]{:S(2)}) collective-permute-start(f32[128,1152]{1,0:T(8,128)} %image.3), channel_id=1, source_target_pairs={{0,1023},{1,1022},{4,2},{5,3},{8,6},{9,7},{12,10},{13,11},{16,14},... | collective-permute-start | bytes 1769480 | tf_op jit(solution)/shard_map/ppermute | solution.py:210
  12.5 33.1 %collective-permute-start.4 = (f32[136,1152]{1,0:T(8,128)}, f32[136,1152]{1,0:T(8,128)S(1)}, u32[]{:S(2)}, u32[]{:S(2)}) collective-permute-start(f32[136,1152]{1,0:T(8,128)} %pack.1), channel_id=1, source_target_pairs={{0,2},{1,3},{2,0},{3,1},{4,6},{5,7},{6,4},{7,5},{8,10},{9,11},{10,... | collective-permute-start | bytes 1880072 | tf_op jit(solution)/shard_map/ppermute | solution.py:210
  33.8 9.9 %collective-permute-start.3 = (s32[1,128]{1,0:T(1,128)}, s32[1,128]{1,0:T(1,128)S(1)}, u32[]{:S(2)}, u32[]{:S(2)}) collective-permute-start(s32[1,128]{1,0:T(1,128)} %bitcast.23), channel_id=1, source_target_pairs={{0,1},{1,0},{2,3},{3,6},{4,5},{5,4},{6,7},{7,10},{8,9},{9,8},{10,1... | collective-permute-start | bytes 1544 | tf_op jit(solution)/shard_map/ppermute | solution.py:210
  43.7 20.6 %collective-permute-start.5 = (f32[128,1152]{1,0:T(8,128)S(1)}, f32[128,1152]{1,0:T(8,128)S(1)}, u32[]{:S(2)}, u32[]{:S(2)}) collective-permute-start(f32[128,1152]{1,0:T(8,128)S(1)} %collective-permute-done.t1), channel_id=1, source_target_pairs={{0,4},{1,5},{2,6},{3,7},{4,8},{5,9},{6,10},{7,11},{8,12},{9,13},{1... | collective-permute-start | bytes 1769480 | tf_op jit(solution)/shard_map/ppermute | solution.py:210
  51.6 42.6 %collective-permute-start.6 = (f32[128,1152]{1,0:T(8,128)}, f32[128,1152]{1,0:T(8,128)}, u32[]{:S(2)}, u32[]{:S(2)}) collective-permute-start(f32[128,1152]{1,0:T(8,128)} %get-tuple-element.42), channel_id=1, source_target_pairs={{0,1},{1,0},{2,3},{3,2},{4,5},{5,4},{6,7},{7,6},{8,9},{9,8},{10,11... | collective-permute-start | bytes 1769480 | tf_op jit(solution)/shard_map/ppermute | solution.py:210
  53.5 40.7 %collective-permute-start.7 = (f32[128,1152]{1,0:T(8,128)}, f32[128,1152]{1,0:T(8,128)}, u32[]{:S(2)}, u32[]{:S(2)}) collective-permute-start(f32[128,1152]{1,0:T(8,128)} %get-tuple-element.43), channel_id=1, source_target_pairs={{0,1021},{1,1020},{2,1023},{3,1022},{4,0},{5,1},{6,2},{7,3},{8,4},... | collective-permute-start | bytes 1769480 | tf_op jit(solution)/shard_map/ppermute | solution.py:210
  67.3 26.9 %collective-permute-start.10 = (f32[128,1152]{1,0:T(8,128)S(1)}, f32[128,1152]{1,0:T(8,128)}, u32[]{:S(2)}, u32[]{:S(2)}) collective-permute-start(f32[128,1152]{1,0:T(8,128)S(1)} %get-tuple-element.46), channel_id=1, source_target_pairs={{2,4},{3,5},{6,8},{7,9},{10,12},{11,13},{14,16},{15,17},{18,20},{1... | collective-permute-start | bytes 1769480 | tf_op jit(solution)/shard_map/ppermute | solution.py:210
  69.4 24.8 %collective-permute-start.8 = (f32[128,1152]{1,0:T(8,128)S(1)}, f32[128,1152]{1,0:T(8,128)}, u32[]{:S(2)}, u32[]{:S(2)}) collective-permute-start(f32[128,1152]{1,0:T(8,128)S(1)} %get-tuple-element.44), channel_id=1, source_target_pairs={{0,1020},{1,1021},{2,1022},{3,1023},{4,1},{5,0},{6,3},{7,2},{8,5},... | collective-permute-start | bytes 1769480 | tf_op jit(solution)/shard_map/ppermute | solution.py:210
  75.6 18.6 %collective-permute-start.9 = (f32[128,1152]{1,0:T(8,128)S(1)}, f32[128,1152]{1,0:T(8,128)}, u32[]{:S(2)}, u32[]{:S(2)}) collective-permute-start(f32[128,1152]{1,0:T(8,128)S(1)} %get-tuple-element.45), channel_id=1, source_target_pairs={{0,2},{1,3},{2,0},{3,1},{4,6},{5,7},{6,4},{7,5},{8,10},{9,11},{10,... | collective-permute-start | bytes 1769480 | tf_op jit(solution)/shard_map/ppermute | solution.py:210
  94.8 14.6 %all-to-all-start.1 = ((f32[16,1,128]{2,1,0:T(1,128)}), f32[16,1,128]{2,1,0:T(1,128)S(1)}, u32[]{:S(2)}, u32[]{:S(2)}) async-start(f32[16,1,128]{2,1,0:T(1,128)} %broadcast_in_dim.22), calls=%async_computation.1 | async-start | bytes 16384 | tf_op jit(solution)/shard_map/all_to_all | solution.py:261

commit v6 on v5

--- a/solution.py
+++ b/solution.py
@@ -254,6 +254,7 @@
     )
     gu1 = send(gu1, lambda b: down(b) ^ 1)
     gi2 = other_core(gi2)
+    gt1, gu0, gi2, gfar = lax.optimization_barrier((gt1, gu0, gi2, gfar))
     gfar = send(gfar, lambda b: up(b) ^ 2, [b for b in everyone if b % 4 >= 2])
 
     def add_up(row, axes):

time: 111 us -> 115 us (1.036)
  waiting for transfers between devices: 16.3 us -> 20.9 us
    all_to_all x1, starting transfers between devices: 3.38 us -> 8.93 us  [add_up(): lax.all_to_all(shares, axes, 0, 0, tiled=True)]
    ppermute x11, starting transfers between devices: 55.7 us -> 50.6 us  [send(): return lax.ppermute(x, NAMES, [(b, to(b)) for b in senders])]
    ppermute x11, waiting for transfers between devices: 8.16 us -> 12.5 us  [send(): return lax.ppermute(x, NAMES, [(b, to(b)) for b in senders])]
  transfers between devices with their start and end apart: 12 -> 12, of which waited for: 3 -> 4; matrix products, arithmetic and copies ran while one was open for 3% -> 3% of each run, Pallas kernels for 10% -> 10%
where the time goes in v6:
time: 115 us
  starting transfers between devices  59.5 us (52%)
  waiting for transfers between devices  20.9 us (18%)
  blocking collectives  15.8 us (14%)
  Pallas kernels  11.9 us (10%)
  other arithmetic  3.11 us (3%)
  between operations  2.13 us (2%)
  local copies, waits for them, and re-layouts  1.22 us (1%)
    ppermute x11, starting transfers between devices, send(): return lax.ppermute(x, NAMES, [(b, to(b)) for b in senders])  50.6 us
    all_to_all x1, blocking collectives, add_up(): lax.all_to_all(shares, axes, 0, 0, tiled=True)  15.8 us
    ppermute x11, waiting for transfers between devices, send(): return lax.ppermute(x, NAMES, [(b, to(b)) for b in senders])  12.5 us
    pallas_call x2, Pallas kernels, kernel_call(): pl.pallas_call(body, out_shape=[jax.ShapeDtypeStruct(shape, dtype) for sh...  9.33 us
    all_to_all x1, starting transfers between devices, add_up(): lax.all_to_all(shares, axes, 0, 0, tiled=True)  8.93 us
    all_to_all x1, waiting for transfers between devices, add_up(): lax.all_to_all(shares, axes, 0, 0, tiled=True)  8.39 us
    add x1, other arithmetic, local(): grad_text = gt0 + gt1 + gu0 + gu1  2.91 us
    pallas_call x1, Pallas kernels, pack(): pl.pallas_call(pack_kernel, out_shape=jax.ShapeDtypeStruct((size + 8, wid...  2.56 us
  transfers between devices with their start and end apart: 12, of which 4 were waited for; matrix products, arithmetic and copies ran while one was open for 3% of the time, Pallas kernels for 10%

profile of v6, /device:TPU:1, one launch (start us, length us, event | category | flops | bytes accessed | tf_op | source)
XLA Modules:
  0.0 114.5 jit_solution(15425369932087824181)
XLA Ops:
  0.6 4.0 %collective-permute-start = (f32[128,1152]{1,0:T(8,128)}, f32[128,1152]{1,0:T(8,128)S(1)}, u32[]{:S(2)}, u32[]{:S(2)}) collective-permute-start(f32[128,1152]{1,0:T(8,128)} %text.1), channel_id=1, source_target_pairs={{0,1},{1,0},{2,3},{3,2},{4,5},{5,4},{6,7},{7,6},{8,9},{9,8},{10,11... | collective-permute-start | bytes 1769480 | tf_op jit(solution)/shard_map/ppermute | solution.py:210
  4.6 4.0 %collective-permute-start.1 = (f32[128,1152]{1,0:T(8,128)}, f32[128,1152]{1,0:T(8,128)S(1)}, u32[]{:S(2)}, u32[]{:S(2)}) collective-permute-start(f32[128,1152]{1,0:T(8,128)} %text.1), channel_id=1, source_target_pairs={{0,4},{1,5},{2,6},{3,7},{4,8},{5,9},{6,10},{7,11},{8,12},{9,13},{1... | collective-permute-start | bytes 1769480 | tf_op jit(solution)/shard_map/ppermute | solution.py:210
  8.6 1.3 %collective-permute-start.2 = (f32[128,1152]{1,0:T(8,128)}, f32[128,1152]{1,0:T(8,128)S(1)}, u32[]{:S(2)}, u32[]{:S(2)}) collective-permute-start(f32[128,1152]{1,0:T(8,128)} %image.3), channel_id=1, source_target_pairs={{0,1023},{1,1022},{4,2},{5,3},{8,6},{9,7},{12,10},{13,11},{16,14},... | collective-permute-start | bytes 1769480 | tf_op jit(solution)/shard_map/ppermute | solution.py:210
  9.9 2.6 %pack.1 = f32[136,1152]{1,0:T(8,128)} custom-call(s32[1,128]{1,0:T(1,128)} %bitcast.22, f32[128,1152]{1,0:T(8,128)} %image.3), custom_call_target="tpu_custom_call" | custom-call | bytes 2097152 | tf_op jit(solution)/shard_map/pack/pallas_call | solution.py:172
  12.5 21.3 %collective-permute-start.4 = (f32[136,1152]{1,0:T(8,128)}, f32[136,1152]{1,0:T(8,128)S(1)}, u32[]{:S(2)}, u32[]{:S(2)}) collective-permute-start(f32[136,1152]{1,0:T(8,128)} %pack.1), channel_id=1, source_target_pairs={{0,2},{1,3},{2,0},{3,1},{4,6},{5,7},{6,4},{7,5},{8,10},{9,11},{10,... | collective-permute-start | bytes 1880072 | tf_op jit(solution)/shard_map/ppermute | solution.py:210
  33.8 2.2 %collective-permute-start.3 = (s32[1,128]{1,0:T(1,128)}, s32[1,128]{1,0:T(1,128)S(1)}, u32[]{:S(2)}, u32[]{:S(2)}) collective-permute-start(s32[1,128]{1,0:T(1,128)} %bitcast.23), channel_id=1, source_target_pairs={{0,1},{1,0},{2,3},{3,6},{4,5},{5,4},{6,7},{7,10},{8,9},{9,8},{10,1... | collective-permute-start | bytes 1544 | tf_op jit(solution)/shard_map/ppermute | solution.py:210
  37.4 0.1 pad_add_fusion.place
  37.5 6.2 %collective-permute-done.3.before = s32[1,128]{1,0:T(1,128)S(1)} collective-permute-done((s32[1,128]{1,0:T(1,128)}, s32[1,128]{1,0:T(1,128)S(1)}, u32[]{:S(2)}, u32[]{:S(2)}) %collective-permute-start.3) | collective-permute-done | bytes 544 | tf_op jit(solution)/shard_map/ppermute | solution.py:210
  43.7 1.9 %collective-permute-start.5 = (f32[128,1152]{1,0:T(8,128)S(1)}, f32[128,1152]{1,0:T(8,128)S(1)}, u32[]{:S(2)}, u32[]{:S(2)}) collective-permute-start(f32[128,1152]{1,0:T(8,128)S(1)} %collective-permute-done.t1), channel_id=1, source_target_pairs={{0,4},{1,5},{2,6},{3,7},{4,8},{5,9},{6,10},{7,11},{8,12},{9,13},{1... | collective-permute-start | bytes 1769480 | tf_op jit(solution)/shard_map/ppermute | solution.py:210
  45.6 6.3 %first.1 = (bf16[384,1152]{1,0:T(8,128)(2,1)S(1)}, bf16[384,1152]{1,0:T(8,128)(2,1)S(1)}, f32[384,1152]{1,0:T(8,128)S(1)}, f32[128,1152]{1,0:T(8,128)S(1)}, f32[...) custom-call(s32[4]{0:T(128)S(1)} %pad_add_fusion.place, ...), custom_call_target="tpu_custom_call" | custom-call | flops 3057647616 | bytes 7077888 | tf_op jit(solution)/shard_map/first/pallas_call | solution.py:189
  52.0 1.9 %collective-permute-start.6 = (f32[128,1152]{1,0:T(8,128)S(1)}, f32[128,1152]{1,0:T(8,128)S(1)}, u32[]{:S(2)}, u32[]{:S(2)}) collective-permute-start(f32[128,1152]{1,0:T(8,128)S(1)} %get-tuple-element.46), channel_id=1, source_target_pairs={{0,1},{1,0},{2,3},{3,2},{4,5},{5,4},{6,7},{7,6},{8,9},{9,8},{10,11... | collective-permute-start | bytes 1769480 | tf_op jit(solution)/shard_map/ppermute | solution.py:210
  53.9 8.8 %collective-permute-start.7 = (f32[128,1152]{1,0:T(8,128)S(1)}, f32[128,1152]{1,0:T(8,128)S(1)}, u32[]{:S(2)}, u32[]{:S(2)}) collective-permute-start(f32[128,1152]{1,0:T(8,128)S(1)} %get-tuple-element.47), channel_id=1, source_target_pairs={{0,1021},{1,1020},{2,1023},{3,1022},{4,0},{5,1},{6,2},{7,3},{8,4},... | collective-permute-start | bytes 1769480 | tf_op jit(solution)/shard_map/ppermute | solution.py:210
  62.7 1.6 %collective-permute-done.5.u1 = f32[128,1152]{1,0:T(8,128)S(1)} collective-permute-done((f32[128,1152]{1,0:T(8,128)S(1)}, f32[128,1152]{1,0:T(8,128)S(1)}, u32[]{:S(2)}, u32[]{:S(2)}) %collective-permute-start.5) | collective-permute-done | bytes 589856 | tf_op jit(solution)/shard_map/ppermute | solution.py:210
  64.3 3.0 %last.1 = (f32[128,1152]{1,0:T(8,128)S(1)}, f32[128,1152]{1,0:T(8,128)S(1)}, f32[128,1152]{1,0:T(8,128)S(1)}, f32[128,1152]{1,0:T(8,128)S(1)}, f32[1,128]{1,0:T(1,128)S(1)}) custom-call(s32[4]{0:T(128)S(1)} %pad_add_fusion.place, f32[2]{0:T(128)S(1)} %pad_maximum_fusion.params, f32[3,128]{1,0:T(4,128)S(1)} %get-tuple-element.40.tags, ...), custom_call_target="tpu_custom_call" | custom-call | flops 1019215872 | bytes 4718592 | tf_op jit(solution)/shard_map/last/pallas_call | solution.py:189
  67.3 1.9 %collective-permute-start.8 = (f32[128,1152]{1,0:T(8,128)S(1)}, f32[128,1152]{1,0:T(8,128)S(1)}, u32[]{:S(2)}, u32[]{:S(2)}) collective-permute-start(f32[128,1152]{1,0:T(8,128)S(1)} %get-tuple-element.48), channel_id=1, source_target_pairs={{0,2},{1,3},{2,0},{3,1},{4,6},{5,7},{6,4},{7,5},{8,10},{9,11},{10,... | collective-permute-start | bytes 1769480 | tf_op jit(solution)/shard_map/ppermute | solution.py:210
  69.2 1.9 %collective-permute-start.9 = (f32[128,1152]{1,0:T(8,128)S(1)}, f32[128,1152]{1,0:T(8,128)}, u32[]{:S(2)}, u32[]{:S(2)}) collective-permute-start(f32[128,1152]{1,0:T(8,128)S(1)} %get-tuple-element.52), channel_id=1, source_target_pairs={{0,1020},{1,1021},{2,1022},{3,1023},{4,1},{5,0},{6,3},{7,2},{8,5},... | collective-permute-start | bytes 1769480 | tf_op jit(solution)/shard_map/ppermute | solution.py:210
  71.2 4.7 %collective-permute-done.7 = f32[128,1152]{1,0:T(8,128)S(1)} collective-permute-done((f32[128,1152]{1,0:T(8,128)S(1)}, f32[128,1152]{1,0:T(8,128)S(1)}, u32[]{:S(2)}, u32[]{:S(2)}) %collective-permute-start.7) | collective-permute-done | bytes 589856 | tf_op jit(solution)/shard_map/ppermute | solution.py:210
  75.9 1.3 %collective-permute-start.10 = (f32[128,1152]{1,0:T(8,128)S(1)}, f32[128,1152]{1,0:T(8,128)S(1)}, u32[]{:S(2)}, u32[]{:S(2)}) collective-permute-start(f32[128,1152]{1,0:T(8,128)S(1)} %get-tuple-element.54), channel_id=1, source_target_pairs={{2,4},{3,5},{6,8},{7,9},{10,12},{11,13},{14,16},{15,17},{18,20},{1... | collective-permute-start | bytes 1769480 | tf_op jit(solution)/shard_map/ppermute | solution.py:210
  77.3 15.8 %all_to_all.12 = f32[64,1,128]{2,1,0:T(1,128)S(1)} all-to-all(f32[64,1,128]{2,1,0:T(1,128)S(1)} %broadcast_in_dim.20), channel_id=1, replica_groups=mesh['y_hi'=2,'y_lo'=4,'x_hi'=2,'z_hi'=4,'z_lo'=4,'core'=2,'x_lo'=2] {'y..., dimensions={0} | all-to-all | bytes 65536 | tf_op jit(solution)/shard_map/all_to_all | solution.py:262
  93.1 0.6 broadcast_in_dim.22
  93.7 8.9 %all-to-all-start.1 = ((f32[16,1,128]{2,1,0:T(1,128)}), f32[16,1,128]{2,1,0:T(1,128)S(1)}, u32[]{:S(2)}, u32[]{:S(2)}) async-start(f32[16,1,128]{2,1,0:T(1,128)} %broadcast_in_dim.22), calls=%async_computation.1 | async-start | bytes 16384 | tf_op jit(solution)/shard_map/all_to_all | solution.py:262
  102.6 2.9 %add_add_fusion = (f32[128,1152]{1,0:T(8,128)}, f32[128,1152]{1,0:T(8,128)}) fusion(f32[128,1152]{1,0:T(8,128)} %collective-permute-done.9, f32[128,1152]{1,0:T(8,128)} %copy-done.1, f32[128,1152]{1,0:T(8,128)S(1)} %get-tuple-element.59, f32[128,1152]{1,0:T(8,128)} %copy-done, f32[128,1152]{1,0:T(8,128)S(1)} %collective-permute-done.10, ...), kind=kLoop, calls=%fused_computation | loop fusion | flops 737280 | bytes 5308416 | tf_op jit(solution)/shard_map/add | solution.py:268
  105.5 8.4 %all-to-all-done.1 = f32[16,1,128]{2,1,0:T(1,128)S(1)} async-done(((f32[16,1,128]{2,1,0:T(1,128)}), f32[16,1,128]{2,1,0:T(1,128)S(1)}, u32[]{:S(2)}, u32[]{:S(2)}) %all-to-all-start.1) | async-done | bytes 8224 | tf_op jit(solution)/shard_map/all_to_all | solution.py:262
  113.9 0.6 fusion
  (18 shorter events, 0.2 us)
Async XLA Ops:
  0.6 43.0 %collective-permute-start = (f32[128,1152]{1,0:T(8,128)}, f32[128,1152]{1,0:T(8,128)S(1)}, u32[]{:S(2)}, u32[]{:S(2)}) collective-permute-start(f32[128,1152]{1,0:T(8,128)} %text.1), channel_id=1, source_target_pairs={{0,1},{1,0},{2,3},{3,2},{4,5},{5,4},{6,7},{7,6},{8,9},{9,8},{10,11... | collective-permute-start | bytes 1769480 | tf_op jit(solution)/shard_map/ppermute | solution.py:210
  4.6 39.1 %collective-permute-start.1 = (f32[128,1152]{1,0:T(8,128)}, f32[128,1152]{1,0:T(8,128)S(1)}, u32[]{:S(2)}, u32[]{:S(2)}) collective-permute-start(f32[128,1152]{1,0:T(8,128)} %text.1), channel_id=1, source_target_pairs={{0,4},{1,5},{2,6},{3,7},{4,8},{5,9},{6,10},{7,11},{8,12},{9,13},{1... | collective-permute-start | bytes 1769480 | tf_op jit(solution)/shard_map/ppermute | solution.py:210
  8.6 35.1 %collective-permute-start.2 = (f32[128,1152]{1,0:T(8,128)}, f32[128,1152]{1,0:T(8,128)S(1)}, u32[]{:S(2)}, u32[]{:S(2)}) collective-permute-start(f32[128,1152]{1,0:T(8,128)} %image.3), channel_id=1, source_target_pairs={{0,1023},{1,1022},{4,2},{5,3},{8,6},{9,7},{12,10},{13,11},{16,14},... | collective-permute-start | bytes 1769480 | tf_op jit(solution)/shard_map/ppermute | solution.py:210
  12.5 33.1 %collective-permute-start.4 = (f32[136,1152]{1,0:T(8,128)}, f32[136,1152]{1,0:T(8,128)S(1)}, u32[]{:S(2)}, u32[]{:S(2)}) collective-permute-start(f32[136,1152]{1,0:T(8,128)} %pack.1), channel_id=1, source_target_pairs={{0,2},{1,3},{2,0},{3,1},{4,6},{5,7},{6,4},{7,5},{8,10},{9,11},{10,... | collective-permute-start | bytes 1880072 | tf_op jit(solution)/shard_map/ppermute | solution.py:210
  33.8 9.9 %collective-permute-start.3 = (s32[1,128]{1,0:T(1,128)}, s32[1,128]{1,0:T(1,128)S(1)}, u32[]{:S(2)}, u32[]{:S(2)}) collective-permute-start(s32[1,128]{1,0:T(1,128)} %bitcast.23), channel_id=1, source_target_pairs={{0,1},{1,0},{2,3},{3,6},{4,5},{5,4},{6,7},{7,10},{8,9},{9,8},{10,1... | collective-permute-start | bytes 1544 | tf_op jit(solution)/shard_map/ppermute | solution.py:210
  43.7 20.6 %collective-permute-start.5 = (f32[128,1152]{1,0:T(8,128)S(1)}, f32[128,1152]{1,0:T(8,128)S(1)}, u32[]{:S(2)}, u32[]{:S(2)}) collective-permute-start(f32[128,1152]{1,0:T(8,128)S(1)} %collective-permute-done.t1), channel_id=1, source_target_pairs={{0,4},{1,5},{2,6},{3,7},{4,8},{5,9},{6,10},{7,11},{8,12},{9,13},{1... | collective-permute-start | bytes 1769480 | tf_op jit(solution)/shard_map/ppermute | solution.py:210
  52.0 19.2 %collective-permute-start.6 = (f32[128,1152]{1,0:T(8,128)S(1)}, f32[128,1152]{1,0:T(8,128)S(1)}, u32[]{:S(2)}, u32[]{:S(2)}) collective-permute-start(f32[128,1152]{1,0:T(8,128)S(1)} %get-tuple-element.46), channel_id=1, source_target_pairs={{0,1},{1,0},{2,3},{3,2},{4,5},{5,4},{6,7},{7,6},{8,9},{9,8},{10,11... | collective-permute-start | bytes 1769480 | tf_op jit(solution)/shard_map/ppermute | solution.py:210
  53.9 22.0 %collective-permute-start.7 = (f32[128,1152]{1,0:T(8,128)S(1)}, f32[128,1152]{1,0:T(8,128)S(1)}, u32[]{:S(2)}, u32[]{:S(2)}) collective-permute-start(f32[128,1152]{1,0:T(8,128)S(1)} %get-tuple-element.47), channel_id=1, source_target_pairs={{0,1021},{1,1020},{2,1023},{3,1022},{4,0},{5,1},{6,2},{7,3},{8,4},... | collective-permute-start | bytes 1769480 | tf_op jit(solution)/shard_map/ppermute | solution.py:210
  67.3 8.6 %collective-permute-start.8 = (f32[128,1152]{1,0:T(8,128)S(1)}, f32[128,1152]{1,0:T(8,128)S(1)}, u32[]{:S(2)}, u32[]{:S(2)}) collective-permute-start(f32[128,1152]{1,0:T(8,128)S(1)} %get-tuple-element.48), channel_id=1, source_target_pairs={{0,2},{1,3},{2,0},{3,1},{4,6},{5,7},{6,4},{7,5},{8,10},{9,11},{10,... | collective-permute-start | bytes 1769480 | tf_op jit(solution)/shard_map/ppermute | solution.py:210
  69.2 23.9 %collective-permute-start.9 = (f32[128,1152]{1,0:T(8,128)S(1)}, f32[128,1152]{1,0:T(8,128)}, u32[]{:S(2)}, u32[]{:S(2)}) collective-permute-start(f32[128,1152]{1,0:T(8,128)S(1)} %get-tuple-element.52), channel_id=1, source_target_pairs={{0,1020},{1,1021},{2,1022},{3,1023},{4,1},{5,0},{6,3},{7,2},{8,5},... | collective-permute-start | bytes 1769480 | tf_op jit(solution)/shard_map/ppermute | solution.py:210
  71.2 6.1 %copy-start = (f32[128,1152]{1,0:T(8,128)}, f32[128,1152]{1,0:T(8,128)S(1)}, u32[]{:S(2)}) copy-start(f32[128,1152]{1,0:T(8,128)S(1)} %collective-permute-done.6) | copy-start | bytes 1769476
  75.9 17.2 %copy-start.1 = (f32[128,1152]{1,0:T(8,128)}, f32[128,1152]{1,0:T(8,128)S(1)}, u32[]{:S(2)}) copy-start(f32[128,1152]{1,0:T(8,128)S(1)} %collective-permute-done.7) | copy-start | bytes 1769476
  75.9 1.3 %copy-start.2 = (f32[128,1152]{1,0:T(8,128)}, f32[128,1152]{1,0:T(8,128)S(1)}, u32[]{:S(2)}) copy-start(f32[128,1152]{1,0:T(8,128)S(1)} %collective-permute-done.8) | copy-start | bytes 1769476
  75.9 17.2 %collective-permute-start.10 = (f32[128,1152]{1,0:T(8,128)S(1)}, f32[128,1152]{1,0:T(8,128)S(1)}, u32[]{:S(2)}, u32[]{:S(2)}) collective-permute-start(f32[128,1152]{1,0:T(8,128)S(1)} %get-tuple-element.54), channel_id=1, source_target_pairs={{2,4},{3,5},{6,8},{7,9},{10,12},{11,13},{14,16},{15,17},{18,20},{1... | collective-permute-start | bytes 1769480 | tf_op jit(solution)/shard_map/ppermute | solution.py:210
  93.7 20.2 %all-to-all-start.1 = ((f32[16,1,128]{2,1,0:T(1,128)}), f32[16,1,128]{2,1,0:T(1,128)S(1)}, u32[]{:S(2)}, u32[]{:S(2)}) async-start(f32[16,1,128]{2,1,0:T(1,128)} %broadcast_in_dim.22), calls=%async_computation.1 | async-start | bytes 16384 | tf_op jit(solution)/shard_map/all_to_all | solution.py:262
